TPU v7x, 32 devices: a whole 2x2x4 slice. The times are simulated.
32 devices in a mesh: dp: 16 (over z, y, core), mp: 2 (over x).
Axes of the slice: x: 2, y: 2, z: 4, core: 2. Of those that a mesh axis runs over, the one named last changes fastest.
Arguments:
- acts: bfloat16 [4096, 28672], P('dp', 'mp'), may hold values from -24 to 24
- grads: bfloat16 [4096, 8192], P('dp', 'mp'), may hold values from -6 to 6
- basis_in: bfloat16 [28672, 640], P('mp', 'dp'), may hold values from -0.03125 to 0.03125
- basis_out: bfloat16 [8192, 1024], P('dp', 'mp'), may hold values from -0.0625 to 0.0625
- damping: float32 [1], replicated, may hold values from 0.5 to 2
Outputs:
- update: bfloat16 [28672, 8192], P('mp', 'dp')
- diag: float32 [640, 1024], P('mp', 'dp')
All inputs are finite; a program needn't handle non-finite values.
Results may differ from a plain program's by a relative error of at most 0.0085.
Values may be sent and summed in bfloat16 or wider, within the bound.
No kernel may reach another device: no remote copies, remote signals or barrier semaphores. Data moves between devices by JAX's collectives and lax.ppermute only.
A program may use at most 128 MiB of HBM per device.

v0:
```python
import jax
import jax.numpy as jnp
from jax import lax
from jax.sharding import PartitionSpec as P


def on_device(acts, grads, basis_in, basis_out, damping):
    tok_rows = acts.shape[0]
    tokens_all = tok_rows * lax.axis_size("dp")
    whole_grads = lax.all_gather(grads, "mp", axis=1, tiled=True)
    grad_proj = jnp.dot(
        whole_grads,
        lax.all_gather(basis_out, "dp", axis=0, tiled=True),
        preferred_element_type=jnp.float32,
    ).astype(jnp.bfloat16)
    full_in = lax.all_gather(basis_in, "dp", axis=1, tiled=True)
    act_proj_t = lax.psum_scatter(
        lax.dot_general(
            full_in, acts, (((0,), (1,)), ((), ())), preferred_element_type=jnp.float32
        ),
        "mp",
        scatter_dimension=0,
        tiled=True,
    ).astype(jnp.bfloat16)
    act_sq_t = (act_proj_t.astype(jnp.float32) ** 2).astype(jnp.bfloat16)
    grad_sq = (grad_proj.astype(jnp.float32) ** 2).astype(jnp.bfloat16)
    stacked = jnp.stack([grad_proj, grad_sq])
    piece = lax.all_gather(stacked, "mp", axis=2, tiled=True)
    rotated = jnp.dot(act_proj_t, piece[0], preferred_element_type=jnp.float32)
    squares = jnp.dot(act_sq_t, piece[1], preferred_element_type=jnp.float32)
    partials = jnp.stack([rotated, squares])
    owned = lax.psum_scatter(partials, "dp", scatter_dimension=2, tiled=True)
    diag = owned[1] / tokens_all
    scaled = (owned[0] / (diag + damping[0])).astype(jnp.bfloat16)
    out_rows = lax.all_gather(basis_out, "mp", axis=1, tiled=True)
    dims = (((1,), (1,)), ((), ()))
    scaled_wide = lax.all_gather(scaled, "dp", axis=1, tiled=True)
    back_part = lax.dot_general(
        scaled_wide, out_rows, dims, preferred_element_type=jnp.float32
    ).astype(jnp.bfloat16)
    back = lax.all_gather(back_part, "mp", axis=0, tiled=True)
    update = jnp.dot(full_in, back, preferred_element_type=jnp.float32)
    return (update.astype(jnp.bfloat16), diag)


def solution(mesh):
    placed = (P("dp", "mp"), P("dp", "mp"), P("mp", "dp"), P("dp", "mp"), P())
    return jax.shard_map(
        on_device,
        mesh=mesh,
        in_specs=placed,
        out_specs=(P("mp", "dp"), P("mp", "dp")),
        check_vma=False,
    )
```

profile of v0, /device:TPU:0, one launch (start us, length us, event | category | flops | bytes accessed | tf_op | source)
XLA Modules:
  0.0 477.9 jit_solution(16236234424675882709)
XLA Ops:
  7.2 0.0 all-gather.8.cloned.1.call-start
  7.2 0.7 all-gather.8.cloned.1.call-update
  7.9 0.0 all-gather.10.cloned.1.call-start
  7.9 0.7 all-gather.10.cloned.1.call-update
  8.6 0.0 all-gather.6.cloned.1.call-start
  8.7 0.7 all-gather.6.cloned.1.call-update
  9.4 0.0 all-gather.12.cloned.1.call-start
  9.4 59.6 %all-gather.8.cloned.1.call-done = bf16[256,8192]{1,0:T(8,128)(2,1)} async-done(((bf16[256,4096]{1,0:T(8,128)(2,1)}), bf16[256,8192]{1,0:T(8,128)(2,1)}) %all-gather.8.cloned.1.call-update) | async-done | bytes 4194320 | tf_op jit(solution)/shard_map/all_gather | solution.py:10
  69.0 77.1 %all-gather.10.cloned.1.call-done = bf16[8192,512]{1,0:T(8,128)(2,1)} async-done(((bf16[512,512]{1,0:T(8,128)(2,1)}), bf16[8192,512]{1,0:T(8,128)(2,1)}) %all-gather.10.cloned.1.call-update) | async-done | bytes 8388624 | tf_op jit(solution)/shard_map/all_gather | solution.py:13
  146.1 7.0 %convolution_convert_fusion.2 = bf16[256,512]{1,0:T(8,128)(2,1)S(1)} fusion(bf16[256,8192]{1,0:T(8,128)(2,1)} %all-gather.8.cloned.1.call-done, bf16[8192,512]{1,0:T(8,128)(2,1)} %all-gather.10.cloned.1.call-done), kind=kOutput, calls=%fused_computation.6 | convolution fusion | flops 2147614720 | bytes 12845056 | tf_op jit(solution)/shard_map/dot_general | solution.py:11
  153.2 0.8 pad_maximum_fusion.1
  154.0 0.0 all-gather.12.cloned.1.call-update
  154.0 0.0 reduce-scatter.2.cloned.1.call-start
  154.1 88.4 %all-gather.6.cloned.1.call-done = bf16[14336,640]{0,1:T(8,128)(2,1)} async-done(((bf16[14336,40]{0,1:T(8,128)(2,1)}), bf16[14336,640]{0,1:T(8,128)(2,1)}) %all-gather.6.cloned.1.call-update) | async-done | bytes 18350096 | tf_op jit(solution)/shard_map/all_gather | solution.py:16
  242.5 14.3 %fusion.6 = f32[640,256]{1,0:T(8,128)} fusion(bf16[14336,640]{0,1:T(8,128)(2,1)} %all-gather.6.cloned.1.call-done, bf16[256,14336]{1,0:T(8,128)(2,1)} %param.5), kind=kOutput, calls=%fused_computation.21 | convolution fusion | flops 4697620480 | bytes 26345472 | tf_op jit(solution)/shard_map/dot_general | solution.py:18
  256.8 0.0 reduce-scatter.2.cloned.1.call-update
  256.8 0.0 all-reduce.3.cloned.1.call-start
  256.8 8.4 %all-gather.12.cloned.1.call-done = bf16[2,256,1024]{2,1,0:T(8,128)(2,1)} async-done(((bf16[2,256,512]{2,1,0:T(8,128)(2,1)}), bf16[2,256,1024]{2,1,0:T(8,128)(2,1)}) %all-gather.12.cloned.1.call-update) | async-done | bytes 1048592 | tf_op jit(solution)/shard_map/all_gather | solution.py:28
  265.2 18.7 %reduce-scatter.2.cloned.1.call-done = f32[320,256]{1,0:T(8,128)} async-done(((f32[640,256]{1,0:T(8,128)}), f32[320,256]{1,0:T(8,128)}) %reduce-scatter.2.cloned.1.call-update) | async-done | bytes 327696 | tf_op jit(solution)/shard_map/reduce_scatter | solution.py:17
  283.9 1.5 convolution_bitcast_fusion
  285.4 1.5 convolution_bitcast_fusion.1
  286.9 0.0 copy-start
  286.9 0.2 pad_maximum_fusion
  287.1 3.4 copy.9
  290.5 0.0 all-reduce.3.cloned.1.call-update
  290.5 0.0 all-gather.14.cloned.1.call-start
  290.5 0.7 all-gather.14.cloned.1.call-update
  291.9 0.0 copy-done
  291.9 0.6 dynamic-slice
  293.1 101.0 %all-reduce.3.cloned.1.call-done = f32[2,320,1024]{1,0,2:T(2,128)} async-done(((f32[2,320,1024]{1,0,2:T(2,128)}), f32[2,320,1024]{1,0,2:T(2,128)}) %all-reduce.3.cloned.1.call-update) | async-done | bytes 2621456
  394.1 1.2 dynamic-slice_multiply_fusion
  395.3 0.7 fusion.3
  396.0 21.7 %all_gather.25 = bf16[320,1024]{0,1:T(8,128)(2,1)S(1)} all-gather(bf16[320,64]{0,1:T(8,128)(2,1)S(1)} %get-tuple-element.6), channel_id=1, replica_groups=mesh['dp'=16,'mp'=2] {'dp'}, dimensions={1}, use_global_device_ids=true | all-gather | bytes 696320 | tf_op jit(solution)/shard_map/all_gather | solution.py:37
  417.7 0.0 all-gather.14.cloned.1.call-done
  417.7 1.9 convolution_convert_fusion.1
  419.6 10.8 %all_gather.27 = bf16[640,512]{1,0:T(8,128)(2,1)S(1)} all-gather(bf16[320,512]{1,0:T(8,128)(2,1)S(1)} %convolution_convert_fusion.1), channel_id=1, replica_groups=mesh['dp'=16,'mp'=2] {'mp'}, dimensions={0}, use_global_device_ids=true | all-gather | bytes 983040 | tf_op jit(solution)/shard_map/all_gather | solution.py:41
  430.4 20.7 %fusion = bf16[14336,512]{0,1:T(8,128)(2,1)} fusion(bf16[640,512]{1,0:T(8,128)(2,1)S(1)} %all_gather.27, bf16[14336,640]{0,1:T(8,128)(2,1)} %all-gather.6.cloned.1.call-done), kind=kOutput, calls=%fused_computation.1 | convolution fusion | flops 9402580992 | bytes 33685504 | tf_op jit(solution)/shard_map/dot_general | solution.py:42
  451.1 19.9 %copy.11 = bf16[14336,512]{1,0:T(8,128)(2,1)} copy(bf16[14336,512]{0,1:T(8,128)(2,1)} %fusion) | data formatting | bytes 29360128
  (1 shorter events, 0.0 us)
Async XLA Ops:
  7.2 61.9 %all-gather.8.cloned.1.call-start = ((), (), s32[]{:S(2)}) async-start(), calls=%async_computation.3 | async-start | bytes 6291456 | tf_op jit(solution)/shard_map/all_gather | solution.py:10
  7.9 138.2 %all-gather.10.cloned.1.call-start = ((), (), s32[]{:S(2)}) async-start(), calls=%async_computation.4 | async-start | bytes 8912896 | tf_op jit(solution)/shard_map/all_gather | solution.py:13
  8.6 233.8 %all-gather.6.cloned.1.call-start = ((), (), s32[]{:S(2)}) async-start(), calls=%async_computation.1 | async-start | bytes 19496960 | tf_op jit(solution)/shard_map/all_gather | solution.py:16
  9.4 255.8 %all-gather.12.cloned.1.call-start = ((), (), s32[]{:S(2)}) async-start(), calls=%async_computation.5 | async-start | bytes 1572864 | tf_op jit(solution)/shard_map/all_gather | solution.py:28
  154.0 129.9 %reduce-scatter.2.cloned.1.call-start = ((), (), s32[]{:S(2)}) async-start(), calls=%async_computation.2 | async-start | bytes 983040 | tf_op jit(solution)/shard_map/reduce_scatter | solution.py:17
  256.8 137.4 %all-reduce.3.cloned.1.call-start = ((), (), s32[]{:S(2)}) async-start(), calls=%async_computation.7 | async-start | bytes 6291456
  286.9 5.0 %copy-start = (u32[32]{0:T(128)S(1)}, u32[32]{0:T(128)}, u32[]{:S(2)}) copy-start(u32[32]{0:T(128)} %constant.6) | copy-start | bytes 388
  290.5 127.2 %all-gather.14.cloned.1.call-start = ((), (), s32[]{:S(2)}) async-start(), calls=%async_computation.6 | async-start | bytes 1572864 | tf_op jit(solution)/shard_map/all_gather | solution.py:35
Sparse Core Ops, SparseCore 0:
  9.5 59.4 all-gather.7
  71.2 74.8 all-gather.9
  147.7 94.7 all-gather.5
  243.9 21.2 all-gather.11
  267.9 15.9 reduce-scatter.1
  290.6 103.4 all-reduce.2
  395.8 20.4 all-gather.13
where the time goes:
time: 479 us; the launch traced here: 478 us
  waiting for transfers between devices  356 us (74%)
  matrix products  46.8 us (10%)
  blocking collectives  32.5 us (7%)
  local copies, waits for them, and re-layouts  23.9 us (5%)
  between operations  15.5 us (3%)
    unnamed x8, waiting for transfers between devices  104 us
    all_gather x1, waiting for transfers between devices, on_device(): full_in = lax.all_gather(basis_in, 'dp', axis=1, tiled=True)  88.4 us
    all_gather x1, waiting for transfers between devices, on_device(): lax.all_gather(basis_out, 'dp', axis=0, tiled=True)  77.1 us
    all_gather x1, waiting for transfers between devices, on_device(): whole_grads = lax.all_gather(grads, 'mp', axis=1, tiled=True)  59.6 us
    all_gather x1, blocking collectives, on_device(): scaled_wide = lax.all_gather(scaled, 'dp', axis=1, tiled=True)  21.7 us
    dot_general x1, matrix products, on_device(): update = jnp.dot(full_in, back, preferred_element_type=jnp.float32)  20.7 us
    unnamed x4, local copies, waits for them, and re-layouts  20.5 us
    reduce_scatter x1, waiting for transfers between devices, on_device(): lax.psum_scatter(lax.dot_general(full_in, acts, (((0,), (1,)), ((), ())),...  18.7 us
  transfers between devices with their start and end apart: 7, of which 6 were waited for; matrix products, arithmetic and copies ran while one was open for 5% of the time, Pallas kernels for 0%

commit v1 on v0

v1 whole, which is shorter than its diff:
```python
import functools

import jax
import jax.numpy as jnp
from jax import lax
from jax.experimental import pallas as pl
from jax.experimental.pallas import tpu as pltpu
from jax.sharding import PartitionSpec as P

BF16, F32 = jnp.bfloat16, jnp.float32
VMEM_BYTES = 40 * 1024 * 1024


def flip(x, axis_name, bit):
    size = lax.axis_size(axis_name)
    return lax.ppermute(x, axis_name, [(i, i ^ bit) for i in range(size)])


def bits(axis_name):
    size = lax.axis_size(axis_name)
    assert size & (size - 1) == 0
    return [1 << k for k in range(size.bit_length() - 1)]


def reduce_halving(x, axis_name, axis):
    me = lax.axis_index(axis_name)
    for bit in bits(axis_name):
        shape = x.shape
        x = x.reshape(shape[:axis] + (shape[axis] // 2, 2) + shape[axis + 1 :])
        side = (me // bit) % 2
        sent = lax.dynamic_index_in_dim(x, 1 - side, axis + 1, False).astype(BF16)
        kept = lax.dynamic_index_in_dim(x, side, axis + 1, False)
        x = kept + flip(sent, axis_name, bit).astype(F32)
    return lax.squeeze(x, (axis,))


def gather_doubling(x, axis_name):
    me = lax.axis_index(axis_name)
    x = x[None]
    for bit in reversed(bits(axis_name)):
        other = flip(x, axis_name, bit)
        side = (me // bit) % 2
        low = jnp.where(side == 0, x, other)
        high = jnp.where(side == 0, other, x)
        x = jnp.stack([low, high], axis=1).reshape((2 * x.shape[0],) + x.shape[1:])
    return x


def gather_ring(block, axis_name):
    size = lax.axis_size(axis_name)
    half = size // 2
    order = list(range(0, half, 2)) + list(range(half - 1, 0, -2))
    hops = [(order[k], order[(k + 1) % half]) for k in range(half)]
    ahead = [[(2 * s + c, 2 * d + c) for s, d in hops] for c in (0, 1)]
    back = [[(d, s) for s, d in part] for part in ahead]
    me = lax.axis_index(axis_name)
    core, pair = me % 2, me // 2
    place = jnp.where(pair % 2 == 0, pair // 2, half - (pair + 1) // 2)

    def began(step):
        p = (place - step) % half
        return 2 * jnp.where(p < half // 2, 2 * p, 2 * (half - p) - 1) + core

    got = [(block, me)]
    one, two = block, block
    for step in range(1, half // 2):
        one = lax.ppermute(one, axis_name, ahead[0] + ahead[1])
        two = lax.ppermute(two, axis_name, back[0] + back[1])
        got += [(one, began(step)), (two, began(-step))]
    last = lax.ppermute(jnp.where(core == 0, one, two), axis_name, ahead[0] + back[1])
    got.append((last, began(half // 2)))
    return [p for b, j in got for p in ((b, j), (flip(b, axis_name, 1), j ^ 1))]


def tile_of(extent, most):
    return max(t for t in range(128, most + 1, 128) if extent % t == 0)


def project_kernel(basis_ref, acts_ref, out_ref, total):
    @pl.when(pl.program_id(0) == 0)
    def _():
        total[...] = jnp.zeros_like(total)

    total[...] += lax.dot_general(
        basis_ref[...], acts_ref[...], (((1,), (1,)), ((), ())), preferred_element_type=F32
    )

    @pl.when(pl.program_id(0) == pl.num_programs(0) - 1)
    def _():
        out_ref[...] = total[...]


def project(basis_t, acts):
    rows, units = basis_t.shape
    tokens = acts.shape[0]
    tile = tile_of(units, 2048)
    return pl.pallas_call(
        project_kernel,
        grid=(units // tile,),
        in_specs=[
            pl.BlockSpec((rows, tile), lambda i: (0, i)),
            pl.BlockSpec((tokens, tile), lambda i: (0, i)),
        ],
        out_specs=pl.BlockSpec((rows, tokens), lambda i: (0, 0)),
        out_shape=jax.ShapeDtypeStruct((rows, tokens), F32),
        scratch_shapes=[pltpu.VMEM((rows, tokens), F32)],
        compiler_params=pltpu.CompilerParams(vmem_limit_bytes=VMEM_BYTES),
        cost_estimate=pl.CostEstimate(
            flops=2 * rows * units * tokens, bytes_accessed=2 * units * (rows + tokens), transcendentals=0
        ),
        name="project_acts",
    )(basis_t, acts)


def update_kernel(basis_ref, back_ref, out_ref):
    out_ref[...] = lax.dot_general(
        basis_ref[...], back_ref[...], (((0,), (0,)), ((), ())), preferred_element_type=F32
    ).astype(out_ref.dtype)


def expand(basis_t, back):
    rows, units = basis_t.shape
    columns = back.shape[1]
    tile = tile_of(units, 1024)
    return pl.pallas_call(
        update_kernel,
        grid=(units // tile,),
        in_specs=[
            pl.BlockSpec((rows, tile), lambda i: (0, i)),
            pl.BlockSpec((rows, columns), lambda i: (0, 0)),
        ],
        out_specs=pl.BlockSpec((tile, columns), lambda i: (i, 0)),
        out_shape=jax.ShapeDtypeStruct((units, columns), BF16),
        compiler_params=pltpu.CompilerParams(vmem_limit_bytes=VMEM_BYTES),
        cost_estimate=pl.CostEstimate(
            flops=2 * rows * units * columns, bytes_accessed=2 * units * (rows + columns), transcendentals=0
        ),
        name="expand_update",
    )(basis_t, back)


def on_device(acts, grads, basis_in, basis_out, damping):
    tok_rows = acts.shape[0]
    n_dp, n_mp = lax.axis_size("dp"), lax.axis_size("mp")
    tokens_all = tok_rows * n_dp

    full_in_t = lax.all_gather(basis_in.T, "dp", axis=0, tiled=True)
    wide_grads = gather_doubling(grads, "mp")
    out_rows = gather_doubling(basis_out, "mp")
    out_units = basis_out.shape[0]
    grad_proj = jnp.zeros((tok_rows, basis_out.shape[1]), F32)
    for block, origin in gather_ring(basis_out, "dp"):
        part = origin * n_mp // n_dp
        first = (origin - part * (n_dp // n_mp)) * out_units
        columns = lax.dynamic_slice(wide_grads, (part, 0, first), (1, tok_rows, out_units))[0]
        grad_proj += jnp.dot(columns, block, preferred_element_type=F32)
    grad_proj = gather_doubling(grad_proj.astype(BF16), "mp")

    act_part = project(full_in_t, acts)
    act_part = act_part.reshape((n_mp, -1) + act_part.shape[1:])
    act_proj_t = reduce_halving(act_part, "mp", 0).astype(BF16)

    act_sq_t = (act_proj_t.astype(F32) ** 2).astype(BF16)
    grad_sq = (grad_proj.astype(F32) ** 2).astype(BF16)
    dims = (((1,), (1,)), ((), ()))

    def over_tokens(g, a):
        g = g.transpose(0, 2, 1)
        both = lax.dot_general(g.reshape((-1, tok_rows)), a, dims, preferred_element_type=F32)
        return both.reshape((n_dp, -1, a.shape[0]))

    partials = jnp.stack([over_tokens(grad_proj, act_proj_t), over_tokens(grad_sq, act_sq_t)])
    owned = reduce_halving(partials, "dp", 1)
    diag_t = owned[1] / tokens_all
    scaled_t = (owned[0] / (diag_t + damping[0])).astype(BF16)

    scaled_wide = gather_doubling(scaled_t, "dp").reshape((-1, scaled_t.shape[1]))
    rows_wide = out_rows.transpose(1, 0, 2).reshape((out_units, -1))
    back_part = lax.dot_general(
        scaled_wide, rows_wide, (((0,), (1,)), ((), ())), preferred_element_type=F32
    ).astype(BF16)
    back = gather_doubling(back_part, "mp").reshape((-1, out_units))
    return (expand(full_in_t, back), diag_t.T)


def solution(mesh):
    placed = (P("dp", "mp"), P("dp", "mp"), P("mp", "dp"), P("dp", "mp"), P())
    return jax.shard_map(
        on_device,
        mesh=mesh,
        in_specs=placed,
        out_specs=(P("mp", "dp"), P("mp", "dp")),
        check_vma=False,
    )
```

time: 479 us -> 252 us (0.53)
  waiting for transfers between devices: 356 us -> 153 us
  matrix products: 46.8 us -> 9.58 us
  blocking collectives: 32.5 us -> 0 us
  Pallas kernels: 0 us -> 32 us
  starting transfers between devices: 0.28 us -> 26.8 us
  local copies, waits for them, and re-layouts: 23.9 us -> 6.67 us
    all_gather x5 -> x1, waiting for transfers between devices: 233 us -> 20.9 us  [on_device(): full_in_t = lax.all_gather(basis_in.T, 'dp', axis=0, tiled=True)]
    ppermute x0 -> x28, waiting for transfers between devices: none -> 132 us  [the longest x3 59.9 us: gather_ring(): one = lax.ppermute(one, axis_name, ahead[0] + ahead[1])]
    unnamed x8 -> x1, waiting for transfers between devices: 104 us -> 0.68 us
    dot_general x6 -> x19, matrix products: 46.8 us -> 9.58 us  [the longest x16 8.13 us: on_device(): grad_proj += jnp.dot(columns, block, preferred_element_type=F32)]
    all_gather x2 -> x0, blocking collectives: 32.5 us -> none  [the longest x1 21.7 us: on_device(): scaled_wide = lax.all_gather(scaled, 'dp', axis=1, tiled=True)]
    pallas_call x0 -> x2, Pallas kernels: none -> 32 us  [the longest x1 21.2 us: expand(): pl.pallas_call(update_kernel, grid=(units // tile,), in_specs=[pl.BlockSp...]
    ppermute x0 -> x28, starting transfers between devices: none -> 26.8 us  [the longest x21 16.7 us: flip(): return lax.ppermute(x, axis_name, [(i, i ^ bit) for i in range(size)])]
    reduce_scatter x1 -> x0, waiting for transfers between devices: 18.7 us -> none  [on_device(): lax.psum_scatter(lax.dot_general(full_in, acts, (((0,), (1,)), ((), ())),...]
  transfers between devices with their start and end apart: 7 -> 29, of which waited for: 6 -> 19; matrix products, arithmetic and copies ran while one was open for 5% -> 5% of each run, Pallas kernels for 0% -> 0%
where the time goes in v1:
time: 252 us; the launch traced here: 251 us
  waiting for transfers between devices  153 us (61%)
  Pallas kernels  32 us (13%)
  starting transfers between devices  26.8 us (11%)
  between operations  15.3 us (6%)
  matrix products  9.58 us (4%)
  other arithmetic  7.21 us (3%)
  local copies, waits for them, and re-layouts  6.67 us (3%)
    ppermute x3, waiting for transfers between devices, gather_ring(): one = lax.ppermute(one, axis_name, ahead[0] + ahead[1])  59.9 us
    ppermute x21, waiting for transfers between devices, flip(): return lax.ppermute(x, axis_name, [(i, i ^ bit) for i in range(size)])  53.6 us
    pallas_call x1, Pallas kernels, expand(): pl.pallas_call(update_kernel, grid=(units // tile,), in_specs=[pl.BlockSp...  21.2 us
    all_gather x1, waiting for transfers between devices, on_device(): full_in_t = lax.all_gather(basis_in.T, 'dp', axis=0, tiled=True)  20.9 us
    ppermute x21, starting transfers between devices, flip(): return lax.ppermute(x, axis_name, [(i, i ^ bit) for i in range(size)])  16.7 us
    ppermute x1, waiting for transfers between devices, gather_ring(): lax.ppermute(jnp.where(core == 0, one, two), axis_name, ahead[0] + back[1])  15.7 us
    pallas_call x1, Pallas kernels, project(): pl.pallas_call(project_kernel, grid=(units // tile,), in_specs=[pl.BlockS...  10.8 us
    dot_general x16, matrix products, on_device(): grad_proj += jnp.dot(columns, block, preferred_element_type=F32)  8.13 us
  transfers between devices with their start and end apart: 29, of which 19 were waited for; matrix products, arithmetic and copies ran while one was open for 5% of the time, Pallas kernels for 0%

profile of v1, /device:TPU:0, one launch (start us, length us, event | category | flops | bytes accessed | tf_op | source)
XLA Modules:
  0.0 251.0 jit_solution(5332261679674905272)
XLA Ops:
  7.2 0.7 all-gather.2.cloned.1.call-update
  7.9 3.0 %collective-permute-start = (bf16[1,256,4096]{2,1,0:T(8,128)(2,1)}, bf16[1,256,4096]{2,1,0:T(8,128)(2,1)}, u32[]{:S(2)}, u32[]{:S(2)}) collective-permute-start(bf16[1,256,4096]{2,1,0:T(8,128)(2,1)} %bitcast.202), channel_id=1, source_target_pairs={{0,1},{1,0},{2,3},{3,2},{4,5},{5,4},{6,7},{7,6},{8,9},{9,8},{10,11... | collective-permute-start | bytes 6291464 | tf_op jit(solution)/shard_map/ppermute | solution.py:16
  10.9 1.6 collective-permute-start.2
  12.9 17.6 %collective-permute-done.2 = bf16[512,512]{1,0:T(8,128)(2,1)S(1)} collective-permute-done((bf16[512,512]{1,0:T(8,128)(2,1)}, bf16[512,512]{1,0:T(8,128)(2,1)S(1)}, u32[]{:S(2)}, u32[]{:S(2)}) %collective-permute-start.2) | collective-permute-done | bytes 524320 | tf_op jit(solution)/shard_map/ppermute | solution.py:67
  30.5 2.4 collective-permute-start.6
  33.0 0.7 collective-permute-start.8
  33.7 21.8 %collective-permute-done.6 = bf16[512,512]{1,0:T(8,128)(2,1)} collective-permute-done((bf16[512,512]{1,0:T(8,128)(2,1)S(1)}, bf16[512,512]{1,0:T(8,128)(2,1)}, u32[]{:S(2)}, u32[]{:S(2)}) %collective-permute-start.6) | collective-permute-done | bytes 524320 | tf_op jit(solution)/shard_map/ppermute | solution.py:67
  55.6 2.4 collective-permute-start.10
  58.1 0.7 collective-permute-start.12
  59.3 20.5 %collective-permute-done.10 = bf16[512,512]{1,0:T(8,128)(2,1)S(1)} collective-permute-done((bf16[512,512]{1,0:T(8,128)(2,1)}, bf16[512,512]{1,0:T(8,128)(2,1)S(1)}, u32[]{:S(2)}, u32[]{:S(2)}) %collective-permute-start.10) | collective-permute-done | bytes 524320 | tf_op jit(solution)/shard_map/ppermute | solution.py:67
  79.8 2.4 collective-permute-done.12
  82.3 0.6 collective-permute-start.9
  82.9 1.9 select_bitcast_fusion
  85.1 0.7 copy-done.7
  86.1 1.4 fusion.48
  87.5 1.4 fusion.45
  88.9 1.9 collective-permute-start.14
  90.8 1.3 fusion.55
  93.2 0.6 collective-permute-start.13
  93.8 15.7 %collective-permute-done.14 = bf16[512,512]{1,0:T(8,128)(2,1)S(1)} collective-permute-done((bf16[512,512]{1,0:T(8,128)(2,1)S(1)}, bf16[512,512]{1,0:T(8,128)(2,1)S(1)}, u32[]{:S(2)}, u32[]{:S(2)}) %collective-permute-start.14) | collective-permute-done | bytes 524320 | tf_op jit(solution)/shard_map/ppermute | solution.py:70
  112.2 8.7 %collective-permute-done.16 = bf16[1,256,512]{2,1,0:T(8,128)(2,1)S(1)} collective-permute-done((bf16[1,256,512]{2,1,0:T(8,128)(2,1)S(1)}, bf16[1,256,512]{2,1,0:T(8,128)(2,1)S(1)}, u32[]{:S(2)}, u32[]{:S(2)}) %collective-permute-start.16) | collective-permute-done | bytes 262176 | tf_op jit(solution)/shard_map/ppermute | solution.py:16
  121.0 20.9 %all-gather.2.cloned.1.call-done.basis_ref = bf16[640,14336]{1,0:T(8,128)(2,1)} async-done(((bf16[40,14336]{1,0:T(8,128)(2,1)}), bf16[640,14336]{1,0:T(8,128)(2,1)}) %all-gather.2.cloned.1.call-update) | async-done | bytes 18350096 | tf_op jit(solution)/shard_map/all_gather | solution.py:147
  141.8 3.1 %copy-done = bf16[256,14336]{1,0:T(8,128)(2,1)S(1)} copy-done((bf16[256,14336]{1,0:T(8,128)(2,1)S(1)}, bf16[256,14336]{1,0:T(8,128)(2,1)}, u32[]{:S(2)}) %copy-start) | copy-done | bytes 7340056
  144.9 10.8 %project_acts.1 = f32[640,256]{1,0:T(8,128)S(1)} custom-call(bf16[640,14336]{1,0:T(8,128)(2,1)} %all-gather.2.cloned.1.call-done.basis_ref, bf16[256,14336]{1,0:T(8,128)(2,1)S(1)} %copy-done), custom_call_target="tpu_custom_call" | custom-call | flops 4697620480 | bytes 25690112 | tf_op jit(solution)/shard_map/project_acts/pallas_call | solution.py:97
  155.7 0.6 collective-permute-start.17
  156.4 1.0 copy.15
  157.7 4.5 %collective-permute-done.17 = bf16[1,320,256]{2,1,0:T(8,128)(2,1)S(1)} collective-permute-done((bf16[1,320,256]{2,1,0:T(8,128)(2,1)S(1)}, bf16[1,320,256]{2,1,0:T(8,128)(2,1)S(1)}, u32[]{:S(2)}, u32[]{:S(2)}) %collective-permute-start.17) | collective-permute-done | bytes 163872 | tf_op jit(solution)/shard_map/ppermute | solution.py:16
  163.1 1.0 fusion.14
  164.2 2.6 %collective-permute-done.18 = bf16[2,8,64,320]{3,2,1,0:T(8,128)(2,1)} collective-permute-done((bf16[2,8,64,320]{3,2,1,0:T(8,128)(2,1)}, bf16[2,8,64,320]{3,2,1,0:T(8,128)(2,1)}, u32[]{:S(2)}, u32[]{:S(2)}) %collective-permute-start.18) | collective-permute-done | bytes 655392 | tf_op jit(solution)/shard_map/ppermute | solution.py:16
  166.8 1.3 fusion.4
  168.1 1.1 copy-done.1
  169.8 10.7 %collective-permute-done.19 = bf16[2,4,64,320]{3,2,1,0:T(8,128)(2,1)S(1)} collective-permute-done((bf16[2,4,64,320]{3,2,1,0:T(8,128)(2,1)S(1)}, bf16[2,4,64,320]{3,2,1,0:T(8,128)(2,1)S(1)}, u32[]{:S(2)}, u32[]{:S(2)}) %collective-permute-start.19) | collective-permute-done | bytes 327712 | tf_op jit(solution)/shard_map/ppermute | solution.py:16
  180.5 1.2 bitcast_add_fusion
  181.8 1.6 collective-permute-start.20
  183.4 4.5 %collective-permute-done.20 = bf16[2,2,64,320]{3,2,1,0:T(8,128)(2,1)S(1)} collective-permute-done((bf16[2,2,64,320]{3,2,1,0:T(8,128)(2,1)S(1)}, bf16[2,2,64,320]{3,2,1,0:T(8,128)(2,1)S(1)}, u32[]{:S(2)}, u32[]{:S(2)}) %collective-permute-start.20) | collective-permute-done | bytes 163872 | tf_op jit(solution)/shard_map/ppermute | solution.py:16
  188.0 2.7 %collective-permute-start.21 = (bf16[2,1,64,320]{3,2,1,0:T(8,128)(2,1)S(1)}, bf16[2,1,64,320]{3,2,1,0:T(8,128)(2,1)S(1)}, u32[]{:S(2)}, u32[]{:S(2)}) collective-permute-start(bf16[2,1,64,320]{3,2,1,0:T(8,128)(2,1)S(1)} %dynamic-slice_convert_fusion.2), channel_id=1, source_target_pairs={{0,16},{2,18},{4,20},{6,22},{8,24},{10,26},{12,28},{14,30},{16,0},... | collective-permute-start | bytes 245768 | tf_op jit(solution)/shard_map/ppermute | solution.py:16
  191.3 2.3 collective-permute-done.21
  193.6 0.7 fusion.81
  194.3 2.7 %collective-permute-start.22 = (bf16[1,64,320]{2,1,0:T(8,128)(2,1)S(1)}, bf16[1,64,320]{2,1,0:T(8,128)(2,1)S(1)}, u32[]{:S(2)}, u32[]{:S(2)}) collective-permute-start(bf16[1,64,320]{2,1,0:T(8,128)(2,1)S(1)} %get-tuple-element.15), channel_id=1, source_target_pairs={{0,16},{2,18},{4,20},{6,22},{8,24},{10,26},{12,28},{14,30},{16,0},... | collective-permute-start | bytes 122888 | tf_op jit(solution)/shard_map/ppermute | solution.py:16
  197.0 2.4 collective-permute-done.22
  199.4 2.3 collective-permute-start.23
  201.7 2.6 %collective-permute-done.23 = bf16[2,64,320]{2,1,0:T(8,128)(2,1)S(1)} collective-permute-done((bf16[2,64,320]{2,1,0:T(8,128)(2,1)S(1)}, bf16[2,64,320]{2,1,0:T(8,128)(2,1)S(1)}, u32[]{:S(2)}, u32[]{:S(2)}) %collective-permute-start.23) | collective-permute-done | bytes 81952 | tf_op jit(solution)/shard_map/ppermute | solution.py:16
  205.0 0.6 collective-permute-start.26
  205.6 4.5 %collective-permute-done.24 = bf16[4,64,320]{2,1,0:T(8,128)(2,1)S(1)} collective-permute-done((bf16[4,64,320]{2,1,0:T(8,128)(2,1)S(1)}, bf16[4,64,320]{2,1,0:T(8,128)(2,1)S(1)}, u32[]{:S(2)}, u32[]{:S(2)}) %collective-permute-start.24) | collective-permute-done | bytes 163872 | tf_op jit(solution)/shard_map/ppermute | solution.py:16
  210.4 4.2 %collective-permute-done.26 = bf16[1,512,512]{1,2,0:T(8,128)(2,1)S(1)} collective-permute-done((bf16[1,512,512]{1,2,0:T(8,128)(2,1)S(1)}, bf16[1,512,512]{1,2,0:T(8,128)(2,1)S(1)}, u32[]{:S(2)}, u32[]{:S(2)}) %collective-permute-start.26) | collective-permute-done | bytes 524320 | tf_op jit(solution)/shard_map/ppermute | solution.py:16
  215.2 0.5 fusion.12
  216.2 6.7 %collective-permute-done.27 = bf16[1,320,512]{2,1,0:T(8,128)(2,1)S(1)} collective-permute-done((bf16[1,320,512]{2,1,0:T(8,128)(2,1)S(1)}, bf16[1,320,512]{2,1,0:T(8,128)(2,1)S(1)}, u32[]{:S(2)}, u32[]{:S(2)}) %collective-permute-start.27) | collective-permute-done | bytes 327712 | tf_op jit(solution)/shard_map/ppermute | solution.py:16
  223.0 21.2 %expand_update.1 = bf16[14336,512]{1,0:T(8,128)(2,1)} custom-call(bf16[640,14336]{1,0:T(8,128)(2,1)} %all-gather.2.cloned.1.call-done.basis_ref, bf16[640,512]{1,0:T(8,128)(2,1)S(1)} %bitcast.194), custom_call_target="tpu_custom_call" | custom-call | flops 9395240960 | bytes 33030144 | tf_op jit(solution)/shard_map/expand_update/pallas_call | solution.py:125
  (86 shorter events, 9.7 us)
Async XLA Ops:
  7.2 75.7 %copy-start.3 = (bf16[256,4096]{1,0:T(8,128)(2,1)S(1)}, bf16[256,4096]{1,0:T(8,128)(2,1)}, u32[]{:S(2)}) copy-start(bf16[256,4096]{1,0:T(8,128)(2,1)} %param.6) | copy-start | bytes 6291460
  7.2 134.7 %all-gather.2.cloned.1.call-start = ((), (), s32[]{:S(2)}) async-start(), calls=%async_computation | async-start | bytes 19496960 | tf_op jit(solution)/shard_map/all_gather | solution.py:147
  7.9 74.4 %collective-permute-start = (bf16[1,256,4096]{2,1,0:T(8,128)(2,1)}, bf16[1,256,4096]{2,1,0:T(8,128)(2,1)}, u32[]{:S(2)}, u32[]{:S(2)}) collective-permute-start(bf16[1,256,4096]{2,1,0:T(8,128)(2,1)} %bitcast.202), channel_id=1, source_target_pairs={{0,1},{1,0},{2,3},{3,2},{4,5},{5,4},{6,7},{7,6},{8,9},{9,8},{10,11... | collective-permute-start | bytes 6291464 | tf_op jit(solution)/shard_map/ppermute | solution.py:16
  10.9 19.6 %collective-permute-start.2 = (bf16[512,512]{1,0:T(8,128)(2,1)}, bf16[512,512]{1,0:T(8,128)(2,1)S(1)}, u32[]{:S(2)}, u32[]{:S(2)}) collective-permute-start(bf16[512,512]{1,0:T(8,128)(2,1)} %param.8), channel_id=1, source_target_pairs={{0,8},{8,16},{16,24},{24,28},{28,20},{20,12},{12,4},{4,0},{2,10},{... | collective-permute-start | bytes 1572872 | tf_op jit(solution)/shard_map/ppermute | solution.py:67
  12.5 20.5 %collective-permute-start.4 = (bf16[512,512]{1,0:T(8,128)(2,1)}, bf16[512,512]{1,0:T(8,128)(2,1)S(1)}, u32[]{:S(2)}, u32[]{:S(2)}) collective-permute-start(bf16[512,512]{1,0:T(8,128)(2,1)} %param.8), channel_id=1, source_target_pairs={{8,0},{16,8},{24,16},{28,24},{20,28},{12,20},{4,12},{0,4},{10,2},{... | collective-permute-start | bytes 1572872 | tf_op jit(solution)/shard_map/ppermute | solution.py:68
  30.5 3.2 %copy-start.8 = (bf16[512,512]{1,0:T(8,128)(2,1)}, bf16[512,512]{1,0:T(8,128)(2,1)S(1)}, u32[]{:S(2)}) copy-start(bf16[512,512]{1,0:T(8,128)(2,1)S(1)} %collective-permute-done.2) | copy-start | bytes 1572868
  30.5 25.1 %collective-permute-start.6 = (bf16[512,512]{1,0:T(8,128)(2,1)S(1)}, bf16[512,512]{1,0:T(8,128)(2,1)}, u32[]{:S(2)}, u32[]{:S(2)}) collective-permute-start(bf16[512,512]{1,0:T(8,128)(2,1)S(1)} %collective-permute-done.2), channel_id=1, source_target_pairs={{0,8},{8,16},{16,24},{24,28},{28,20},{20,12},{12,4},{4,0},{2,10},{... | collective-permute-start | bytes 1572872 | tf_op jit(solution)/shard_map/ppermute | solution.py:67
  33.0 25.0 %copy-start.6 = (bf16[512,512]{1,0:T(8,128)(2,1)}, bf16[512,512]{1,0:T(8,128)(2,1)S(1)}, u32[]{:S(2)}) copy-start(bf16[512,512]{1,0:T(8,128)(2,1)S(1)} %collective-permute-done.4) | copy-start | bytes 1572868
  33.0 25.1 %collective-permute-start.8 = (bf16[512,512]{1,0:T(8,128)(2,1)S(1)}, bf16[512,512]{1,0:T(8,128)(2,1)}, u32[]{:S(2)}, u32[]{:S(2)}) collective-permute-start(bf16[512,512]{1,0:T(8,128)(2,1)S(1)} %collective-permute-done.4), channel_id=1, source_target_pairs={{8,0},{16,8},{24,16},{28,24},{20,28},{12,20},{4,12},{0,4},{10,2},{... | collective-permute-start | bytes 1572872 | tf_op jit(solution)/shard_map/ppermute | solution.py:68
  55.6 24.2 %collective-permute-start.10 = (bf16[512,512]{1,0:T(8,128)(2,1)}, bf16[512,512]{1,0:T(8,128)(2,1)S(1)}, u32[]{:S(2)}, u32[]{:S(2)}) collective-permute-start(bf16[512,512]{1,0:T(8,128)(2,1)} %collective-permute-done.6), channel_id=1, source_target_pairs={{0,8},{8,16},{16,24},{24,28},{28,20},{20,12},{12,4},{4,0},{2,10},{... | collective-permute-start | bytes 1572872 | tf_op jit(solution)/shard_map/ppermute | solution.py:67
  58.1 24.1 %collective-permute-start.12 = (bf16[512,512]{1,0:T(8,128)(2,1)}, bf16[512,512]{1,0:T(8,128)(2,1)S(1)}, u32[]{:S(2)}, u32[]{:S(2)}) collective-permute-start(bf16[512,512]{1,0:T(8,128)(2,1)} %collective-permute-done.8), channel_id=1, source_target_pairs={{8,0},{16,8},{24,16},{28,24},{20,28},{12,20},{4,12},{0,4},{10,2},{... | collective-permute-start | bytes 1572872 | tf_op jit(solution)/shard_map/ppermute | solution.py:68
  58.8 30.1 %collective-permute-start.1 = (bf16[512,512]{1,0:T(8,128)(2,1)}, bf16[512,512]{1,0:T(8,128)(2,1)}, u32[]{:S(2)}, u32[]{:S(2)}) collective-permute-start(bf16[512,512]{1,0:T(8,128)(2,1)} %param.8), channel_id=1, source_target_pairs={{0,2},{2,0},{4,6},{6,4},{8,10},{10,8},{12,14},{14,12},{16,18},{18,... | collective-permute-start | bytes 1572872 | tf_op jit(solution)/shard_map/ppermute | solution.py:16
  58.9 33.6 %collective-permute-start.3 = (bf16[512,512]{1,0:T(8,128)(2,1)}, bf16[512,512]{1,0:T(8,128)(2,1)S(1)}, u32[]{:S(2)}, u32[]{:S(2)}) collective-permute-start(bf16[512,512]{1,0:T(8,128)(2,1)} %copy-done.8), channel_id=1, source_target_pairs={{0,2},{2,0},{4,6},{6,4},{8,10},{10,8},{12,14},{14,12},{16,18},{18,... | collective-permute-start | bytes 1572872 | tf_op jit(solution)/shard_map/ppermute | solution.py:16
  79.8 13.4 %collective-permute-start.5 = (bf16[512,512]{1,0:T(8,128)(2,1)}, bf16[512,512]{1,0:T(8,128)(2,1)S(1)}, u32[]{:S(2)}, u32[]{:S(2)}) collective-permute-start(bf16[512,512]{1,0:T(8,128)(2,1)} %copy-done.6), channel_id=1, source_target_pairs={{0,2},{2,0},{4,6},{6,4},{8,10},{10,8},{12,14},{14,12},{16,18},{18,... | collective-permute-start | bytes 1572872 | tf_op jit(solution)/shard_map/ppermute | solution.py:16
  82.2 27.6 %collective-permute-start.7 = (bf16[512,512]{1,0:T(8,128)(2,1)}, bf16[512,512]{1,0:T(8,128)(2,1)S(1)}, u32[]{:S(2)}, u32[]{:S(2)}) collective-permute-start(bf16[512,512]{1,0:T(8,128)(2,1)} %collective-permute-done.6), channel_id=1, source_target_pairs={{0,2},{2,0},{4,6},{6,4},{8,10},{10,8},{12,14},{14,12},{16,18},{18,... | collective-permute-start | bytes 1572872 | tf_op jit(solution)/shard_map/ppermute | solution.py:16
  82.3 2.5 copy-start.4
  82.3 28.2 %collective-permute-start.9 = (bf16[512,512]{1,0:T(8,128)(2,1)}, bf16[512,512]{1,0:T(8,128)(2,1)S(1)}, u32[]{:S(2)}, u32[]{:S(2)}) collective-permute-start(bf16[512,512]{1,0:T(8,128)(2,1)} %collective-permute-done.8), channel_id=1, source_target_pairs={{0,2},{2,0},{4,6},{6,4},{8,10},{10,8},{12,14},{14,12},{16,18},{18,... | collective-permute-start | bytes 1572872 | tf_op jit(solution)/shard_map/ppermute | solution.py:16
  84.8 1.0 copy-start.7
  88.9 3.3 %copy-start.9 = (bf16[512,512]{1,0:T(8,128)(2,1)S(1)}, bf16[512,512]{1,0:T(8,128)(2,1)}, u32[]{:S(2)}) copy-start(bf16[512,512]{1,0:T(8,128)(2,1)} %copy-done.8) | copy-start | bytes 1572868
  88.9 20.6 %collective-permute-start.14 = (bf16[512,512]{1,0:T(8,128)(2,1)S(1)}, bf16[512,512]{1,0:T(8,128)(2,1)S(1)}, u32[]{:S(2)}, u32[]{:S(2)}) collective-permute-start(bf16[512,512]{1,0:T(8,128)(2,1)S(1)} %broadcast_select_fusion), channel_id=1, source_target_pairs={{0,8},{8,16},{16,24},{24,28},{28,20},{20,12},{12,4},{4,0},{10,2},{... | collective-permute-start | bytes 1572872 | tf_op jit(solution)/shard_map/ppermute | solution.py:70
  92.5 18.3 %collective-permute-start.11 = (bf16[512,512]{1,0:T(8,128)(2,1)S(1)}, bf16[512,512]{1,0:T(8,128)(2,1)S(1)}, u32[]{:S(2)}, u32[]{:S(2)}) collective-permute-start(bf16[512,512]{1,0:T(8,128)(2,1)S(1)} %collective-permute-done.10), channel_id=1, source_target_pairs={{0,2},{2,0},{4,6},{6,4},{8,10},{10,8},{12,14},{14,12},{16,18},{18,... | collective-permute-start | bytes 1572872 | tf_op jit(solution)/shard_map/ppermute | solution.py:16
  93.2 18.2 %collective-permute-start.13 = (bf16[512,512]{1,0:T(8,128)(2,1)S(1)}, bf16[512,512]{1,0:T(8,128)(2,1)S(1)}, u32[]{:S(2)}, u32[]{:S(2)}) collective-permute-start(bf16[512,512]{1,0:T(8,128)(2,1)S(1)} %collective-permute-done.12), channel_id=1, source_target_pairs={{0,2},{2,0},{4,6},{6,4},{8,10},{10,8},{12,14},{14,12},{16,18},{18,... | collective-permute-start | bytes 1572872 | tf_op jit(solution)/shard_map/ppermute | solution.py:16
  109.5 2.3 collective-permute-start.15
  112.1 8.8 %collective-permute-start.16 = (bf16[1,256,512]{2,1,0:T(8,128)(2,1)S(1)}, bf16[1,256,512]{2,1,0:T(8,128)(2,1)S(1)}, u32[]{:S(2)}, u32[]{:S(2)}) collective-permute-start(bf16[1,256,512]{2,1,0:T(8,128)(2,1)S(1)} %fusion.13), channel_id=1, source_target_pairs={{0,1},{1,0},{2,3},{3,2},{4,5},{5,4},{6,7},{7,6},{8,9},{9,8},{10,11... | collective-permute-start | bytes 786440 | tf_op jit(solution)/shard_map/ppermute | solution.py:16
  141.8 3.1 %copy-start = (bf16[256,14336]{1,0:T(8,128)(2,1)S(1)}, bf16[256,14336]{1,0:T(8,128)(2,1)}, u32[]{:S(2)}) copy-start(bf16[256,14336]{1,0:T(8,128)(2,1)} %acts_ref.1) | copy-start | bytes 22020100
  155.7 6.4 %collective-permute-start.17 = (bf16[1,320,256]{2,1,0:T(8,128)(2,1)S(1)}, bf16[1,320,256]{2,1,0:T(8,128)(2,1)S(1)}, u32[]{:S(2)}, u32[]{:S(2)}) collective-permute-start(bf16[1,320,256]{2,1,0:T(8,128)(2,1)S(1)} %fusion.76), channel_id=1, source_target_pairs={{0,1},{1,0},{2,3},{3,2},{4,5},{5,4},{6,7},{7,6},{8,9},{9,8},{10,11... | collective-permute-start | bytes 491528 | tf_op jit(solution)/shard_map/ppermute | solution.py:16
  157.7 5.0 %copy-start.2 = (bf16[2,512,256]{2,1,0:T(8,128)(2,1)S(1)}, bf16[2,512,256]{2,1,0:T(8,128)(2,1)}, u32[]{:S(2)}) copy-start(bf16[2,512,256]{2,1,0:T(8,128)(2,1)} %copy.15) | copy-start | bytes 1572868
  164.1 2.6 %collective-permute-start.18 = (bf16[2,8,64,320]{3,2,1,0:T(8,128)(2,1)}, bf16[2,8,64,320]{3,2,1,0:T(8,128)(2,1)}, u32[]{:S(2)}, u32[]{:S(2)}) collective-permute-start(bf16[2,8,64,320]{3,2,1,0:T(8,128)(2,1)} %fusion.14), channel_id=1, source_target_pairs={{0,2},{2,0},{4,6},{6,4},{8,10},{10,8},{12,14},{14,12},{16,18},{18,... | collective-permute-start | bytes 1966088 | tf_op jit(solution)/shard_map/ppermute | solution.py:16
  168.1 1.1 copy-start.1
  169.3 11.2 %collective-permute-start.19 = (bf16[2,4,64,320]{3,2,1,0:T(8,128)(2,1)S(1)}, bf16[2,4,64,320]{3,2,1,0:T(8,128)(2,1)S(1)}, u32[]{:S(2)}, u32[]{:S(2)}) collective-permute-start(bf16[2,4,64,320]{3,2,1,0:T(8,128)(2,1)S(1)} %fusion.16), channel_id=1, source_target_pairs={{0,4},{2,6},{4,0},{6,2},{8,12},{10,14},{12,8},{14,10},{16,20},{18,... | collective-permute-start | bytes 983048 | tf_op jit(solution)/shard_map/ppermute | solution.py:16
  181.7 23.1 %copy-start.5 = (bf16[512,512]{1,0:T(8,128)(2,1)S(1)}, bf16[512,512]{1,0:T(8,128)(2,1)}, u32[]{:S(2)}) copy-start(bf16[512,512]{1,0:T(8,128)(2,1)} %param.8) | copy-start | bytes 1572868
  181.8 6.2 %collective-permute-start.20 = (bf16[2,2,64,320]{3,2,1,0:T(8,128)(2,1)S(1)}, bf16[2,2,64,320]{3,2,1,0:T(8,128)(2,1)S(1)}, u32[]{:S(2)}, u32[]{:S(2)}) collective-permute-start(bf16[2,2,64,320]{3,2,1,0:T(8,128)(2,1)S(1)} %fusion.75), channel_id=1, source_target_pairs={{0,8},{2,10},{4,12},{6,14},{8,0},{10,2},{12,4},{14,6},{16,24},{18,... | collective-permute-start | bytes 491528 | tf_op jit(solution)/shard_map/ppermute | solution.py:16
  188.0 5.6 %collective-permute-start.21 = (bf16[2,1,64,320]{3,2,1,0:T(8,128)(2,1)S(1)}, bf16[2,1,64,320]{3,2,1,0:T(8,128)(2,1)S(1)}, u32[]{:S(2)}, u32[]{:S(2)}) collective-permute-start(bf16[2,1,64,320]{3,2,1,0:T(8,128)(2,1)S(1)} %dynamic-slice_convert_fusion.2), channel_id=1, source_target_pairs={{0,16},{2,18},{4,20},{6,22},{8,24},{10,26},{12,28},{14,30},{16,0},... | collective-permute-start | bytes 245768 | tf_op jit(solution)/shard_map/ppermute | solution.py:16
  194.3 5.0 %collective-permute-start.22 = (bf16[1,64,320]{2,1,0:T(8,128)(2,1)S(1)}, bf16[1,64,320]{2,1,0:T(8,128)(2,1)S(1)}, u32[]{:S(2)}, u32[]{:S(2)}) collective-permute-start(bf16[1,64,320]{2,1,0:T(8,128)(2,1)S(1)} %get-tuple-element.15), channel_id=1, source_target_pairs={{0,16},{2,18},{4,20},{6,22},{8,24},{10,26},{12,28},{14,30},{16,0},... | collective-permute-start | bytes 122888 | tf_op jit(solution)/shard_map/ppermute | solution.py:16
  199.4 4.9 %collective-permute-start.23 = (bf16[2,64,320]{2,1,0:T(8,128)(2,1)S(1)}, bf16[2,64,320]{2,1,0:T(8,128)(2,1)S(1)}, u32[]{:S(2)}, u32[]{:S(2)}) collective-permute-start(bf16[2,64,320]{2,1,0:T(8,128)(2,1)S(1)} %maximum_bitcast_fusion), channel_id=1, source_target_pairs={{0,8},{2,10},{4,12},{6,14},{8,0},{10,2},{12,4},{14,6},{16,24},{18,... | collective-permute-start | bytes 245768 | tf_op jit(solution)/shard_map/ppermute | solution.py:16
  204.4 5.7 %collective-permute-start.24 = (bf16[4,64,320]{2,1,0:T(8,128)(2,1)S(1)}, bf16[4,64,320]{2,1,0:T(8,128)(2,1)S(1)}, u32[]{:S(2)}, u32[]{:S(2)}) collective-permute-start(bf16[4,64,320]{2,1,0:T(8,128)(2,1)S(1)} %bitcast.207), channel_id=1, source_target_pairs={{0,4},{2,6},{4,0},{6,2},{8,12},{10,14},{12,8},{14,10},{16,20},{18,... | collective-permute-start | bytes 491528 | tf_op jit(solution)/shard_map/ppermute | solution.py:16
  205.0 9.6 %collective-permute-start.26 = (bf16[1,512,512]{1,2,0:T(8,128)(2,1)S(1)}, bf16[1,512,512]{1,2,0:T(8,128)(2,1)S(1)}, u32[]{:S(2)}, u32[]{:S(2)}) collective-permute-start(bf16[1,512,512]{1,2,0:T(8,128)(2,1)S(1)} %bitcast.199), channel_id=1, source_target_pairs={{0,1},{1,0},{2,3},{3,2},{4,5},{5,4},{6,7},{7,6},{8,9},{9,8},{10,11... | collective-permute-start | bytes 1572872 | tf_op jit(solution)/shard_map/ppermute | solution.py:16
  210.3 4.5 %collective-permute-start.25 = (bf16[8,64,320]{2,1,0:T(8,128)(2,1)S(1)}, bf16[8,64,320]{2,1,0:T(8,128)(2,1)S(1)}, u32[]{:S(2)}, u32[]{:S(2)}) collective-permute-start(bf16[8,64,320]{2,1,0:T(8,128)(2,1)S(1)} %bitcast.203), channel_id=1, source_target_pairs={{0,2},{2,0},{4,6},{6,4},{8,10},{10,8},{12,14},{14,12},{16,18},{18,... | collective-permute-start | bytes 983048 | tf_op jit(solution)/shard_map/ppermute | solution.py:16
  215.7 7.1 %collective-permute-start.27 = (bf16[1,320,512]{2,1,0:T(8,128)(2,1)S(1)}, bf16[1,320,512]{2,1,0:T(8,128)(2,1)S(1)}, u32[]{:S(2)}, u32[]{:S(2)}) collective-permute-start(bf16[1,320,512]{2,1,0:T(8,128)(2,1)S(1)} %fusion.12), channel_id=1, source_target_pairs={{0,1},{1,0},{2,3},{3,2},{4,5},{5,4},{6,7},{7,6},{8,9},{9,8},{10,11... | collective-permute-start | bytes 983048 | tf_op jit(solution)/shard_map/ppermute | solution.py:16
Sparse Core Ops, SparseCore 0:
  9.6 132.1 all-gather.1

commit v2 on v0

v2 whole, which is shorter than its diff:
```python
import functools

import jax
import jax.numpy as jnp
from jax import lax
from jax.experimental import pallas as pl
from jax.experimental.pallas import tpu as pltpu
from jax.sharding import PartitionSpec as P

BF16, F32 = jnp.bfloat16, jnp.float32
VMEM_BYTES = 48 * 1024 * 1024
EXPAND_ROWS = 4096


def flip(x, axis_name, bit):
    size = lax.axis_size(axis_name)
    return lax.ppermute(x, axis_name, [(i, i ^ bit) for i in range(size)])


def bits(axis_name):
    size = lax.axis_size(axis_name)
    assert size & (size - 1) == 0
    return [1 << k for k in range(size.bit_length() - 1)]


def gather_doubling(x, axis_name):
    me = lax.axis_index(axis_name)
    x = x[None]
    for bit in reversed(bits(axis_name)):
        other = flip(x, axis_name, bit)
        side = (me // bit) % 2
        low = jnp.where(side == 0, x, other)
        high = jnp.where(side == 0, other, x)
        x = jnp.stack([low, high], axis=1).reshape((2 * x.shape[0],) + x.shape[1:])
    return x


def ring_hops(size):
    half = size // 2
    order = list(range(0, half, 2)) + list(range(half - 1, 0, -2))
    hops = [(order[k], order[(k + 1) % half]) for k in range(half)]
    ahead = [[(2 * s + c, 2 * d + c) for s, d in hops] for c in (0, 1)]
    return ahead, [[(d, s) for s, d in part] for part in ahead]


def ring_place(axis_name):
    half = lax.axis_size(axis_name) // 2
    pair = lax.axis_index(axis_name) // 2
    place = jnp.where(pair % 2 == 0, pair // 2, half - (pair + 1) // 2)

    def began(step):
        p = (place - step) % half
        return jnp.where(p < half // 2, 2 * p, 2 * (half - p) - 1)

    return began


def tile_of(extent, most):
    return max(t for t in range(128, most + 1, 128) if extent % t == 0)


def whole_block(shape):
    return pl.BlockSpec(shape, lambda *_: (0,) * len(shape))


def halves_spec(shape, tiles, second):
    if second:
        return pl.BlockSpec(shape, lambda i, *_: (jnp.maximum(i - tiles, 0), 0))
    return pl.BlockSpec(shape, lambda i, *_: (jnp.minimum(i, tiles - 1), 0))


def tile_index(i, tiles, at_ref):
    return jnp.where(i < tiles, at_ref[0], 1 - at_ref[0]) * tiles + i % tiles


def project_kernel(tiles, rows, at_ref, acts_ref, *refs):
    sums_ref = refs[-1]
    count = len(refs) // 2
    step = pl.program_id(0)
    lanes = refs[0].shape[1]

    @pl.when(step == 0)
    def _():
        sums_ref[...] = jnp.zeros_like(sums_ref)

    def add(pieces):
        total = sums_ref[...]
        for c in range(pieces[0].shape[0] // rows):
            part = jnp.concatenate([piece[c * rows : (c + 1) * rows] for piece in pieces], axis=0)
            total += lax.dot_general(
                part,
                acts_ref[:, c * lanes : (c + 1) * lanes],
                (((1,), (1,)), ((), ())),
                preferred_element_type=F32,
            )
        sums_ref[...] = total

    pl.when(step < tiles)(lambda: add(refs[:count]))
    pl.when(step >= tiles)(lambda: add(refs[count:-1]))


def project(owns, others, rows, core, acts, costed=False):
    tokens, units = acts.shape
    lanes = owns[0].shape[1]
    chunks = units // 2 // lanes
    if rows % 16:
        total = 0
        for pieces, side in ((owns, core), (others, 1 - core)):
            half = lax.dynamic_slice(acts, (0, side * (units // 2)), (tokens, units // 2))
            plain = [unchunk(piece, rows, chunks) for piece in pieces]
            total += jnp.concatenate(
                [lax.dot_general(p, half, (((1,), (1,)), ((), ())), preferred_element_type=F32) for p in plain]
            )
        return total
    group = max(g for g in range(1, chunks + 1) if chunks % g == 0 and g * lanes <= 4096)
    tiles = chunks // group
    return pl.pallas_call(
        functools.partial(project_kernel, tiles, rows),
        grid_spec=pltpu.PrefetchScalarGridSpec(
            num_scalar_prefetch=1,
            grid=(2 * tiles,),
            in_specs=[pl.BlockSpec((tokens, group * lanes), lambda i, at_ref: (0, tile_index(i, tiles, at_ref)))]
            + [halves_spec((group * rows, lanes), tiles, False)] * len(owns)
            + [halves_spec((group * rows, lanes), tiles, True)] * len(owns),
            out_specs=whole_block((len(owns) * rows, tokens)),
        ),
        out_shape=jax.ShapeDtypeStruct((len(owns) * rows, tokens), F32),
        compiler_params=pltpu.CompilerParams(vmem_limit_bytes=VMEM_BYTES),
        cost_estimate=pl.CostEstimate(
            flops=2 * len(owns) * rows * units * tokens if costed else 1,
            bytes_accessed=2 * units * (len(owns) * rows + tokens) if costed else 1,
            transcendentals=0,
        ),
        name="project_acts",
    )(core.astype(jnp.int32).reshape((1,)), acts, *owns, *others)


def unchunk(piece, rows, chunks):
    lanes = piece.shape[1]
    return piece[: chunks * rows].reshape((chunks, rows, lanes)).transpose(1, 0, 2).reshape((rows, -1))


def add_grads_kernel(at_ref, *refs):
    total_ref, out_ref, held, arrived = refs[-4:]
    count = (len(refs) - 4) // 2
    copies = []
    for k in range(count):
        start = refs[k].shape[0] - held.shape[1]
        copies.append(
            pltpu.make_async_copy(refs[k].at[pl.ds(start, held.shape[1])], held.at[k], arrived.at[k])
        )
        copies[-1].start()
    total = total_ref[...]
    for k in range(count):
        copies[k].wait()
        total += lax.dot_general(
            held[k], refs[count + k][0], (((1,), (1,)), ((), ())), preferred_element_type=F32
        )
    out_ref[...] = total


def add_grads(pieces, origins, wide_grads, total, n_dp):
    directions, units = total.shape[0], pieces[0].shape[1]
    n_mp, tokens, _ = wide_grads.shape
    share = n_dp // n_mp
    count = len(pieces)
    at = jnp.stack([f(origin, share) for origin in origins for f in (jnp.floor_divide, jnp.remainder)])

    def columns(k):
        return pl.BlockSpec((1, tokens, units), lambda i, at_ref: (at_ref[2 * k], 0, at_ref[2 * k + 1]))

    return pl.pallas_call(
        add_grads_kernel,
        grid_spec=pltpu.PrefetchScalarGridSpec(
            num_scalar_prefetch=1,
            grid=(1,),
            in_specs=[pl.BlockSpec(memory_space=pl.ANY)] * count
            + [columns(k) for k in range(count)]
            + [whole_block(total.shape)],
            out_specs=whole_block(total.shape),
            scratch_shapes=[
                pltpu.VMEM((count, directions, units), BF16),
                pltpu.SemaphoreType.DMA((count,)),
            ],
        ),
        out_shape=jax.ShapeDtypeStruct(total.shape, F32),
        compiler_params=pltpu.CompilerParams(vmem_limit_bytes=VMEM_BYTES),
        cost_estimate=pl.CostEstimate(flops=1, bytes_accessed=1, transcendentals=0),
        name="add_grads",
    )(at.astype(jnp.int32), *pieces, *[wide_grads] * count, total)


def join_kernel(at_ref, early_ref, late_ref, out_ref):
    count = early_ref.shape[0]
    for k in range(count):
        out_ref[at_ref[k]] = early_ref[k]
    out_ref[at_ref[count]] = late_ref[0]


def join(early, late, at):
    whole = pl.BlockSpec(memory_space=pltpu.VMEM)
    return pl.pallas_call(
        join_kernel,
        in_specs=[pl.BlockSpec(memory_space=pltpu.SMEM), whole, whole],
        out_specs=whole,
        out_shape=jax.ShapeDtypeStruct((early.shape[0] + 1,) + early.shape[1:], early.dtype),
        name="join_pairs",
    )(at, early, late)


def expand_kernel(tiles, rows, at_ref, near_ref, far_ref, turn_ref, *refs):
    out_ref, back, held = refs[-3:]
    count = back.shape[0] // rows
    step = pl.program_id(0)

    @pl.when(step == 0)
    def _():
        dims = (((0,), (0,)), ((), ()))
        depth = near_ref.shape[0]
        total = lax.dot_general(near_ref[...], turn_ref[:depth], dims, preferred_element_type=F32)
        total += lax.dot_general(far_ref[...], turn_ref[depth:], dims, preferred_element_type=F32)
        back[...] = total.astype(BF16)
        for k in range(count):
            start = pl.multiple_of(at_ref[1 + k] * rows, 16)
            held[k * rows : (k + 1) * rows] = back[pl.ds(start, rows)]

    def fill(pieces):
        lanes = pieces[0].shape[1]
        for c in range(pieces[0].shape[0] // rows):
            part = jnp.concatenate([piece[c * rows : (c + 1) * rows] for piece in pieces], axis=0)
            out_ref[c * lanes : (c + 1) * lanes] = lax.dot_general(
                part, held[...], (((0,), (0,)), ((), ())), preferred_element_type=F32
            ).astype(out_ref.dtype)

    pl.when(step < tiles)(lambda: fill(refs[:count]))
    pl.when(step >= tiles)(lambda: fill(refs[count:-3]))


def expand(owns, others, pairs, rows, units, core, near, far, turn):
    lanes = owns[0].shape[1]
    chunks = units // 2 // lanes
    columns = turn.shape[1]
    at = jnp.stack([core] + list(pairs)).astype(jnp.int32)
    if rows % 16:
        wide = jnp.concatenate([near, far])
        back = lax.dot_general(wide, turn, (((0,), (0,)), ((), ())), preferred_element_type=F32).astype(BF16)
        held = jnp.take(back.reshape((-1, rows, columns)), at[1:], axis=0).reshape((-1, columns))
        sides = []
        for pieces in (owns, others):
            plain = jnp.concatenate([unchunk(piece, rows, chunks) for piece in pieces])
            sides.append(lax.dot_general(plain, held, (((0,), (0,)), ((), ())), preferred_element_type=F32).astype(BF16))
        return jnp.where(core == 0, jnp.concatenate(sides), jnp.concatenate(sides[::-1]))
    group = max(g for g in range(1, chunks + 1) if chunks % g == 0 and g * lanes <= EXPAND_ROWS)
    tiles = chunks // group
    return pl.pallas_call(
        functools.partial(expand_kernel, tiles, rows),
        grid_spec=pltpu.PrefetchScalarGridSpec(
            num_scalar_prefetch=1,
            grid=(2 * tiles,),
            in_specs=[whole_block(near.shape), whole_block(far.shape), whole_block(turn.shape)]
            + [halves_spec((group * rows, lanes), tiles, False)] * len(owns)
            + [halves_spec((group * rows, lanes), tiles, True)] * len(owns),
            out_specs=pl.BlockSpec((group * lanes, columns), lambda i, at_ref: (tile_index(i, tiles, at_ref), 0)),
            scratch_shapes=[pltpu.VMEM((len(owns) * rows, columns), BF16)] * 2,
        ),
        out_shape=jax.ShapeDtypeStruct((units, columns), BF16),
        compiler_params=pltpu.CompilerParams(vmem_limit_bytes=VMEM_BYTES),
        cost_estimate=pl.CostEstimate(
            flops=2 * rows * len(owns) * units * columns, bytes_accessed=2 * units * columns, transcendentals=0
        ),
        name="expand_update",
    )(at, near, far, turn, *owns, *others)


def gather_near_first(x, axis_name):
    x = x[None]
    for bit in bits(axis_name):
        x = jnp.concatenate([x, flip(x, axis_name, bit)], axis=0)
    return x


def near_first(x, axis, me):
    size = x.shape[axis]
    for k in range(size.bit_length() - 1):
        shape = x.shape[:axis] + (size >> (k + 1), 2, 1 << k) + x.shape[axis + 1 :]
        parts = x.reshape(shape)
        swapped = jnp.flip(parts, axis + 1)
        x = jnp.where((me >> k) % 2 == 1, swapped, parts).reshape(x.shape)
    return x


def products(g, a):
    dims = (((1,), (1,)), ((), ()))
    g = g.astype(BF16)
    g_sq = (g.astype(F32) ** 2).astype(BF16)
    a_sq = (a.astype(F32) ** 2).astype(BF16)
    return (
        lax.dot_general(g, a, dims, preferred_element_type=F32),
        lax.dot_general(g_sq, a_sq, dims, preferred_element_type=F32),
    )


def picked(me_ref, g_ref, flipped):
    pairs = g_ref.shape[0] // 2
    core, pair = me_ref[0] % 2, me_ref[0] // 2
    return jnp.concatenate(
        [g_ref[(pair ^ r) * 2 + (core ^ flipped)] for r in range(pairs)], axis=0
    )


def theirs_kernel(rows, me_ref, at_ref, g_ref, *refs):
    out_ref, a_ref = refs[-2:]
    count = len(refs) // 2 - 1
    k = 0
    for own_ref, got_ref in zip(refs[:count], refs[count:-2]):
        total = (own_ref[...] + got_ref[...].astype(F32)).astype(BF16)
        for i in range(total.shape[0] // rows):
            start = pl.multiple_of(at_ref[k] * rows, 16)
            a_ref[pl.ds(start, rows)] = total[i * rows : (i + 1) * rows]
            k += 1
    rotated, squares = products(picked(me_ref, g_ref, 1), a_ref[...])
    out_ref[0] = rotated.astype(BF16)
    out_ref[1] = squares.astype(BF16)


def ours_kernel(me_ref, g_ref, a_ref, got_ref, *out_refs):
    width = g_ref.shape[1]
    rotated, squares = products(picked(me_ref, g_ref, 0), a_ref[...])
    rotated += got_ref[0].astype(F32)
    squares += got_ref[1].astype(F32)
    for r, out_ref in enumerate(out_refs):
        out_ref[0] = rotated[r * width : (r + 1) * width].astype(BF16)
        out_ref[1] = squares[r * width : (r + 1) * width].astype(BF16)


def token_sums(grad_proj_t, sums, gots, order, pair_rows):
    blocks, width, tokens = grad_proj_t.shape
    pairs = blocks // 2
    rows = pairs * pair_rows
    order = jnp.stack(order).astype(jnp.int32)
    me = lax.axis_index("dp")
    whole = pl.BlockSpec(memory_space=pltpu.VMEM)
    if width % 16 == 0 and pair_rows % 16 == 0 and gots:
        params = pltpu.CompilerParams(vmem_limit_bytes=VMEM_BYTES)
        cost = pl.CostEstimate(
            flops=2 * blocks * width * rows * tokens,
            bytes_accessed=4 * blocks * width * tokens + 2 * rows * tokens + 2 * blocks * width * rows,
            transcendentals=0,
        )
        index = me.astype(jnp.int32).reshape((1,))
        index_spec = pl.BlockSpec(memory_space=pltpu.SMEM)
        sent, act_proj_t = pl.pallas_call(
            functools.partial(theirs_kernel, pair_rows),
            in_specs=[index_spec, index_spec, whole] + [whole] * (len(sums) + len(gots)),
            out_specs=[whole, whole],
            out_shape=[
                jax.ShapeDtypeStruct((2, pairs * width, rows), BF16),
                jax.ShapeDtypeStruct((rows, tokens), BF16),
            ],
            compiler_params=params,
            cost_estimate=cost,
            name="sums_for_other_core",
        )(index, order, grad_proj_t, *sums, *gots)
        got = flip(sent, "dp", 1)
        ours = pl.pallas_call(
            ours_kernel,
            in_specs=[index_spec, whole, whole, whole],
            out_specs=[whole] * pairs,
            out_shape=[jax.ShapeDtypeStruct((2, width, rows), BF16)] * pairs,
            compiler_params=params,
            cost_estimate=cost,
            name="sums_for_own_core",
        )(index, grad_proj_t, act_proj_t, got)
    else:
        act_proj_t = jnp.concatenate(sums)
        for bit in bits("mp"):
            act_proj_t = act_proj_t + flip(act_proj_t.astype(BF16), "mp", bit).astype(F32)
        act_proj_t = act_proj_t.astype(BF16).reshape((-1, pair_rows, tokens))
        act_proj_t = join(act_proj_t[:-1], act_proj_t[-1:], order).reshape((-1, tokens))
        near = near_first(near_first(grad_proj_t.reshape((pairs, 2, width, tokens)), 0, me // 2), 1, me % 2)
        near = near.transpose(1, 0, 2, 3).reshape((2 * pairs * width, tokens))
        both = jnp.stack(products(near, act_proj_t)).reshape((2, 2, pairs, width, rows))
        total = both[:, 0] + flip(both[:, 1].astype(BF16), "dp", 1).astype(F32)
        ours = [total[:, r].astype(BF16) for r in range(pairs)]
    total = ours[0].astype(F32)
    for r in range(1, pairs):
        total += flip(ours[r], "dp", 2 * r).astype(F32)
    return total[0], total[1]


def gather_scaled(scaled, diag):
    pairs, n_mp = lax.axis_size("dp") // 2, lax.axis_size("mp")
    x = jnp.stack([scaled] + [flip(scaled, "dp", 2 * r) for r in range(2, pairs, 2)])
    parts = {}
    for m in range(n_mp):
        for low in range(2):
            hops = []
            for i in range(2 * pairs):
                hops += [(i * n_mp + k, (i ^ (2 * low)) * n_mp + (k ^ m)) for k in range(n_mp)]
            parts[m, low] = lax.ppermute(x, ("dp", "mp"), hops) if m or low else x
    x = jnp.stack([jnp.stack([parts[m, 0], parts[m, 1]], axis=1) for m in range(n_mp)])
    x, diag = lax.optimization_barrier((x, diag))
    return x, flip(x, "dp", 1), diag


def place_diag(diag_t):
    n_dp, n_mp = lax.axis_size("dp"), lax.axis_size("mp")
    width, rows = diag_t.shape[0], diag_t.shape[1] // n_mp
    here, block = lax.axis_index("mp"), lax.axis_index("mp") * n_dp + lax.axis_index("dp")
    out = jnp.zeros((n_mp, width, rows), diag_t.dtype)
    for k in range(n_mp):
        pairs = []
        for b in range(n_mp * n_dp):
            pairs.append(((b % n_dp) * n_mp + b // n_dp, (b // n_mp) * n_mp + (b + k) % n_mp))
        target = (block + k) % n_mp
        sent = lax.dynamic_slice(diag_t, (0, target * rows), (width, rows))
        got = lax.ppermute(sent, ("dp", "mp"), pairs)
        out = lax.dynamic_update_slice(out, got[None], ((here - k) % n_mp, 0, 0))
    return out.reshape((n_mp * width, rows)).T


def on_device(acts, grads, basis_in, basis_out, damping):
    tok_rows = acts.shape[0]
    n_dp, n_mp = lax.axis_size("dp"), lax.axis_size("mp")
    me = lax.axis_index("dp")
    tokens_all = tok_rows * n_dp
    out_units, directions = basis_out.shape
    width = directions // n_dp

    core, half = me % 2, n_dp // 2
    units = acts.shape[1]
    chunks = units // 2 // out_units
    own_rows = basis_in.shape[1]
    mine = basis_in.T.reshape((own_rows, 2, chunks, out_units)).transpose(1, 2, 0, 3)
    kept = lax.dynamic_index_in_dim(mine, core, 0, False)
    got = flip(lax.dynamic_index_in_dim(mine, 1 - core, 0, False), "dp", 1)
    both = jnp.stack([jnp.where(core == 0, kept, got), jnp.where(core == 0, got, kept)], axis=1)
    rows = 2 * own_rows
    in_rows = chunks * rows
    basis_out_t = basis_out.T
    own_piece = jnp.concatenate([both.reshape((in_rows, out_units)), basis_out_t])

    wide_grads = gather_doubling(grads, "mp")

    ahead, back_hops = ring_hops(n_dp)
    everyone = (ahead[0] + ahead[1], back_hops[0] + back_hops[1])
    last_hops = ahead[0] + back_hops[1]
    began = ring_place("dp")
    grad_proj_t = jnp.zeros((directions, tok_rows), F32)
    owns, others, pairs, sums, gots = [], [], [], [], []
    rows_near = basis_out_t

    def take_grads(pieces, where_from):
        nonlocal grad_proj_t
        origins = [2 * p + core for p in where_from] + [2 * p + 1 - core for p in where_from]
        grad_proj_t = add_grads(pieces, origins, wide_grads, grad_proj_t, n_dp)

    def use(pieces, where_from, grads_too=True, costed=False):
        swapped = [flip(piece, "dp", 1) for piece in pieces]
        sums.append(project(pieces, swapped, rows, core, acts, costed))
        gots.append([flip(sums[-1].astype(BF16), "mp", 1)] if n_mp == 2 else [])
        owns.extend(pieces)
        others.extend(swapped)
        pairs.extend(where_from)
        if grads_too:
            take_grads(pieces + swapped, where_from)

    moving = [own_piece, own_piece]
    waiting = [own_piece], [me // 2]
    for step in range(1, half // 2):
        moving = [lax.ppermute(x, "dp", everyone[k]) for k, x in enumerate(moving)]
        if step == 1:
            moving, own_piece = lax.optimization_barrier((moving, own_piece))
            waiting = [own_piece], [me // 2]
        else:
            use(*waiting)
            moving, sums[-1], gots[:-1], grad_proj_t, rows_near = lax.optimization_barrier(
                (moving, sums[-1], gots[:-1], grad_proj_t, rows_near)
            )
            waiting = [], []
        if step == min(2, half // 2 - 1):
            rows_near = gather_near_first(rows_near, "mp")
        waiting = waiting[0] + moving, waiting[1] + [began(step), began(-step)]

    last = lax.ppermute(
        jnp.where(core == 0, moving[0][:in_rows], moving[1][:in_rows]), "dp", last_hops
    )
    held = jnp.where(core == 0, moving[0][in_rows:], moving[1][in_rows:])
    use(*waiting)
    held, last, sums[-1], grad_proj_t = lax.optimization_barrier((held, last, sums[-1], grad_proj_t))
    last_out = lax.ppermute(held, "dp", last_hops)
    last_pair = began(half // 2)
    use([last], [last_pair], False, True)
    last_out, sums[-1] = lax.optimization_barrier((last_out, sums[-1]))
    grad_proj_t = add_grads(
        [last_out, flip(last_out, "dp", 1)],
        [2 * last_pair + core, 2 * last_pair + 1 - core],
        wide_grads,
        grad_proj_t,
        n_dp,
    )

    rows_near = rows_near.reshape((n_mp, half, 2, width, out_units))
    rows_near = near_first(near_first(rows_near, 1, me // 2), 2, core)
    rows_near = rows_near.transpose(2, 0, 1, 3, 4).reshape((n_mp * directions, out_units))

    rotated, squares = token_sums(
        grad_proj_t.reshape((n_dp, width, tok_rows)), sums, [got for part in gots for got in part], pairs, rows
    )
    diag_t = squares / tokens_all
    scaled = (rotated / (diag_t + damping[0])).astype(BF16)
    near, far, diag = gather_scaled(scaled, place_diag(diag_t))
    near, far = (x.reshape((directions * n_mp // 2, -1)) for x in (near, far))
    return (expand(owns, others, pairs, rows, units, core, near, far, rows_near), diag)


def solution(mesh):
    placed = (P("dp", "mp"), P("dp", "mp"), P("mp", "dp"), P("dp", "mp"), P())
    return jax.shard_map(
        on_device,
        mesh=mesh,
        in_specs=placed,
        out_specs=(P("mp", "dp"), P("mp", "dp")),
        check_vma=False,
    )
```

time: 479 us -> 235 us (0.49)
  waiting for transfers between devices: 356 us -> 102 us
  Pallas kernels: 0 us -> 61 us
  matrix products: 46.8 us -> 0 us
  starting transfers between devices: 0.28 us -> 45 us
  blocking collectives: 32.5 us -> 0 us
  local copies, waits for them, and re-layouts: 23.9 us -> 8.24 us
  between operations: 15.5 us -> 2.06 us
  other arithmetic: 2.91 us -> 15.2 us
    all_gather x5 -> x0, waiting for transfers between devices: 233 us -> none  [the longest x1 88.4 us: on_device(): full_in = lax.all_gather(basis_in, 'dp', axis=1, tiled=True)]
    unnamed x8 -> x0, waiting for transfers between devices: 104 us -> none
    ppermute x0 -> x41, waiting for transfers between devices: none -> 102 us  [the longest x6 66 us: on_device(): moving = [lax.ppermute(x, 'dp', everyone[k]) for k, x in enumerate(moving)]]
    pallas_call x0 -> x11, Pallas kernels: none -> 61 us  [the longest x4 24.4 us: project(): pl.pallas_call(functools.partial(project_kernel, tiles, rows), grid_spec=...]
    dot_general x6 -> x0, matrix products: 46.8 us -> none  [the longest x1 20.7 us: on_device(): update = jnp.dot(full_in, back, preferred_element_type=jnp.float32)]
    ppermute x0 -> x41, starting transfers between devices: none -> 45 us  [the longest x28 28.4 us: flip(): return lax.ppermute(x, axis_name, [(i, i ^ bit) for i in range(size)])]
    all_gather x2 -> x0, blocking collectives: 32.5 us -> none  [the longest x1 21.7 us: on_device(): scaled_wide = lax.all_gather(scaled, 'dp', axis=1, tiled=True)]
    reduce_scatter x1 -> x0, waiting for transfers between devices: 18.7 us -> none  [on_device(): lax.psum_scatter(lax.dot_general(full_in, acts, (((0,), (1,)), ((), ())),...]
  transfers between devices with their start and end apart: 7 -> 41, of which waited for: 6 -> 20; matrix products, arithmetic and copies ran while one was open for 5% -> 7% of each run, Pallas kernels for 0% -> 17%
where the time goes in v2:
time: 235 us; the launch traced here: 234 us
  waiting for transfers between devices  102 us (43%)
  Pallas kernels  61 us (26%)
  starting transfers between devices  45 us (19%)
  other arithmetic  15.2 us (6%)
  local copies, waits for them, and re-layouts  8.24 us (4%)
    ppermute x6, waiting for transfers between devices, on_device(): moving = [lax.ppermute(x, 'dp', everyone[k]) for k, x in enumerate(moving)]  66 us
    ppermute x28, starting transfers between devices, flip(): return lax.ppermute(x, axis_name, [(i, i ^ bit) for i in range(size)])  28.4 us
    ppermute x28, waiting for transfers between devices, flip(): return lax.ppermute(x, axis_name, [(i, i ^ bit) for i in range(size)])  27.2 us
    pallas_call x4, Pallas kernels, project(): pl.pallas_call(functools.partial(project_kernel, tiles, rows), grid_spec=...  24.4 us
    pallas_call x1, Pallas kernels, expand(): pl.pallas_call(functools.partial(expand_kernel, tiles, rows), grid_spec=p...  19.5 us
    pallas_call x4, Pallas kernels, add_grads(): pl.pallas_call(add_grads_kernel, grid_spec=pltpu.PrefetchScalarGridSpec(n...  15.6 us
    ppermute x3, waiting for transfers between devices, gather_scaled(): parts[m, low] = lax.ppermute(x, ('dp', 'mp'), hops) if m or low else x  7.22 us
    ppermute x6, starting transfers between devices, on_device(): moving = [lax.ppermute(x, 'dp', everyone[k]) for k, x in enumerate(moving)]  6.4 us
  transfers between devices with their start and end apart: 41, of which 20 were waited for; matrix products, arithmetic and copies ran while one was open for 7% of the time, Pallas kernels for 17%

profile of v2, /device:TPU:0, one launch (start us, length us, event | category | flops | bytes accessed | tf_op | source)
XLA Modules:
  0.0 233.9 jit_solution(11085626197853442890)
XLA Ops:
  0.6 2.1 reshape.47
  3.7 2.6 %collective-permute-start.8 = (bf16[1,256,4096]{2,1,0:T(8,128)(2,1)}, bf16[1,256,4096]{2,1,0:T(8,128)(2,1)}, u32[]{:S(2)}, u32[]{:S(2)}) collective-permute-start(bf16[1,256,4096]{2,1,0:T(8,128)(2,1)} %bitcast.36), channel_id=1, source_target_pairs={{0,1},{1,0},{2,3},{3,2},{4,5},{5,4},{6,7},{7,6},{8,9},{9,8},{10,11... | collective-permute-start | bytes 6291464 | tf_op jit(solution)/shard_map/ppermute | solution.py:17
  8.3 1.2 pad_maximum_fusion.refs_0_
  9.5 1.6 collective-permute-start.2
  11.5 36.5 %collective-permute-done.2.refs_2_ = bf16[1632,512]{1,0:T(8,128)(2,1)S(1)} collective-permute-done((bf16[1632,512]{1,0:T(8,128)(2,1)S(1)}, bf16[1632,512]{1,0:T(8,128)(2,1)S(1)}, u32[]{:S(2)}, u32[]{:S(2)}) %collective-permute-start.2) | collective-permute-done | bytes 1671200 | tf_op jit(solution)/shard_map/ppermute | solution.py:471
  48.1 1.3 collective-permute-done.1.refs_1_
  50.4 2.3 collective-permute-done.8
  52.8 1.8 collective-permute-start.4
  54.7 2.5 %select_bitcast_fusion.1 = (bf16[1,1,256,4096]{3,2,1,0:T(8,128)(2,1)S(1)}, bf16[1,1,256,4096]{3,2,1,0:T(8,128)(2,1)S(1)}) fusion(bf16[1,256,4096]{2,1,0:T(8,128)(2,1)} %collective-permute-done.8, pred[]{:T(512)S(6)} %eq.62, bf16[256,4096]{1,0:T(8,128)(2,1)} %param.6), kind=kLoop, calls=%fused_computation.2 | loop fusion | flops 2097152 | bytes 8388609 | tf_op jit(solution)/shard_map/stack | solution.py:34
  57.2 2.4 %maximum_bitcast_fusion.refs_6_.refs_7_.refs_8_.refs_9_.refs_10_.refs_11_.refs_4_.refs_5_.refs_2_.refs_3_ = bf16[2,256,4096]{2,1,0:T(8,128)(2,1)} fusion(bf16[1,1,256,4096]{3,2,1,0:T(8,128)(2,1)S(1)} %get-tuple-element.67, bf16[1,1,256,4096]{3,2,1,0:T(8,128)(2,1)S(1)} %get-tuple-element.66), kind=kLoop, calls=%fused_computation | loop fusion | flops 2097152 | bytes 8388608 | tf_op jit(solution)/shard_map/reshape | solution.py:34
  59.5 6.5 %project_acts.4.refs_0_ = f32[240,256]{1,0:T(8,128)S(1)} custom-call(s32[1]{0:T(128)} %bitcast.at_ref, bf16[256,14336]{1,0:T(8,128)(2,1)} %acts_ref.7, bf16[1632,512]{1,0:T(8,128)(2,1)S(1)} %pad_maximum_fusion.refs_0_, bf16[1632,512]{1,0:T(8,128)(2,1)} %collective-permute-done.1.refs_1_, bf16[1632,512]{1,0:T(8,128)(2,1)S(1)} %collective-permute-done.2.refs_2_, ...), custom_call_target="tpu_custom_call" | custom-call | flops 1 | bytes 1 | tf_op jit(solution)/shard_map/project_acts/pallas_call | solution.py:117
  66.8 5.0 %add_grads.4.refs_8_ = f32[512,256]{1,0:T(8,128)S(1)} custom-call(s32[12]{0:T(128)S(1)} %stack.237.at_ref, bf16[1632,512]{1,0:T(8,128)(2,1)S(1)} %pad_maximum_fusion.refs_0_, bf16[1632,512]{1,0:T(8,128)(2,1)} %collective-permute-done.1.refs_1_, bf16[1632,512]{1,0:T(8,128)(2,1)S(1)} %collective-permute-done.2.refs_2_, ...), custom_call_target="tpu_custom_call" | custom-call | flops 1 | bytes 1 | tf_op jit(solution)/shard_map/add_grads/pallas_call | solution.py:172
  72.5 16.6 %collective-permute-done.3.refs_0_.refs_3_ = bf16[1632,512]{1,0:T(8,128)(2,1)} collective-permute-done((bf16[1632,512]{1,0:T(8,128)(2,1)}, bf16[1632,512]{1,0:T(8,128)(2,1)}, u32[]{:S(2)}, u32[]{:S(2)}) %collective-permute-start.3) | collective-permute-done | bytes 1671200 | tf_op jit(solution)/shard_map/ppermute | solution.py:471
  89.2 2.0 collective-permute-done.4.refs_1_.refs_4_
  91.7 1.7 collective-permute-start.9
  93.7 1.6 collective-permute-start.14
  96.3 11.0 %collective-permute-done.14 = bf16[1,512,512]{2,1,0:T(8,128)(2,1)} collective-permute-done((bf16[1,512,512]{2,1,0:T(8,128)(2,1)}, bf16[1,512,512]{2,1,0:T(8,128)(2,1)}, u32[]{:S(2)}, u32[]{:S(2)}) %collective-permute-start.14) | collective-permute-done | bytes 524320 | tf_op jit(solution)/shard_map/ppermute | solution.py:17
  107.3 1.6 collective-permute-start.13
  108.8 2.3 pad_maximum_fusion.2
  111.1 6.6 %project_acts.5.refs_1_ = f32[160,256]{1,0:T(8,128)S(1)} custom-call(s32[1]{0:T(128)} %bitcast.at_ref, bf16[256,14336]{1,0:T(8,128)(2,1)} %acts_ref.7, bf16[1632,512]{1,0:T(8,128)(2,1)} %collective-permute-done.3.refs_0_.refs_3_, bf16[1632,512]{1,0:T(8,128)(2,1)} %collective-permute-done.4.refs_1_.refs_4_, ...), custom_call_target="tpu_custom_call" | custom-call | flops 1 | bytes 1 | tf_op jit(solution)/shard_map/project_acts/pallas_call | solution.py:117
  117.7 4.4 %add_grads.5.refs_8_ = f32[512,256]{1,0:T(8,128)S(1)} custom-call(s32[8]{0:T(128)S(1)} %stack.249.at_ref, bf16[1632,512]{1,0:T(8,128)(2,1)} %collective-permute-done.3.refs_0_.refs_3_, bf16[1632,512]{1,0:T(8,128)(2,1)} %collective-permute-done.4.refs_1_.refs_4_, bf16[1632,512]{1,0:T(8,128)(2,1)} %collective-permute-done.11.refs_2_.refs_11_, ...), custom_call_target="tpu_custom_call" | custom-call | flops 1 | bytes 1 | tf_op jit(solution)/shard_map/add_grads/pallas_call | solution.py:172
  122.1 8.1 %collective-permute-done.9.refs_0_.refs_5_ = bf16[1632,512]{1,0:T(8,128)(2,1)S(1)} collective-permute-done((bf16[1632,512]{1,0:T(8,128)(2,1)}, bf16[1632,512]{1,0:T(8,128)(2,1)S(1)}, u32[]{:S(2)}, u32[]{:S(2)}) %collective-permute-start.9) | collective-permute-done | bytes 1671200 | tf_op jit(solution)/shard_map/ppermute | solution.py:471
  130.3 1.4 collective-permute-done.10.refs_1_.refs_6_
  133.3 1.6 collective-permute-start.15
  135.3 2.4 %collective-permute-done.17.refs_3_.refs_14_ = bf16[1632,512]{1,0:T(8,128)(2,1)} collective-permute-done((bf16[1632,512]{1,0:T(8,128)(2,1)S(1)}, bf16[1632,512]{1,0:T(8,128)(2,1)}, u32[]{:S(2)}, u32[]{:S(2)}) %collective-permute-start.17) | collective-permute-done | bytes 1671200 | tf_op jit(solution)/shard_map/ppermute | solution.py:17
  137.7 6.0 %project_acts.6.refs_2_ = f32[160,256]{1,0:T(8,128)S(1)} custom-call(s32[1]{0:T(128)} %bitcast.at_ref, bf16[256,14336]{1,0:T(8,128)(2,1)} %acts_ref.7, bf16[1632,512]{1,0:T(8,128)(2,1)S(1)} %collective-permute-done.9.refs_0_.refs_5_, bf16[1632,512]{1,0:T(8,128)(2,1)S(1)} %collective-permute-done.10.refs_1_.refs_6_, ...), custom_call_target="tpu_custom_call" | custom-call | flops 1 | bytes 1 | tf_op jit(solution)/shard_map/project_acts/pallas_call | solution.py:117
  144.5 3.7 %add_grads.6.refs_4_ = f32[512,256]{1,0:T(8,128)S(1)} custom-call(s32[8]{0:T(128)S(1)} %stack.258.at_ref, bf16[1632,512]{1,0:T(8,128)(2,1)S(1)} %collective-permute-done.9.refs_0_.refs_5_, bf16[1632,512]{1,0:T(8,128)(2,1)S(1)} %collective-permute-done.10.refs_1_.refs_6_, bf16[1632,512]{1,0:T(8,128)(2,1)} %collective-permute-done.16.refs_2_.refs_13_, ...), custom_call_target="tpu_custom_call" | custom-call | flops 1 | bytes 1 | tf_op jit(solution)/shard_map/add_grads/pallas_call | solution.py:172
  148.2 1.3 collective-permute-done.15.refs_0_.refs_7_
  149.5 1.6 collective-permute-start.18
  151.0 1.4 collective-permute-done.19.refs_1_.refs_15_
  152.5 5.4 %project_acts.7.refs_3_ = f32[80,256]{1,0:T(8,128)S(1)} custom-call(s32[1]{0:T(128)} %bitcast.at_ref, bf16[256,14336]{1,0:T(8,128)(2,1)} %acts_ref.7, bf16[1120,512]{1,0:T(8,128)(2,1)} %collective-permute-done.15.refs_0_.refs_7_, bf16[1120,512]{1,0:T(8,128)(2,1)S(1)} %collective-permute-done.19.refs_1_.refs_15_), custom_call_target="tpu_custom_call" | custom-call | flops 587202560 | bytes 9633792 | tf_op jit(solution)/shard_map/project_acts/pallas_call | solution.py:117
  159.3 1.5 collective-permute-start.21
  162.0 1.5 collective-permute-start.23
  164.7 2.6 %add_grads.7 = f32[512,256]{1,0:T(8,128)S(1)} custom-call(s32[4]{0:T(128)S(1)} %pad_add_fusion.at_ref, bf16[512,512]{1,0:T(8,128)(2,1)S(1)} %collective-permute-done.18.refs_0_, bf16[512,512]{1,0:T(8,128)(2,1)S(1)} %collective-permute-done.20.refs_1_, ...), custom_call_target="tpu_custom_call" | custom-call | flops 1 | bytes 1 | tf_op jit(solution)/shard_map/add_grads/pallas_call | solution.py:172
  168.5 2.1 collective-permute-done.24.got_ref
  171.7 1.6 collective-permute-start.26
  174.0 1.4 collective-permute-start.27
  175.4 2.6 %collective-permute-start.28 = (bf16[2,32,640]{2,1,0:T(8,128)(2,1)S(1)}, bf16[2,32,640]{2,1,0:T(8,128)(2,1)S(1)}, u32[]{:S(2)}, u32[]{:S(2)}) collective-permute-start(bf16[2,32,640]{2,1,0:T(8,128)(2,1)S(1)} %get-tuple-element.59), channel_id=1, source_target_pairs={{0,16},{2,18},{4,20},{6,22},{8,24},{10,26},{12,28},{14,30},{16,0},... | collective-permute-start | bytes 245768 | tf_op jit(solution)/shard_map/ppermute | solution.py:17
  178.4 3.6 %collective-permute-start.30 = (bf16[2,32,640]{2,1,0:T(8,128)(2,1)S(1)}, bf16[2,32,640]{2,1,0:T(8,128)(2,1)S(1)}, u32[]{:S(2)}, u32[]{:S(2)}) collective-permute-start(bf16[2,32,640]{2,1,0:T(8,128)(2,1)S(1)} %get-tuple-element.61), channel_id=1, source_target_pairs={{0,24},{2,26},{4,28},{6,30},{8,16},{10,18},{12,20},{14,22},{16,8},... | collective-permute-start | bytes 245768 | tf_op jit(solution)/shard_map/ppermute | solution.py:17
  183.0 1.9 reverse_select_fusion.3
  185.0 2.6 %collective-permute-done.28 = bf16[2,32,640]{2,1,0:T(8,128)(2,1)S(1)} collective-permute-done((bf16[2,32,640]{2,1,0:T(8,128)(2,1)S(1)}, bf16[2,32,640]{2,1,0:T(8,128)(2,1)S(1)}, u32[]{:S(2)}, u32[]{:S(2)}) %collective-permute-start.28) | collective-permute-done | bytes 81952 | tf_op jit(solution)/shard_map/ppermute | solution.py:17
  187.5 2.3 collective-permute-done.29
  190.0 2.9 %collective-permute-start.34 = (bf16[32,640]{1,0:T(8,128)(2,1)S(1)}, bf16[32,640]{1,0:T(8,128)(2,1)S(1)}, u32[]{:S(2)}, u32[]{:S(2)}) collective-permute-start(bf16[32,640]{1,0:T(8,128)(2,1)S(1)} %bitcast.124), channel_id=1, source_target_pairs={{0,24},{2,26},{4,28},{6,30},{8,16},{10,18},{12,20},{14,22},{16,8},... | collective-permute-start | bytes 122888 | tf_op jit(solution)/shard_map/ppermute | solution.py:17
  192.9 2.4 %collective-permute-start.33 = (bf16[32,640]{1,0:T(8,128)(2,1)S(1)}, bf16[32,640]{1,0:T(8,128)(2,1)S(1)}, u32[]{:S(2)}, u32[]{:S(2)}) collective-permute-start(bf16[32,640]{1,0:T(8,128)(2,1)S(1)} %bitcast.125), channel_id=1, source_target_pairs={{0,16},{2,18},{4,20},{6,22},{8,24},{10,26},{12,28},{14,30},{16,0},... | collective-permute-start | bytes 122888 | tf_op jit(solution)/shard_map/ppermute | solution.py:17
  197.9 1.4 collective-permute-done.32
  199.3 3.6 %collective-permute-start.36 = (bf16[4,32,640]{2,1,0:T(8,128)(2,1)S(1)}, bf16[4,32,640]{2,1,0:T(8,128)(2,1)S(1)}, u32[]{:S(2)}, u32[]{:S(2)}) collective-permute-start(bf16[4,32,640]{2,1,0:T(8,128)(2,1)S(1)} %get-tuple-element.73), channel_id=1, source_target_pairs={{0,1},{1,0},{2,3},{3,2},{4,5},{5,4},{6,7},{7,6},{8,9},{9,8},{10,11... | collective-permute-start | bytes 491528 | tf_op jit(solution)/shard_map/ppermute | solution.py:400
  204.6 7.2 %collective-permute-done.35 = bf16[4,32,640]{2,1,0:T(8,128)(2,1)S(1)} collective-permute-done((bf16[4,32,640]{2,1,0:T(8,128)(2,1)S(1)}, bf16[4,32,640]{2,1,0:T(8,128)(2,1)S(1)}, u32[]{:S(2)}, u32[]{:S(2)}) %collective-permute-start.35) | collective-permute-done | bytes 163872 | tf_op jit(solution)/shard_map/ppermute | solution.py:400
  214.2 19.5 %expand_update.1 = bf16[14336,512]{1,0:T(8,128)(2,1)} custom-call(s32[9]{0:T(128)S(1)} %stack.216.at_ref, bf16[512,640]{1,0:T(8,128)(2,1)S(1)} %bitcast.113, bf16[512,640]{1,0:T(8,128)(2,1)S(1)} %bitcast.114, bf16[1024,512]{1,0:T(8,128)(2,1)S(1)} %bitcast.112, bf16[1632,512]{1,0:T(8,128)(2,1)} %copy-done, bf16[1632,512]{1,0:T(8,128)(2,1)} %collective-permute-done.1.refs_1_, ...), custom_call_target="tpu_custom_call" | custom-call | flops 9395240960 | bytes 14680064 | tf_op jit(solution)/shard_map/expand_update/pallas_call | solution.py:255
  (122 shorter events, 25.1 us)
Async XLA Ops:
  3.2 4.1 %collective-permute-start = (bf16[14,40,512]{2,1,0:T(8,128)(2,1)S(1)}, bf16[14,40,512]{2,1,0:T(8,128)(2,1)S(1)}, u32[]{:S(2)}, u32[]{:S(2)}) collective-permute-start(bf16[14,40,512]{2,1,0:T(8,128)(2,1)S(1)} %copy.22), channel_id=1, source_target_pairs={{0,2},{2,0},{4,6},{6,4},{8,10},{10,8},{12,14},{14,12},{16,18},{18,... | collective-permute-start | bytes 1720328 | tf_op jit(solution)/shard_map/ppermute | solution.py:17
  3.7 49.1 %collective-permute-start.8 = (bf16[1,256,4096]{2,1,0:T(8,128)(2,1)}, bf16[1,256,4096]{2,1,0:T(8,128)(2,1)}, u32[]{:S(2)}, u32[]{:S(2)}) collective-permute-start(bf16[1,256,4096]{2,1,0:T(8,128)(2,1)} %bitcast.36), channel_id=1, source_target_pairs={{0,1},{1,0},{2,3},{3,2},{4,5},{5,4},{6,7},{7,6},{8,9},{9,8},{10,11... | collective-permute-start | bytes 6291464 | tf_op jit(solution)/shard_map/ppermute | solution.py:17
  9.4 57.3 %copy-start = (bf16[1632,512]{1,0:T(8,128)(2,1)}, bf16[1632,512]{1,0:T(8,128)(2,1)S(1)}, u32[]{:S(2)}) copy-start(bf16[1632,512]{1,0:T(8,128)(2,1)S(1)} %pad_maximum_fusion.refs_0_) | copy-start | bytes 5013508
  9.5 38.6 %collective-permute-start.2 = (bf16[1632,512]{1,0:T(8,128)(2,1)S(1)}, bf16[1632,512]{1,0:T(8,128)(2,1)S(1)}, u32[]{:S(2)}, u32[]{:S(2)}) collective-permute-start(bf16[1632,512]{1,0:T(8,128)(2,1)S(1)} %pad_maximum_fusion.refs_0_), channel_id=1, source_target_pairs={{8,0},{16,8},{24,16},{28,24},{20,28},{12,20},{4,12},{0,4},{10,2},{... | collective-permute-start | bytes 5013512 | tf_op jit(solution)/shard_map/ppermute | solution.py:471
  11.0 38.4 %collective-permute-start.1 = (bf16[1632,512]{1,0:T(8,128)(2,1)S(1)}, bf16[1632,512]{1,0:T(8,128)(2,1)}, u32[]{:S(2)}, u32[]{:S(2)}) collective-permute-start(bf16[1632,512]{1,0:T(8,128)(2,1)S(1)} %pad_maximum_fusion.refs_0_), channel_id=1, source_target_pairs={{0,8},{8,16},{16,24},{24,28},{28,20},{20,12},{12,4},{4,0},{2,10},{... | collective-permute-start | bytes 5013512 | tf_op jit(solution)/shard_map/ppermute | solution.py:471
  48.1 18.7 %copy-start.3 = (bf16[1632,512]{1,0:T(8,128)(2,1)}, bf16[1632,512]{1,0:T(8,128)(2,1)S(1)}, u32[]{:S(2)}) copy-start(bf16[1632,512]{1,0:T(8,128)(2,1)S(1)} %collective-permute-done.2.refs_2_) | copy-start | bytes 5013508
  49.4 10.1 %collective-permute-start.5 = (bf16[1632,512]{1,0:T(8,128)(2,1)S(1)}, bf16[1632,512]{1,0:T(8,128)(2,1)}, u32[]{:S(2)}, u32[]{:S(2)}) collective-permute-start(bf16[1632,512]{1,0:T(8,128)(2,1)S(1)} %pad_maximum_fusion.refs_0_), channel_id=1, source_target_pairs={{0,2},{2,0},{4,6},{6,4},{8,10},{10,8},{12,14},{14,12},{16,18},{18,... | collective-permute-start | bytes 5013512 | tf_op jit(solution)/shard_map/ppermute | solution.py:17
  49.4 10.1 %collective-permute-start.6 = (bf16[1632,512]{1,0:T(8,128)(2,1)}, bf16[1632,512]{1,0:T(8,128)(2,1)}, u32[]{:S(2)}, u32[]{:S(2)}) collective-permute-start(bf16[1632,512]{1,0:T(8,128)(2,1)} %collective-permute-done.1.refs_1_), channel_id=1, source_target_pairs={{0,2},{2,0},{4,6},{6,4},{8,10},{10,8},{12,14},{14,12},{16,18},{18,... | collective-permute-start | bytes 5013512 | tf_op jit(solution)/shard_map/ppermute | solution.py:17
  49.9 9.6 %collective-permute-start.7 = (bf16[1632,512]{1,0:T(8,128)(2,1)S(1)}, bf16[1632,512]{1,0:T(8,128)(2,1)}, u32[]{:S(2)}, u32[]{:S(2)}) collective-permute-start(bf16[1632,512]{1,0:T(8,128)(2,1)S(1)} %collective-permute-done.2.refs_2_), channel_id=1, source_target_pairs={{0,2},{2,0},{4,6},{6,4},{8,10},{10,8},{12,14},{14,12},{16,18},{18,... | collective-permute-start | bytes 5013512 | tf_op jit(solution)/shard_map/ppermute | solution.py:17
  49.9 39.2 %collective-permute-start.3 = (bf16[1632,512]{1,0:T(8,128)(2,1)}, bf16[1632,512]{1,0:T(8,128)(2,1)}, u32[]{:S(2)}, u32[]{:S(2)}) collective-permute-start(bf16[1632,512]{1,0:T(8,128)(2,1)} %collective-permute-done.1.refs_1_), channel_id=1, source_target_pairs={{0,8},{8,16},{16,24},{24,28},{28,20},{20,12},{12,4},{4,0},{2,10},{... | collective-permute-start | bytes 5013512 | tf_op jit(solution)/shard_map/ppermute | solution.py:471
  52.8 38.4 %collective-permute-start.4 = (bf16[1632,512]{1,0:T(8,128)(2,1)S(1)}, bf16[1632,512]{1,0:T(8,128)(2,1)}, u32[]{:S(2)}, u32[]{:S(2)}) collective-permute-start(bf16[1632,512]{1,0:T(8,128)(2,1)S(1)} %collective-permute-done.2.refs_2_), channel_id=1, source_target_pairs={{8,0},{16,8},{24,16},{28,24},{20,28},{12,20},{4,12},{0,4},{10,2},{... | collective-permute-start | bytes 5013512 | tf_op jit(solution)/shard_map/ppermute | solution.py:471
  91.1 20.0 %collective-permute-start.11 = (bf16[1632,512]{1,0:T(8,128)(2,1)}, bf16[1632,512]{1,0:T(8,128)(2,1)}, u32[]{:S(2)}, u32[]{:S(2)}) collective-permute-start(bf16[1632,512]{1,0:T(8,128)(2,1)} %collective-permute-done.3.refs_0_.refs_3_), channel_id=1, source_target_pairs={{0,2},{2,0},{4,6},{6,4},{8,10},{10,8},{12,14},{14,12},{16,18},{18,... | collective-permute-start | bytes 5013512 | tf_op jit(solution)/shard_map/ppermute | solution.py:17
  91.1 20.0 %collective-permute-start.12 = (bf16[1632,512]{1,0:T(8,128)(2,1)}, bf16[1632,512]{1,0:T(8,128)(2,1)}, u32[]{:S(2)}, u32[]{:S(2)}) collective-permute-start(bf16[1632,512]{1,0:T(8,128)(2,1)} %collective-permute-done.4.refs_1_.refs_4_), channel_id=1, source_target_pairs={{0,2},{2,0},{4,6},{6,4},{8,10},{10,8},{12,14},{14,12},{16,18},{18,... | collective-permute-start | bytes 5013512 | tf_op jit(solution)/shard_map/ppermute | solution.py:17
  91.7 38.6 %collective-permute-start.9 = (bf16[1632,512]{1,0:T(8,128)(2,1)}, bf16[1632,512]{1,0:T(8,128)(2,1)S(1)}, u32[]{:S(2)}, u32[]{:S(2)}) collective-permute-start(bf16[1632,512]{1,0:T(8,128)(2,1)} %collective-permute-done.3.refs_0_.refs_3_), channel_id=1, source_target_pairs={{0,8},{8,16},{16,24},{24,28},{28,20},{20,12},{12,4},{4,0},{2,10},{... | collective-permute-start | bytes 5013512 | tf_op jit(solution)/shard_map/ppermute | solution.py:471
  93.3 38.3 %collective-permute-start.10 = (bf16[1632,512]{1,0:T(8,128)(2,1)}, bf16[1632,512]{1,0:T(8,128)(2,1)S(1)}, u32[]{:S(2)}, u32[]{:S(2)}) collective-permute-start(bf16[1632,512]{1,0:T(8,128)(2,1)} %collective-permute-done.4.refs_1_.refs_4_), channel_id=1, source_target_pairs={{8,0},{16,8},{24,16},{28,24},{20,28},{12,20},{4,12},{0,4},{10,2},{... | collective-permute-start | bytes 5013512 | tf_op jit(solution)/shard_map/ppermute | solution.py:471
  93.7 13.6 %collective-permute-start.14 = (bf16[1,512,512]{2,1,0:T(8,128)(2,1)}, bf16[1,512,512]{2,1,0:T(8,128)(2,1)}, u32[]{:S(2)}, u32[]{:S(2)}) collective-permute-start(bf16[1,512,512]{2,1,0:T(8,128)(2,1)} %bitcast.48), channel_id=1, source_target_pairs={{0,1},{1,0},{2,3},{3,2},{4,5},{5,4},{6,7},{7,6},{8,9},{9,8},{10,11... | collective-permute-start | bytes 1572872 | tf_op jit(solution)/shard_map/ppermute | solution.py:17
  107.3 14.9 %collective-permute-start.13 = (bf16[240,256]{1,0:T(8,128)(2,1)S(1)}, bf16[240,256]{1,0:T(8,128)(2,1)S(1)}, u32[]{:S(2)}, u32[]{:S(2)}) collective-permute-start(bf16[240,256]{1,0:T(8,128)(2,1)S(1)} %convert_element_type.43), channel_id=1, source_target_pairs={{0,1},{1,0},{2,3},{3,2},{4,5},{5,4},{6,7},{7,6},{8,9},{9,8},{10,11... | collective-permute-start | bytes 368648 | tf_op jit(solution)/shard_map/ppermute | solution.py:17
  122.1 11.2 %copy-start.8 = (f32[512,256]{1,0:T(8,128)}, f32[512,256]{1,0:T(8,128)S(1)}, u32[]{:S(2)}) copy-start(f32[512,256]{1,0:T(8,128)S(1)} %add_grads.5.refs_8_) | copy-start | bytes 1572868
  122.1 11.2 %copy-start.14 = (bf16[240,256]{1,0:T(8,128)(2,1)}, bf16[240,256]{1,0:T(8,128)(2,1)S(1)}, u32[]{:S(2)}) copy-start(bf16[240,256]{1,0:T(8,128)(2,1)S(1)} %collective-permute-done.13.refs_4_) | copy-start | bytes 368644
  130.3 13.5 %copy-start.1 = (bf16[1632,512]{1,0:T(8,128)(2,1)}, bf16[1632,512]{1,0:T(8,128)(2,1)S(1)}, u32[]{:S(2)}) copy-start(bf16[1632,512]{1,0:T(8,128)(2,1)S(1)} %collective-permute-done.9.refs_0_.refs_5_) | copy-start | bytes 5013508
  131.6 12.1 %copy-start.2 = (bf16[1632,512]{1,0:T(8,128)(2,1)}, bf16[1632,512]{1,0:T(8,128)(2,1)S(1)}, u32[]{:S(2)}) copy-start(bf16[1632,512]{1,0:T(8,128)(2,1)S(1)} %collective-permute-done.10.refs_1_.refs_6_) | copy-start | bytes 5013508
  131.6 3.7 %collective-permute-start.16 = (bf16[1632,512]{1,0:T(8,128)(2,1)S(1)}, bf16[1632,512]{1,0:T(8,128)(2,1)}, u32[]{:S(2)}, u32[]{:S(2)}) collective-permute-start(bf16[1632,512]{1,0:T(8,128)(2,1)S(1)} %collective-permute-done.9.refs_0_.refs_5_), channel_id=1, source_target_pairs={{0,2},{2,0},{4,6},{6,4},{8,10},{10,8},{12,14},{14,12},{16,18},{18,... | collective-permute-start | bytes 5013512 | tf_op jit(solution)/shard_map/ppermute | solution.py:17
  131.7 6.1 %collective-permute-start.17 = (bf16[1632,512]{1,0:T(8,128)(2,1)S(1)}, bf16[1632,512]{1,0:T(8,128)(2,1)}, u32[]{:S(2)}, u32[]{:S(2)}) collective-permute-start(bf16[1632,512]{1,0:T(8,128)(2,1)S(1)} %collective-permute-done.10.refs_1_.refs_6_), channel_id=1, source_target_pairs={{0,2},{2,0},{4,6},{6,4},{8,10},{10,8},{12,14},{14,12},{16,18},{18,... | collective-permute-start | bytes 5013512 | tf_op jit(solution)/shard_map/ppermute | solution.py:17
  133.3 16.2 %collective-permute-start.15 = (bf16[1120,512]{1,0:T(8,128)(2,1)}, bf16[1120,512]{1,0:T(8,128)(2,1)}, u32[]{:S(2)}, u32[]{:S(2)}) collective-permute-start(bf16[1120,512]{1,0:T(8,128)(2,1)} %slice_select_fusion), channel_id=1, source_target_pairs={{0,8},{8,16},{16,24},{24,28},{28,20},{20,12},{12,4},{4,0},{10,2},{... | collective-permute-start | bytes 3440648 | tf_op jit(solution)/shard_map/ppermute | solution.py:485
  148.2 12.6 %copy-start.13 = (f32[160,256]{1,0:T(8,128)S(1)}, f32[160,256]{1,0:T(8,128)}, u32[]{:S(2)}) copy-start(f32[160,256]{1,0:T(8,128)} %copy-done.12) | copy-start | bytes 491524
  149.5 3.0 %collective-permute-start.19 = (bf16[1120,512]{1,0:T(8,128)(2,1)}, bf16[1120,512]{1,0:T(8,128)(2,1)S(1)}, u32[]{:S(2)}, u32[]{:S(2)}) collective-permute-start(bf16[1120,512]{1,0:T(8,128)(2,1)} %collective-permute-done.15.refs_0_.refs_7_), channel_id=1, source_target_pairs={{0,2},{2,0},{4,6},{6,4},{8,10},{10,8},{12,14},{14,12},{16,18},{18,... | collective-permute-start | bytes 3440648 | tf_op jit(solution)/shard_map/ppermute | solution.py:17
  149.5 9.2 %collective-permute-start.18 = (bf16[512,512]{1,0:T(8,128)(2,1)S(1)}, bf16[512,512]{1,0:T(8,128)(2,1)S(1)}, u32[]{:S(2)}, u32[]{:S(2)}) collective-permute-start(bf16[512,512]{1,0:T(8,128)(2,1)S(1)} %slice_select_fusion.1), channel_id=1, source_target_pairs={{0,8},{8,16},{16,24},{24,28},{28,20},{20,12},{12,4},{4,0},{10,2},{... | collective-permute-start | bytes 1572872 | tf_op jit(solution)/shard_map/ppermute | solution.py:491
  158.6 5.0 %collective-permute-start.20 = (bf16[512,512]{1,0:T(8,128)(2,1)S(1)}, bf16[512,512]{1,0:T(8,128)(2,1)S(1)}, u32[]{:S(2)}, u32[]{:S(2)}) collective-permute-start(bf16[512,512]{1,0:T(8,128)(2,1)S(1)} %collective-permute-done.18.refs_0_), channel_id=1, source_target_pairs={{0,2},{2,0},{4,6},{6,4},{8,10},{10,8},{12,14},{14,12},{16,18},{18,... | collective-permute-start | bytes 1572872 | tf_op jit(solution)/shard_map/ppermute | solution.py:17
  159.3 8.0 %collective-permute-start.21 = (bf16[160,256]{1,0:T(8,128)(2,1)}, bf16[160,256]{1,0:T(8,128)(2,1)S(1)}, u32[]{:S(2)}, u32[]{:S(2)}) collective-permute-start(bf16[160,256]{1,0:T(8,128)(2,1)} %convert_element_type.44), channel_id=1, source_target_pairs={{0,1},{1,0},{2,3},{3,2},{4,5},{5,4},{6,7},{7,6},{8,9},{9,8},{10,11... | collective-permute-start | bytes 245768 | tf_op jit(solution)/shard_map/ppermute | solution.py:17
  161.4 5.9 %collective-permute-start.22 = (bf16[160,256]{1,0:T(8,128)(2,1)}, bf16[160,256]{1,0:T(8,128)(2,1)S(1)}, u32[]{:S(2)}, u32[]{:S(2)}) collective-permute-start(bf16[160,256]{1,0:T(8,128)(2,1)} %convert_element_type.45), channel_id=1, source_target_pairs={{0,1},{1,0},{2,3},{3,2},{4,5},{5,4},{6,7},{7,6},{8,9},{9,8},{10,11... | collective-permute-start | bytes 245768 | tf_op jit(solution)/shard_map/ppermute | solution.py:17
  162.0 5.4 %collective-permute-start.23 = (bf16[80,256]{1,0:T(8,128)(2,1)S(1)}, bf16[80,256]{1,0:T(8,128)(2,1)S(1)}, u32[]{:S(2)}, u32[]{:S(2)}) collective-permute-start(bf16[80,256]{1,0:T(8,128)(2,1)S(1)} %convert_element_type.46), channel_id=1, source_target_pairs={{0,1},{1,0},{2,3},{3,2},{4,5},{5,4},{6,7},{7,6},{8,9},{9,8},{10,11... | collective-permute-start | bytes 122888 | tf_op jit(solution)/shard_map/ppermute | solution.py:17
  168.4 2.2 collective-permute-start.24
  171.0 7.4 %collective-permute-start.25 = (bf16[2,32,640]{2,1,0:T(8,128)(2,1)S(1)}, bf16[2,32,640]{2,1,0:T(8,128)(2,1)S(1)}, u32[]{:S(2)}, u32[]{:S(2)}) collective-permute-start(bf16[2,32,640]{2,1,0:T(8,128)(2,1)S(1)} %get-tuple-element.56), channel_id=1, source_target_pairs={{0,4},{2,6},{4,0},{6,2},{8,12},{10,14},{12,8},{14,10},{16,20},{18,... | collective-permute-start | bytes 245768 | tf_op jit(solution)/shard_map/ppermute | solution.py:17
  171.7 10.3 %collective-permute-start.26 = (bf16[2,32,640]{2,1,0:T(8,128)(2,1)S(1)}, bf16[2,32,640]{2,1,0:T(8,128)(2,1)S(1)}, u32[]{:S(2)}, u32[]{:S(2)}) collective-permute-start(bf16[2,32,640]{2,1,0:T(8,128)(2,1)S(1)} %get-tuple-element.57), channel_id=1, source_target_pairs={{0,8},{2,10},{4,12},{6,14},{8,0},{10,2},{12,4},{14,6},{16,24},{18,... | collective-permute-start | bytes 245768 | tf_op jit(solution)/shard_map/ppermute | solution.py:17
  174.0 11.0 %collective-permute-start.27 = (bf16[2,32,640]{2,1,0:T(8,128)(2,1)S(1)}, bf16[2,32,640]{2,1,0:T(8,128)(2,1)S(1)}, u32[]{:S(2)}, u32[]{:S(2)}) collective-permute-start(bf16[2,32,640]{2,1,0:T(8,128)(2,1)S(1)} %get-tuple-element.58), channel_id=1, source_target_pairs={{0,12},{2,14},{4,8},{6,10},{8,4},{10,6},{12,0},{14,2},{16,28},{18,... | collective-permute-start | bytes 245768 | tf_op jit(solution)/shard_map/ppermute | solution.py:17
  175.4 12.2 %collective-permute-start.28 = (bf16[2,32,640]{2,1,0:T(8,128)(2,1)S(1)}, bf16[2,32,640]{2,1,0:T(8,128)(2,1)S(1)}, u32[]{:S(2)}, u32[]{:S(2)}) collective-permute-start(bf16[2,32,640]{2,1,0:T(8,128)(2,1)S(1)} %get-tuple-element.59), channel_id=1, source_target_pairs={{0,16},{2,18},{4,20},{6,22},{8,24},{10,26},{12,28},{14,30},{16,0},... | collective-permute-start | bytes 245768 | tf_op jit(solution)/shard_map/ppermute | solution.py:17
  177.9 11.9 %collective-permute-start.29 = (bf16[2,32,640]{2,1,0:T(8,128)(2,1)S(1)}, bf16[2,32,640]{2,1,0:T(8,128)(2,1)S(1)}, u32[]{:S(2)}, u32[]{:S(2)}) collective-permute-start(bf16[2,32,640]{2,1,0:T(8,128)(2,1)S(1)} %get-tuple-element.60), channel_id=1, source_target_pairs={{0,20},{2,22},{4,16},{6,18},{8,28},{10,30},{12,24},{14,26},{16,4},... | collective-permute-start | bytes 245768 | tf_op jit(solution)/shard_map/ppermute | solution.py:17
  178.4 11.4 %collective-permute-start.30 = (bf16[2,32,640]{2,1,0:T(8,128)(2,1)S(1)}, bf16[2,32,640]{2,1,0:T(8,128)(2,1)S(1)}, u32[]{:S(2)}, u32[]{:S(2)}) collective-permute-start(bf16[2,32,640]{2,1,0:T(8,128)(2,1)S(1)} %get-tuple-element.61), channel_id=1, source_target_pairs={{0,24},{2,26},{4,28},{6,30},{8,16},{10,18},{12,20},{14,22},{16,8},... | collective-permute-start | bytes 245768 | tf_op jit(solution)/shard_map/ppermute | solution.py:17
  182.0 7.9 %collective-permute-start.31 = (bf16[2,32,640]{2,1,0:T(8,128)(2,1)S(1)}, bf16[2,32,640]{2,1,0:T(8,128)(2,1)S(1)}, u32[]{:S(2)}, u32[]{:S(2)}) collective-permute-start(bf16[2,32,640]{2,1,0:T(8,128)(2,1)S(1)} %get-tuple-element.62), channel_id=1, source_target_pairs={{0,28},{2,30},{4,24},{6,26},{8,20},{10,22},{12,16},{14,18},{16,12}... | collective-permute-start | bytes 245768 | tf_op jit(solution)/shard_map/ppermute | solution.py:17
  190.0 7.7 %collective-permute-start.34 = (bf16[32,640]{1,0:T(8,128)(2,1)S(1)}, bf16[32,640]{1,0:T(8,128)(2,1)S(1)}, u32[]{:S(2)}, u32[]{:S(2)}) collective-permute-start(bf16[32,640]{1,0:T(8,128)(2,1)S(1)} %bitcast.124), channel_id=1, source_target_pairs={{0,24},{2,26},{4,28},{6,30},{8,16},{10,18},{12,20},{14,22},{16,8},... | collective-permute-start | bytes 122888 | tf_op jit(solution)/shard_map/ppermute | solution.py:17
  192.9 5.0 %collective-permute-start.33 = (bf16[32,640]{1,0:T(8,128)(2,1)S(1)}, bf16[32,640]{1,0:T(8,128)(2,1)S(1)}, u32[]{:S(2)}, u32[]{:S(2)}) collective-permute-start(bf16[32,640]{1,0:T(8,128)(2,1)S(1)} %bitcast.125), channel_id=1, source_target_pairs={{0,16},{2,18},{4,20},{6,22},{8,24},{10,26},{12,28},{14,30},{16,0},... | collective-permute-start | bytes 122888 | tf_op jit(solution)/shard_map/ppermute | solution.py:17
  195.3 4.0 %collective-permute-start.32 = (bf16[32,640]{1,0:T(8,128)(2,1)S(1)}, bf16[32,640]{1,0:T(8,128)(2,1)S(1)}, u32[]{:S(2)}, u32[]{:S(2)}) collective-permute-start(bf16[32,640]{1,0:T(8,128)(2,1)S(1)} %bitcast.126), channel_id=1, source_target_pairs={{0,8},{2,10},{4,12},{6,14},{8,0},{10,2},{12,4},{14,6},{16,24},{18,... | collective-permute-start | bytes 122888 | tf_op jit(solution)/shard_map/ppermute | solution.py:17
  195.8 8.7 %collective-permute-start.39 = (f32[32,320]{1,0:T(8,128)S(1)}, f32[32,320]{1,0:T(8,128)S(1)}, u32[]{:S(2)}, u32[]{:S(2)}) collective-permute-start(f32[32,320]{1,0:T(8,128)S(1)} %get-tuple-element.74), channel_id=1, source_target_pairs={{0,1},{2,0},{4,3},{6,2},{8,5},{10,4},{12,7},{14,6},{16,9},{18,8},{... | collective-permute-start | bytes 122888 | tf_op jit(solution)/shard_map/ppermute | solution.py:417
  197.0 7.6 %collective-permute-start.38 = (f32[32,320]{1,0:T(8,128)S(1)}, f32[32,320]{1,0:T(8,128)S(1)}, u32[]{:S(2)}, u32[]{:S(2)}) collective-permute-start(f32[32,320]{1,0:T(8,128)S(1)} %get-tuple-element.75), channel_id=1, source_target_pairs={{0,0},{2,1},{4,2},{6,3},{8,4},{10,5},{12,6},{14,7},{16,8},{18,9},{... | collective-permute-start | bytes 122888 | tf_op jit(solution)/shard_map/ppermute | solution.py:417
  199.3 12.5 %collective-permute-start.36 = (bf16[4,32,640]{2,1,0:T(8,128)(2,1)S(1)}, bf16[4,32,640]{2,1,0:T(8,128)(2,1)S(1)}, u32[]{:S(2)}, u32[]{:S(2)}) collective-permute-start(bf16[4,32,640]{2,1,0:T(8,128)(2,1)S(1)} %get-tuple-element.73), channel_id=1, source_target_pairs={{0,1},{1,0},{2,3},{3,2},{4,5},{5,4},{6,7},{7,6},{8,9},{9,8},{10,11... | collective-permute-start | bytes 491528 | tf_op jit(solution)/shard_map/ppermute | solution.py:400
  203.0 8.8 %collective-permute-start.35 = (bf16[4,32,640]{2,1,0:T(8,128)(2,1)S(1)}, bf16[4,32,640]{2,1,0:T(8,128)(2,1)S(1)}, u32[]{:S(2)}, u32[]{:S(2)}) collective-permute-start(bf16[4,32,640]{2,1,0:T(8,128)(2,1)S(1)} %get-tuple-element.73), channel_id=1, source_target_pairs={{0,4},{1,5},{2,6},{3,7},{4,0},{5,1},{6,2},{7,3},{8,12},{9,13},{10,... | collective-permute-start | bytes 491528 | tf_op jit(solution)/shard_map/ppermute | solution.py:400
  203.6 8.2 %collective-permute-start.37 = (bf16[4,32,640]{2,1,0:T(8,128)(2,1)S(1)}, bf16[4,32,640]{2,1,0:T(8,128)(2,1)S(1)}, u32[]{:S(2)}, u32[]{:S(2)}) collective-permute-start(bf16[4,32,640]{2,1,0:T(8,128)(2,1)S(1)} %get-tuple-element.73), channel_id=1, source_target_pairs={{0,5},{1,4},{2,7},{3,6},{4,1},{5,0},{6,3},{7,2},{8,13},{9,12},{10,... | collective-permute-start | bytes 491528 | tf_op jit(solution)/shard_map/ppermute | solution.py:400
  212.0 2.2 collective-permute-start.40
  (11 other events, 46.7 us)

commit v3 on v2

--- a/solution.py
+++ b/solution.py
@@ -10,6 +10,8 @@
 BF16, F32 = jnp.bfloat16, jnp.float32
 VMEM_BYTES = 48 * 1024 * 1024
 EXPAND_ROWS = 4096
+AHEAD = 2
+PROJECT_UNITS = 8192
 
 
 def flip(x, axis_name, bit):
@@ -74,29 +76,33 @@
 
 
 def project_kernel(tiles, rows, at_ref, acts_ref, *refs):
-    sums_ref = refs[-1]
-    count = len(refs) // 2
+    sums_ref, held = refs[-2:]
+    count = len(refs) // 2 - 1
     step = pl.program_id(0)
     lanes = refs[0].shape[1]
 
     @pl.when(step == 0)
     def _():
-        sums_ref[...] = jnp.zeros_like(sums_ref)
+        held[...] = jnp.zeros_like(held)
 
     def add(pieces):
-        total = sums_ref[...]
+        total = held[...]
         for c in range(pieces[0].shape[0] // rows):
             part = jnp.concatenate([piece[c * rows : (c + 1) * rows] for piece in pieces], axis=0)
             total += lax.dot_general(
+                acts_ref[:, c * lanes : (c + 1) * lanes],
                 part,
-                acts_ref[:, c * lanes : (c + 1) * lanes],
                 (((1,), (1,)), ((), ())),
                 preferred_element_type=F32,
             )
-        sums_ref[...] = total
+        held[...] = total
 
     pl.when(step < tiles)(lambda: add(refs[:count]))
-    pl.when(step >= tiles)(lambda: add(refs[count:-1]))
+    pl.when(step >= tiles)(lambda: add(refs[count:-2]))
+
+    @pl.when(step == 2 * tiles - 1)
+    def _():
+        sums_ref[...] = held[...].T
 
 
 def project(owns, others, rows, core, acts, costed=False):
@@ -112,7 +118,7 @@
                 [lax.dot_general(p, half, (((1,), (1,)), ((), ())), preferred_element_type=F32) for p in plain]
             )
         return total
-    group = max(g for g in range(1, chunks + 1) if chunks % g == 0 and g * lanes <= 4096)
+    group = max(g for g in range(1, chunks + 1) if chunks % g == 0 and g * lanes <= PROJECT_UNITS)
     tiles = chunks // group
     return pl.pallas_call(
         functools.partial(project_kernel, tiles, rows),
@@ -123,6 +129,7 @@
             + [halves_spec((group * rows, lanes), tiles, False)] * len(owns)
             + [halves_spec((group * rows, lanes), tiles, True)] * len(owns),
             out_specs=whole_block((len(owns) * rows, tokens)),
+            scratch_shapes=[pltpu.VMEM((tokens, len(owns) * rows), F32)],
         ),
         out_shape=jax.ShapeDtypeStruct((len(owns) * rows, tokens), F32),
         compiler_params=pltpu.CompilerParams(vmem_limit_bytes=VMEM_BYTES),
@@ -209,31 +216,81 @@
 
 
 def expand_kernel(tiles, rows, at_ref, near_ref, far_ref, turn_ref, *refs):
-    out_ref, back, held = refs[-3:]
-    count = back.shape[0] // rows
-    step = pl.program_id(0)
-
-    @pl.when(step == 0)
-    def _():
-        dims = (((0,), (0,)), ((), ()))
-        depth = near_ref.shape[0]
-        total = lax.dot_general(near_ref[...], turn_ref[:depth], dims, preferred_element_type=F32)
-        total += lax.dot_general(far_ref[...], turn_ref[depth:], dims, preferred_element_type=F32)
-        back[...] = total.astype(BF16)
-        for k in range(count):
-            start = pl.multiple_of(at_ref[1 + k] * rows, 16)
-            held[k * rows : (k + 1) * rows] = back[pl.ds(start, rows)]
-
-    def fill(pieces):
-        lanes = pieces[0].shape[1]
-        for c in range(pieces[0].shape[0] // rows):
-            part = jnp.concatenate([piece[c * rows : (c + 1) * rows] for piece in pieces], axis=0)
-            out_ref[c * lanes : (c + 1) * lanes] = lax.dot_general(
-                part, held[...], (((0,), (0,)), ((), ())), preferred_element_type=F32
-            ).astype(out_ref.dtype)
-
-    pl.when(step < tiles)(lambda: fill(refs[:count]))
-    pl.when(step >= tiles)(lambda: fill(refs[count:-3]))
+    count = (len(refs) - 9) // 2
+    owns, others, out_ref = refs[:count], refs[count : 2 * count], refs[2 * count]
+    scaled, turned, back, held, pieces, sent, first_sem, piece_sem, out_sem = refs[-9:]
+    deep = pieces.shape[2]
+    ahead = min(AHEAD, tiles)
+    depth, lanes = near_ref.shape[0], pieces.shape[3]
+    out_rows = sent.shape[1]
+
+    def fetch(group, half, t):
+        tile = half * tiles + t
+        return [
+            pltpu.make_async_copy(ref.at[pl.ds(t * deep, deep)], pieces.at[tile, k], piece_sem.at[tile, k])
+            for k, ref in enumerate(group)
+        ]
+
+    def store(half, t):
+        side = at_ref[0] if half == 0 else 1 - at_ref[0]
+        tile = half * tiles + t
+        return pltpu.make_async_copy(
+            sent.at[tile % 2], out_ref.at[pl.ds((side * tiles + t) * out_rows, out_rows)], out_sem.at[tile % 2]
+        )
+
+    opening = [
+        pltpu.make_async_copy(near_ref, scaled.at[0], first_sem.at[0]),
+        pltpu.make_async_copy(far_ref, scaled.at[1], first_sem.at[1]),
+        pltpu.make_async_copy(turn_ref, turned, first_sem.at[2]),
+    ]
+    for copy in opening:
+        copy.start()
+    for t in range(ahead):
+        for copy in fetch(owns, 0, t):
+            copy.start()
+    for copy in opening:
+        copy.wait()
+    dims = (((0,), (0,)), ((), ()))
+    total = lax.dot_general(scaled[0], turned[:depth], dims, preferred_element_type=F32)
+    total += lax.dot_general(scaled[1], turned[depth:], dims, preferred_element_type=F32)
+    back[...] = total.astype(BF16)
+    for k in range(count):
+        start = pl.multiple_of(at_ref[1 + k] * rows, 16)
+        held[k * rows : (k + 1) * rows] = back[pl.ds(start, rows)]
+
+    def step(half, group, t, more, next_half, next_group, next_t, settled):
+        if more:
+            for copy in fetch(next_group, next_half, next_t):
+                copy.start()
+        for copy in fetch(group, half, t):
+            copy.wait()
+        tile = half * tiles + t
+        if settled is not None:
+            store(*settled).wait()
+        for c in range(deep // rows):
+            part = jnp.concatenate([pieces[tile, k, c * rows : (c + 1) * rows] for k in range(count)], axis=0)
+            sent[tile % 2, c * lanes : (c + 1) * lanes] = lax.dot_general(
+                part, held[...], dims, preferred_element_type=F32
+            ).astype(BF16)
+        store(half, t).start()
+
+    for half, group in ((0, owns), (1, others)):
+        for t in range(tiles):
+            tile = half * tiles + t
+            coming = tile + ahead
+            before = tile - 2
+            step(
+                half,
+                group,
+                t,
+                coming < 2 * tiles,
+                coming // tiles,
+                owns if coming < tiles else others,
+                coming % tiles,
+                (before // tiles, before % tiles) if before >= 0 else None,
+            )
+    for tile in (2 * tiles - 2, 2 * tiles - 1):
+        store(tile // tiles, tile % tiles).wait()
 
 
 def expand(owns, others, pairs, rows, units, core, near, far, turn):
@@ -252,21 +309,31 @@
         return jnp.where(core == 0, jnp.concatenate(sides), jnp.concatenate(sides[::-1]))
     group = max(g for g in range(1, chunks + 1) if chunks % g == 0 and g * lanes <= EXPAND_ROWS)
     tiles = chunks // group
+    count = len(owns)
+    anywhere = pl.BlockSpec(memory_space=pl.ANY)
     return pl.pallas_call(
         functools.partial(expand_kernel, tiles, rows),
         grid_spec=pltpu.PrefetchScalarGridSpec(
             num_scalar_prefetch=1,
-            grid=(2 * tiles,),
-            in_specs=[whole_block(near.shape), whole_block(far.shape), whole_block(turn.shape)]
-            + [halves_spec((group * rows, lanes), tiles, False)] * len(owns)
-            + [halves_spec((group * rows, lanes), tiles, True)] * len(owns),
-            out_specs=pl.BlockSpec((group * lanes, columns), lambda i, at_ref: (tile_index(i, tiles, at_ref), 0)),
-            scratch_shapes=[pltpu.VMEM((len(owns) * rows, columns), BF16)] * 2,
+            grid=(1,),
+            in_specs=[anywhere] * (3 + 2 * count),
+            out_specs=anywhere,
+            scratch_shapes=[
+                pltpu.VMEM((2,) + near.shape, BF16),
+                pltpu.VMEM(turn.shape, BF16),
+                pltpu.VMEM((count * rows, columns), BF16),
+                pltpu.VMEM((count * rows, columns), BF16),
+                pltpu.VMEM((2 * tiles, count, group * rows, lanes), BF16),
+                pltpu.VMEM((2, group * lanes, columns), BF16),
+                pltpu.SemaphoreType.DMA((3,)),
+                pltpu.SemaphoreType.DMA((2 * tiles, count)),
+                pltpu.SemaphoreType.DMA((2,)),
+            ],
         ),
         out_shape=jax.ShapeDtypeStruct((units, columns), BF16),
         compiler_params=pltpu.CompilerParams(vmem_limit_bytes=VMEM_BYTES),
         cost_estimate=pl.CostEstimate(
-            flops=2 * rows * len(owns) * units * columns, bytes_accessed=2 * units * columns, transcendentals=0
+            flops=2 * rows * count * units * columns, bytes_accessed=2 * units * columns, transcendentals=0
         ),
         name="expand_update",
     )(at, near, far, turn, *owns, *others)
@@ -431,9 +498,14 @@
     units = acts.shape[1]
     chunks = units // 2 // out_units
     own_rows = basis_in.shape[1]
-    mine = basis_in.T.reshape((own_rows, 2, chunks, out_units)).transpose(1, 2, 0, 3)
-    kept = lax.dynamic_index_in_dim(mine, core, 0, False)
-    got = flip(lax.dynamic_index_in_dim(mine, 1 - core, 0, False), "dp", 1)
+    mine = basis_in.T
+
+    def side_of(side):
+        part = lax.dynamic_slice(mine, (0, side * (units // 2)), (own_rows, units // 2))
+        return jnp.stack([part[:, c * out_units : (c + 1) * out_units] for c in range(chunks)])
+
+    kept = side_of(core)
+    got = flip(side_of(1 - core), "dp", 1)
     both = jnp.stack([jnp.where(core == 0, kept, got), jnp.where(core == 0, got, kept)], axis=1)
     rows = 2 * own_rows
     in_rows = chunks * rows
@@ -455,8 +527,8 @@
         origins = [2 * p + core for p in where_from] + [2 * p + 1 - core for p in where_from]
         grad_proj_t = add_grads(pieces, origins, wide_grads, grad_proj_t, n_dp)
 
-    def use(pieces, where_from, grads_too=True, costed=False):
-        swapped = [flip(piece, "dp", 1) for piece in pieces]
+    def use(pieces, where_from, grads_too=True, costed=False, known=()):
+        swapped = list(known) + [flip(piece, "dp", 1) for piece in pieces[len(known) :]]
         sums.append(project(pieces, swapped, rows, core, acts, costed))
         gots.append([flip(sums[-1].astype(BF16), "mp", 1)] if n_mp == 2 else [])
         owns.extend(pieces)
@@ -470,10 +542,11 @@
     for step in range(1, half // 2):
         moving = [lax.ppermute(x, "dp", everyone[k]) for k, x in enumerate(moving)]
         if step == 1:
-            moving, own_piece = lax.optimization_barrier((moving, own_piece))
+            swapped = flip(own_piece, "dp", 1)
+            moving, own_piece, swapped = lax.optimization_barrier((moving, own_piece, swapped))
             waiting = [own_piece], [me // 2]
         else:
-            use(*waiting)
+            use(*waiting, known=[swapped] if step == 2 else [])
             moving, sums[-1], gots[:-1], grad_proj_t, rows_near = lax.optimization_barrier(
                 (moving, sums[-1], gots[:-1], grad_proj_t, rows_near)
             )
@@ -487,11 +560,13 @@
     )
     held = jnp.where(core == 0, moving[0][in_rows:], moving[1][in_rows:])
     use(*waiting)
-    held, last, sums[-1], grad_proj_t = lax.optimization_barrier((held, last, sums[-1], grad_proj_t))
+    held, last, sums[-1], gots[:-1], grad_proj_t = lax.optimization_barrier(
+        (held, last, sums[-1], gots[:-1], grad_proj_t)
+    )
     last_out = lax.ppermute(held, "dp", last_hops)
     last_pair = began(half // 2)
     use([last], [last_pair], False, True)
-    last_out, sums[-1] = lax.optimization_barrier((last_out, sums[-1]))
+    last_out, sums[-1], gots[:-1] = lax.optimization_barrier((last_out, sums[-1], gots[:-1]))
     grad_proj_t = add_grads(
         [last_out, flip(last_out, "dp", 1)],
         [2 * last_pair + core, 2 * last_pair + 1 - core],

time: 235 us -> 226 us (0.962)
  Pallas kernels: 61 us -> 56.6 us
  starting transfers between devices: 45 us -> 41.5 us
  waiting for transfers between devices: 102 us -> 105 us
    ppermute x28, starting transfers between devices: 28.4 us -> 25.7 us  [flip(): return lax.ppermute(x, axis_name, [(i, i ^ bit) for i in range(size)])]
    pallas_call x4, Pallas kernels: 24.4 us -> 21.7 us  [project(): pl.pallas_call(functools.partial(project_kernel, tiles, rows), grid_spec=...]
where the time goes in v3:
time: 226 us
  waiting for transfers between devices  105 us (46%)
  Pallas kernels  56.6 us (25%)
  starting transfers between devices  41.5 us (18%)
  other arithmetic  13.8 us (6%)
  local copies, waits for them, and re-layouts  6.07 us (3%)
  between operations  2.32 us (1%)
    ppermute x6, waiting for transfers between devices, on_device(): moving = [lax.ppermute(x, 'dp', everyone[k]) for k, x in enumerate(moving)]  66 us
    ppermute x28, waiting for transfers between devices, flip(): return lax.ppermute(x, axis_name, [(i, i ^ bit) for i in range(size)])  27.6 us
    ppermute x28, starting transfers between devices, flip(): return lax.ppermute(x, axis_name, [(i, i ^ bit) for i in range(size)])  25.7 us
    pallas_call x4, Pallas kernels, project(): pl.pallas_call(functools.partial(project_kernel, tiles, rows), grid_spec=...  21.7 us
    pallas_call x1, Pallas kernels, expand(): pl.pallas_call(functools.partial(expand_kernel, tiles, rows), grid_spec=p...  17.8 us
    pallas_call x4, Pallas kernels, add_grads(): pl.pallas_call(add_grads_kernel, grid_spec=pltpu.PrefetchScalarGridSpec(n...  15.6 us
    ppermute x3, waiting for transfers between devices, gather_scaled(): parts[m, low] = lax.ppermute(x, ('dp', 'mp'), hops) if m or low else x  7.58 us
    ppermute x6, starting transfers between devices, on_device(): moving = [lax.ppermute(x, 'dp', everyone[k]) for k, x in enumerate(moving)]  6.08 us
  transfers between devices with their start and end apart: 41, of which 20 were waited for; matrix products, arithmetic and copies ran while one was open for 7% of the time, Pallas kernels for 17%

profile of v3, /device:TPU:0, one launch (start us, length us, event | category | flops | bytes accessed | tf_op | source)
XLA Modules:
  0.0 225.7 jit_solution(1775720745233102730)
XLA Ops:
  0.7 1.4 dynamic-slice_bitcast_fusion.1
  2.7 2.6 %collective-permute-start.8 = (bf16[1,256,4096]{2,1,0:T(8,128)(2,1)}, bf16[1,256,4096]{2,1,0:T(8,128)(2,1)}, u32[]{:S(2)}, u32[]{:S(2)}) collective-permute-start(bf16[1,256,4096]{2,1,0:T(8,128)(2,1)} %bitcast.60), channel_id=1, source_target_pairs={{0,1},{1,0},{2,3},{3,2},{4,5},{5,4},{6,7},{7,6},{8,9},{9,8},{10,11... | collective-permute-start | bytes 6291464 | tf_op jit(solution)/shard_map/ppermute | solution.py:19
  6.8 1.2 pad_maximum_fusion.refs_0_
  8.2 1.5 collective-permute-start.2
  10.3 1.5 collective-permute-done.3.refs_3_.refs_8_
  11.8 35.2 %collective-permute-done.2.refs_2_ = bf16[1632,512]{1,0:T(8,128)(2,1)S(1)} collective-permute-done((bf16[1632,512]{1,0:T(8,128)(2,1)S(1)}, bf16[1632,512]{1,0:T(8,128)(2,1)S(1)}, u32[]{:S(2)}, u32[]{:S(2)}) %collective-permute-start.2) | collective-permute-done | bytes 1671200 | tf_op jit(solution)/shard_map/ppermute | solution.py:543
  47.0 1.3 collective-permute-done.1.refs_1_
  49.4 1.5 collective-permute-start.5
  51.8 2.5 %select_bitcast_fusion.1 = (bf16[1,1,256,4096]{3,2,1,0:T(8,128)(2,1)S(1)}, bf16[1,1,256,4096]{3,2,1,0:T(8,128)(2,1)S(1)}) fusion(bf16[1,256,4096]{2,1,0:T(8,128)(2,1)} %collective-permute-done.8, pred[]{:T(512)S(6)} %eq.62, bf16[256,4096]{1,0:T(8,128)(2,1)} %param.6), kind=kLoop, calls=%fused_computation.2 | loop fusion | flops 2097152 | bytes 8388609 | tf_op jit(solution)/shard_map/stack | solution.py:36
  54.3 2.4 %maximum_bitcast_fusion.refs_6_.refs_7_.refs_8_.refs_9_.refs_10_.refs_11_.refs_4_.refs_5_.refs_2_.refs_3_ = bf16[2,256,4096]{2,1,0:T(8,128)(2,1)} fusion(bf16[1,1,256,4096]{3,2,1,0:T(8,128)(2,1)S(1)} %get-tuple-element.79, bf16[1,1,256,4096]{3,2,1,0:T(8,128)(2,1)S(1)} %get-tuple-element.78), kind=kLoop, calls=%fused_computation | loop fusion | flops 2097152 | bytes 8388608 | tf_op jit(solution)/shard_map/reshape | solution.py:36
  56.7 5.9 %project_acts.4.refs_0_ = f32[240,256]{1,0:T(8,128)S(1)} custom-call(s32[1]{0:T(128)} %bitcast.at_ref, bf16[256,14336]{1,0:T(8,128)(2,1)} %acts_ref.7, bf16[1632,512]{1,0:T(8,128)(2,1)S(1)} %pad_maximum_fusion.refs_0_, bf16[1632,512]{1,0:T(8,128)(2,1)} %collective-permute-done.1.refs_1_, bf16[1632,512]{1,0:T(8,128)(2,1)S(1)} %collective-permute-done.2.refs_2_, ...), custom_call_target="tpu_custom_call" | custom-call | flops 1 | bytes 1 | tf_op jit(solution)/shard_map/project_acts/pallas_call | solution.py:123
  63.4 5.0 %add_grads.4.refs_8_ = f32[512,256]{1,0:T(8,128)S(1)} custom-call(s32[12]{0:T(128)S(1)} %stack.357.at_ref, bf16[1632,512]{1,0:T(8,128)(2,1)S(1)} %pad_maximum_fusion.refs_0_, bf16[1632,512]{1,0:T(8,128)(2,1)} %collective-permute-done.1.refs_1_, bf16[1632,512]{1,0:T(8,128)(2,1)S(1)} %collective-permute-done.2.refs_2_, ...), custom_call_target="tpu_custom_call" | custom-call | flops 1 | bytes 1 | tf_op jit(solution)/shard_map/add_grads/pallas_call | solution.py:179
  69.2 18.4 %collective-permute-done.4.refs_0_.refs_3_ = bf16[1632,512]{1,0:T(8,128)(2,1)} collective-permute-done((bf16[1632,512]{1,0:T(8,128)(2,1)}, bf16[1632,512]{1,0:T(8,128)(2,1)}, u32[]{:S(2)}, u32[]{:S(2)}) %collective-permute-start.4) | collective-permute-done | bytes 1671200 | tf_op jit(solution)/shard_map/ppermute | solution.py:543
  88.1 1.6 collective-permute-start.9
  91.9 11.9 %collective-permute-done.14 = bf16[1,512,512]{2,1,0:T(8,128)(2,1)} collective-permute-done((bf16[1,512,512]{2,1,0:T(8,128)(2,1)}, bf16[1,512,512]{2,1,0:T(8,128)(2,1)}, u32[]{:S(2)}, u32[]{:S(2)}) %collective-permute-start.14) | collective-permute-done | bytes 524320 | tf_op jit(solution)/shard_map/ppermute | solution.py:19
  104.4 2.3 %pad_maximum_fusion.2 = bf16[2,512,512]{2,1,0:T(8,128)(2,1)} fusion(bf16[1,512,512]{2,1,0:T(8,128)(2,1)} %collective-permute-done.14, bf16[1,512,512]{2,1,0:T(8,128)(2,1)} %bitcast.72), kind=kLoop, calls=%fused_computation.10 | loop fusion | flops 524288 | bytes 2097152 | tf_op jit(solution)/shard_map/concatenate | solution.py:345
  106.7 5.9 %project_acts.5.refs_1_ = f32[160,256]{1,0:T(8,128)S(1)} custom-call(s32[1]{0:T(128)} %bitcast.at_ref, bf16[256,14336]{1,0:T(8,128)(2,1)} %acts_ref.7, bf16[1632,512]{1,0:T(8,128)(2,1)} %collective-permute-done.4.refs_0_.refs_3_, bf16[1632,512]{1,0:T(8,128)(2,1)} %collective-permute-done.5.refs_1_.refs_4_, ...), custom_call_target="tpu_custom_call" | custom-call | flops 1 | bytes 1 | tf_op jit(solution)/shard_map/project_acts/pallas_call | solution.py:123
  112.6 4.4 %add_grads.5.refs_8_ = f32[512,256]{1,0:T(8,128)S(1)} custom-call(s32[8]{0:T(128)S(1)} %stack.369.at_ref, bf16[1632,512]{1,0:T(8,128)(2,1)} %collective-permute-done.4.refs_0_.refs_3_, bf16[1632,512]{1,0:T(8,128)(2,1)} %collective-permute-done.5.refs_1_.refs_4_, bf16[1632,512]{1,0:T(8,128)(2,1)} %collective-permute-done.11.refs_2_.refs_11_, ...), custom_call_target="tpu_custom_call" | custom-call | flops 1 | bytes 1 | tf_op jit(solution)/shard_map/add_grads/pallas_call | solution.py:179
  117.1 9.7 %collective-permute-done.9.refs_0_.refs_5_ = bf16[1632,512]{1,0:T(8,128)(2,1)S(1)} collective-permute-done((bf16[1632,512]{1,0:T(8,128)(2,1)}, bf16[1632,512]{1,0:T(8,128)(2,1)S(1)}, u32[]{:S(2)}, u32[]{:S(2)}) %collective-permute-start.9) | collective-permute-done | bytes 1671200 | tf_op jit(solution)/shard_map/ppermute | solution.py:543
  126.7 1.3 collective-permute-done.10.refs_1_.refs_6_
  128.5 1.1 slice_select_fusion
  129.7 1.6 collective-permute-start.15
  132.2 1.9 collective-permute-done.17.refs_3_.refs_14_
  134.1 5.2 %project_acts.6.refs_2_ = f32[160,256]{1,0:T(8,128)S(1)} custom-call(s32[1]{0:T(128)} %bitcast.at_ref, bf16[256,14336]{1,0:T(8,128)(2,1)} %acts_ref.7, bf16[1632,512]{1,0:T(8,128)(2,1)S(1)} %collective-permute-done.9.refs_0_.refs_5_, bf16[1632,512]{1,0:T(8,128)(2,1)S(1)} %collective-permute-done.10.refs_1_.refs_6_, ...), custom_call_target="tpu_custom_call" | custom-call | flops 1 | bytes 1 | tf_op jit(solution)/shard_map/project_acts/pallas_call | solution.py:123
  139.3 3.7 %add_grads.6.refs_4_ = f32[512,256]{1,0:T(8,128)S(1)} custom-call(s32[8]{0:T(128)S(1)} %stack.378.at_ref, bf16[1632,512]{1,0:T(8,128)(2,1)S(1)} %collective-permute-done.9.refs_0_.refs_5_, bf16[1632,512]{1,0:T(8,128)(2,1)S(1)} %collective-permute-done.10.refs_1_.refs_6_, bf16[1632,512]{1,0:T(8,128)(2,1)} %collective-permute-done.16.refs_2_.refs_13_, ...), custom_call_target="tpu_custom_call" | custom-call | flops 1 | bytes 1 | tf_op jit(solution)/shard_map/add_grads/pallas_call | solution.py:179
  143.0 2.8 %collective-permute-done.15.refs_0_.refs_7_ = bf16[1120,512]{1,0:T(8,128)(2,1)} collective-permute-done((bf16[1120,512]{1,0:T(8,128)(2,1)}, bf16[1120,512]{1,0:T(8,128)(2,1)}, u32[]{:S(2)}, u32[]{:S(2)}) %collective-permute-start.15) | collective-permute-done | bytes 1146912 | tf_op jit(solution)/shard_map/ppermute | solution.py:558
  145.8 1.6 collective-permute-start.19
  148.9 4.7 %project_acts.7.refs_3_ = f32[80,256]{1,0:T(8,128)S(1)} custom-call(s32[1]{0:T(128)} %bitcast.at_ref, bf16[256,14336]{1,0:T(8,128)(2,1)} %acts_ref.7, bf16[1120,512]{1,0:T(8,128)(2,1)} %collective-permute-done.15.refs_0_.refs_7_, bf16[1120,512]{1,0:T(8,128)(2,1)S(1)} %collective-permute-done.20.refs_1_.refs_15_), custom_call_target="tpu_custom_call" | custom-call | flops 587202560 | bytes 9633792 | tf_op jit(solution)/shard_map/project_acts/pallas_call | solution.py:123
  153.6 1.4 collective-permute-done.19.refs_0_
  156.9 1.0 copy-done.11
  158.0 2.6 %add_grads.7 = f32[512,256]{1,0:T(8,128)S(1)} custom-call(s32[4]{0:T(128)S(1)} %pad_add_fusion.at_ref, bf16[512,512]{1,0:T(8,128)(2,1)S(1)} %collective-permute-done.19.refs_0_, bf16[512,512]{1,0:T(8,128)(2,1)S(1)} %collective-permute-done.22.refs_1_, ...), custom_call_target="tpu_custom_call" | custom-call | flops 1 | bytes 1 | tf_op jit(solution)/shard_map/add_grads/pallas_call | solution.py:179
  161.9 2.0 collective-permute-done.24.got_ref
  165.0 1.6 collective-permute-start.26
  167.3 1.3 collective-permute-start.27
  168.6 2.6 %collective-permute-start.28 = (bf16[2,32,640]{2,1,0:T(8,128)(2,1)S(1)}, bf16[2,32,640]{2,1,0:T(8,128)(2,1)S(1)}, u32[]{:S(2)}, u32[]{:S(2)}) collective-permute-start(bf16[2,32,640]{2,1,0:T(8,128)(2,1)S(1)} %get-tuple-element.71), channel_id=1, source_target_pairs={{0,16},{2,18},{4,20},{6,22},{8,24},{10,26},{12,28},{14,30},{16,0},... | collective-permute-start | bytes 245768 | tf_op jit(solution)/shard_map/ppermute | solution.py:19
  171.6 3.6 %collective-permute-start.30 = (bf16[2,32,640]{2,1,0:T(8,128)(2,1)S(1)}, bf16[2,32,640]{2,1,0:T(8,128)(2,1)S(1)}, u32[]{:S(2)}, u32[]{:S(2)}) collective-permute-start(bf16[2,32,640]{2,1,0:T(8,128)(2,1)S(1)} %get-tuple-element.73), channel_id=1, source_target_pairs={{0,24},{2,26},{4,28},{6,30},{8,16},{10,18},{12,20},{14,22},{16,8},... | collective-permute-start | bytes 245768 | tf_op jit(solution)/shard_map/ppermute | solution.py:19
  175.2 1.1 collective-permute-start.31
  176.3 2.0 reverse_select_fusion.3
  178.3 2.5 %collective-permute-done.28 = bf16[2,32,640]{2,1,0:T(8,128)(2,1)S(1)} collective-permute-done((bf16[2,32,640]{2,1,0:T(8,128)(2,1)S(1)}, bf16[2,32,640]{2,1,0:T(8,128)(2,1)S(1)}, u32[]{:S(2)}, u32[]{:S(2)}) %collective-permute-start.28) | collective-permute-done | bytes 81952 | tf_op jit(solution)/shard_map/ppermute | solution.py:19
  180.8 2.3 %collective-permute-done.29 = bf16[2,32,640]{2,1,0:T(8,128)(2,1)S(1)} collective-permute-done((bf16[2,32,640]{2,1,0:T(8,128)(2,1)S(1)}, bf16[2,32,640]{2,1,0:T(8,128)(2,1)S(1)}, u32[]{:S(2)}, u32[]{:S(2)}) %collective-permute-start.29) | collective-permute-done | bytes 81952 | tf_op jit(solution)/shard_map/ppermute | solution.py:19
  183.2 3.0 %collective-permute-start.34 = (bf16[32,640]{1,0:T(8,128)(2,1)S(1)}, bf16[32,640]{1,0:T(8,128)(2,1)S(1)}, u32[]{:S(2)}, u32[]{:S(2)}) collective-permute-start(bf16[32,640]{1,0:T(8,128)(2,1)S(1)} %bitcast.225), channel_id=1, source_target_pairs={{0,24},{2,26},{4,28},{6,30},{8,16},{10,18},{12,20},{14,22},{16,8},... | collective-permute-start | bytes 122888 | tf_op jit(solution)/shard_map/ppermute | solution.py:19
  186.2 2.3 %collective-permute-start.33 = (bf16[32,640]{1,0:T(8,128)(2,1)S(1)}, bf16[32,640]{1,0:T(8,128)(2,1)S(1)}, u32[]{:S(2)}, u32[]{:S(2)}) collective-permute-start(bf16[32,640]{1,0:T(8,128)(2,1)S(1)} %bitcast.226), channel_id=1, source_target_pairs={{0,16},{2,18},{4,20},{6,22},{8,24},{10,26},{12,28},{14,30},{16,0},... | collective-permute-start | bytes 122888 | tf_op jit(solution)/shard_map/ppermute | solution.py:19
  191.2 1.3 collective-permute-done.32
  192.6 3.4 %collective-permute-start.36 = (bf16[4,32,640]{2,1,0:T(8,128)(2,1)S(1)}, bf16[4,32,640]{2,1,0:T(8,128)(2,1)S(1)}, u32[]{:S(2)}, u32[]{:S(2)}) collective-permute-start(bf16[4,32,640]{2,1,0:T(8,128)(2,1)S(1)} %get-tuple-element.87), channel_id=1, source_target_pairs={{0,1},{1,0},{2,3},{3,2},{4,5},{5,4},{6,7},{7,6},{8,9},{9,8},{10,11... | collective-permute-start | bytes 491528 | tf_op jit(solution)/shard_map/ppermute | solution.py:467
  196.0 1.1 collective-permute-start.35
  197.7 7.6 %collective-permute-done.35 = bf16[4,32,640]{2,1,0:T(8,128)(2,1)S(1)} collective-permute-done((bf16[4,32,640]{2,1,0:T(8,128)(2,1)S(1)}, bf16[4,32,640]{2,1,0:T(8,128)(2,1)S(1)}, u32[]{:S(2)}, u32[]{:S(2)}) %collective-permute-start.35) | collective-permute-done | bytes 163872 | tf_op jit(solution)/shard_map/ppermute | solution.py:467
  206.5 1.1 collective-permute-done.40
  207.7 17.8 %expand_update.1 = bf16[14336,512]{1,0:T(8,128)(2,1)} custom-call(s32[9]{0:T(128)S(1)} %stack.306.at_ref, bf16[512,640]{1,0:T(8,128)(2,1)S(1)} %bitcast.215, bf16[512,640]{1,0:T(8,128)(2,1)S(1)} %bitcast.216, bf16[1024,512]{1,0:T(8,128)(2,1)S(1)} %bitcast.214, bf16[1632,512]{1,0:T(8,128)(2,1)} %copy-done, bf16[1632,512]{1,0:T(8,128)(2,1)} %collective-permute-done.1.refs_1_, ...), custom_call_target="tpu_custom_call" | custom-call | flops 9395240960 | bytes 14680064 | tf_op jit(solution)/shard_map/expand_update/pallas_call | solution.py:314
  (152 shorter events, 21.8 us)
Async XLA Ops:
  2.2 4.3 %collective-permute-start = (bf16[14,40,512]{2,1,0:T(8,128)(2,1)S(1)}, bf16[14,40,512]{2,1,0:T(8,128)(2,1)S(1)}, u32[]{:S(2)}, u32[]{:S(2)}) collective-permute-start(bf16[14,40,512]{2,1,0:T(8,128)(2,1)S(1)} %constant_dynamic-update-slice_fusion.14), channel_id=1, source_target_pairs={{0,2},{2,0},{4,6},{6,4},{8,10},{10,8},{12,14},{14,12},{16,18},{18,... | collective-permute-start | bytes 1720328 | tf_op jit(solution)/shard_map/ppermute | solution.py:19
  2.7 49.1 %collective-permute-start.8 = (bf16[1,256,4096]{2,1,0:T(8,128)(2,1)}, bf16[1,256,4096]{2,1,0:T(8,128)(2,1)}, u32[]{:S(2)}, u32[]{:S(2)}) collective-permute-start(bf16[1,256,4096]{2,1,0:T(8,128)(2,1)} %bitcast.60), channel_id=1, source_target_pairs={{0,1},{1,0},{2,3},{3,2},{4,5},{5,4},{6,7},{7,6},{8,9},{9,8},{10,11... | collective-permute-start | bytes 6291464 | tf_op jit(solution)/shard_map/ppermute | solution.py:19
  8.0 55.4 %copy-start = (bf16[1632,512]{1,0:T(8,128)(2,1)}, bf16[1632,512]{1,0:T(8,128)(2,1)S(1)}, u32[]{:S(2)}) copy-start(bf16[1632,512]{1,0:T(8,128)(2,1)S(1)} %pad_maximum_fusion.refs_0_) | copy-start | bytes 5013508
  8.0 3.7 %collective-permute-start.3 = (bf16[1632,512]{1,0:T(8,128)(2,1)S(1)}, bf16[1632,512]{1,0:T(8,128)(2,1)}, u32[]{:S(2)}, u32[]{:S(2)}) collective-permute-start(bf16[1632,512]{1,0:T(8,128)(2,1)S(1)} %pad_maximum_fusion.refs_0_), channel_id=1, source_target_pairs={{0,2},{2,0},{4,6},{6,4},{8,10},{10,8},{12,14},{14,12},{16,18},{18,... | collective-permute-start | bytes 5013512 | tf_op jit(solution)/shard_map/ppermute | solution.py:19
  8.2 38.8 %collective-permute-start.2 = (bf16[1632,512]{1,0:T(8,128)(2,1)S(1)}, bf16[1632,512]{1,0:T(8,128)(2,1)S(1)}, u32[]{:S(2)}, u32[]{:S(2)}) collective-permute-start(bf16[1632,512]{1,0:T(8,128)(2,1)S(1)} %pad_maximum_fusion.refs_0_), channel_id=1, source_target_pairs={{8,0},{16,8},{24,16},{28,24},{20,28},{12,20},{4,12},{0,4},{10,2},{... | collective-permute-start | bytes 5013512 | tf_op jit(solution)/shard_map/ppermute | solution.py:543
  9.8 38.6 %collective-permute-start.1 = (bf16[1632,512]{1,0:T(8,128)(2,1)S(1)}, bf16[1632,512]{1,0:T(8,128)(2,1)}, u32[]{:S(2)}, u32[]{:S(2)}) collective-permute-start(bf16[1632,512]{1,0:T(8,128)(2,1)S(1)} %pad_maximum_fusion.refs_0_), channel_id=1, source_target_pairs={{0,8},{8,16},{16,24},{24,28},{28,20},{20,12},{12,4},{4,0},{2,10},{... | collective-permute-start | bytes 5013512 | tf_op jit(solution)/shard_map/ppermute | solution.py:543
  47.0 16.4 %copy-start.3 = (bf16[1632,512]{1,0:T(8,128)(2,1)}, bf16[1632,512]{1,0:T(8,128)(2,1)S(1)}, u32[]{:S(2)}) copy-start(bf16[1632,512]{1,0:T(8,128)(2,1)S(1)} %collective-permute-done.2.refs_2_) | copy-start | bytes 5013508
  48.3 8.4 %collective-permute-start.6 = (bf16[1632,512]{1,0:T(8,128)(2,1)}, bf16[1632,512]{1,0:T(8,128)(2,1)}, u32[]{:S(2)}, u32[]{:S(2)}) collective-permute-start(bf16[1632,512]{1,0:T(8,128)(2,1)} %collective-permute-done.1.refs_1_), channel_id=1, source_target_pairs={{0,2},{2,0},{4,6},{6,4},{8,10},{10,8},{12,14},{14,12},{16,18},{18,... | collective-permute-start | bytes 5013512 | tf_op jit(solution)/shard_map/ppermute | solution.py:19
  48.3 8.4 %collective-permute-start.7 = (bf16[1632,512]{1,0:T(8,128)(2,1)S(1)}, bf16[1632,512]{1,0:T(8,128)(2,1)}, u32[]{:S(2)}, u32[]{:S(2)}) collective-permute-start(bf16[1632,512]{1,0:T(8,128)(2,1)S(1)} %collective-permute-done.2.refs_2_), channel_id=1, source_target_pairs={{0,2},{2,0},{4,6},{6,4},{8,10},{10,8},{12,14},{14,12},{16,18},{18,... | collective-permute-start | bytes 5013512 | tf_op jit(solution)/shard_map/ppermute | solution.py:19
  48.9 38.7 %collective-permute-start.4 = (bf16[1632,512]{1,0:T(8,128)(2,1)}, bf16[1632,512]{1,0:T(8,128)(2,1)}, u32[]{:S(2)}, u32[]{:S(2)}) collective-permute-start(bf16[1632,512]{1,0:T(8,128)(2,1)} %collective-permute-done.1.refs_1_), channel_id=1, source_target_pairs={{0,8},{8,16},{16,24},{24,28},{28,20},{20,12},{12,4},{4,0},{2,10},{... | collective-permute-start | bytes 5013512 | tf_op jit(solution)/shard_map/ppermute | solution.py:543
  49.4 38.2 %collective-permute-start.5 = (bf16[1632,512]{1,0:T(8,128)(2,1)S(1)}, bf16[1632,512]{1,0:T(8,128)(2,1)}, u32[]{:S(2)}, u32[]{:S(2)}) collective-permute-start(bf16[1632,512]{1,0:T(8,128)(2,1)S(1)} %collective-permute-done.2.refs_2_), channel_id=1, source_target_pairs={{8,0},{16,8},{24,16},{28,24},{20,28},{12,20},{4,12},{0,4},{10,2},{... | collective-permute-start | bytes 5013512 | tf_op jit(solution)/shard_map/ppermute | solution.py:543
  87.6 19.1 %collective-permute-start.11 = (bf16[1632,512]{1,0:T(8,128)(2,1)}, bf16[1632,512]{1,0:T(8,128)(2,1)}, u32[]{:S(2)}, u32[]{:S(2)}) collective-permute-start(bf16[1632,512]{1,0:T(8,128)(2,1)} %collective-permute-done.4.refs_0_.refs_3_), channel_id=1, source_target_pairs={{0,2},{2,0},{4,6},{6,4},{8,10},{10,8},{12,14},{14,12},{16,18},{18,... | collective-permute-start | bytes 5013512 | tf_op jit(solution)/shard_map/ppermute | solution.py:19
  87.6 19.1 %collective-permute-start.12 = (bf16[1632,512]{1,0:T(8,128)(2,1)}, bf16[1632,512]{1,0:T(8,128)(2,1)}, u32[]{:S(2)}, u32[]{:S(2)}) collective-permute-start(bf16[1632,512]{1,0:T(8,128)(2,1)} %collective-permute-done.5.refs_1_.refs_4_), channel_id=1, source_target_pairs={{0,2},{2,0},{4,6},{6,4},{8,10},{10,8},{12,14},{14,12},{16,18},{18,... | collective-permute-start | bytes 5013512 | tf_op jit(solution)/shard_map/ppermute | solution.py:19
  88.1 38.6 %collective-permute-start.9 = (bf16[1632,512]{1,0:T(8,128)(2,1)}, bf16[1632,512]{1,0:T(8,128)(2,1)S(1)}, u32[]{:S(2)}, u32[]{:S(2)}) collective-permute-start(bf16[1632,512]{1,0:T(8,128)(2,1)} %collective-permute-done.4.refs_0_.refs_3_), channel_id=1, source_target_pairs={{0,8},{8,16},{16,24},{24,28},{28,20},{20,12},{12,4},{4,0},{2,10},{... | collective-permute-start | bytes 5013512 | tf_op jit(solution)/shard_map/ppermute | solution.py:543
  89.7 38.3 %collective-permute-start.10 = (bf16[1632,512]{1,0:T(8,128)(2,1)}, bf16[1632,512]{1,0:T(8,128)(2,1)S(1)}, u32[]{:S(2)}, u32[]{:S(2)}) collective-permute-start(bf16[1632,512]{1,0:T(8,128)(2,1)} %collective-permute-done.5.refs_1_.refs_4_), channel_id=1, source_target_pairs={{8,0},{16,8},{24,16},{28,24},{20,28},{12,20},{4,12},{0,4},{10,2},{... | collective-permute-start | bytes 5013512 | tf_op jit(solution)/shard_map/ppermute | solution.py:543
  90.1 13.6 %collective-permute-start.14 = (bf16[1,512,512]{2,1,0:T(8,128)(2,1)}, bf16[1,512,512]{2,1,0:T(8,128)(2,1)}, u32[]{:S(2)}, u32[]{:S(2)}) collective-permute-start(bf16[1,512,512]{2,1,0:T(8,128)(2,1)} %bitcast.72), channel_id=1, source_target_pairs={{0,1},{1,0},{2,3},{3,2},{4,5},{5,4},{6,7},{7,6},{8,9},{9,8},{10,11... | collective-permute-start | bytes 1572872 | tf_op jit(solution)/shard_map/ppermute | solution.py:19
  103.7 13.3 %collective-permute-start.13 = (bf16[240,256]{1,0:T(8,128)(2,1)S(1)}, bf16[240,256]{1,0:T(8,128)(2,1)S(1)}, u32[]{:S(2)}, u32[]{:S(2)}) collective-permute-start(bf16[240,256]{1,0:T(8,128)(2,1)S(1)} %convert_element_type.43), channel_id=1, source_target_pairs={{0,1},{1,0},{2,3},{3,2},{4,5},{5,4},{6,7},{7,6},{8,9},{9,8},{10,11... | collective-permute-start | bytes 368648 | tf_op jit(solution)/shard_map/ppermute | solution.py:19
  117.0 12.6 %copy-start.8 = (f32[512,256]{1,0:T(8,128)}, f32[512,256]{1,0:T(8,128)S(1)}, u32[]{:S(2)}) copy-start(f32[512,256]{1,0:T(8,128)S(1)} %add_grads.5.refs_8_) | copy-start | bytes 1572868
  117.1 12.6 %copy-start.14 = (bf16[240,256]{1,0:T(8,128)(2,1)}, bf16[240,256]{1,0:T(8,128)(2,1)S(1)}, u32[]{:S(2)}) copy-start(bf16[240,256]{1,0:T(8,128)(2,1)S(1)} %collective-permute-done.13.refs_4_) | copy-start | bytes 368644
  126.7 12.5 %copy-start.1 = (bf16[1632,512]{1,0:T(8,128)(2,1)}, bf16[1632,512]{1,0:T(8,128)(2,1)S(1)}, u32[]{:S(2)}) copy-start(bf16[1632,512]{1,0:T(8,128)(2,1)S(1)} %collective-permute-done.9.refs_0_.refs_5_) | copy-start | bytes 5013508
  128.0 11.3 %copy-start.2 = (bf16[1632,512]{1,0:T(8,128)(2,1)}, bf16[1632,512]{1,0:T(8,128)(2,1)S(1)}, u32[]{:S(2)}) copy-start(bf16[1632,512]{1,0:T(8,128)(2,1)S(1)} %collective-permute-done.10.refs_1_.refs_6_) | copy-start | bytes 5013508
  128.0 4.1 %collective-permute-start.16 = (bf16[1632,512]{1,0:T(8,128)(2,1)S(1)}, bf16[1632,512]{1,0:T(8,128)(2,1)}, u32[]{:S(2)}, u32[]{:S(2)}) collective-permute-start(bf16[1632,512]{1,0:T(8,128)(2,1)S(1)} %collective-permute-done.9.refs_0_.refs_5_), channel_id=1, source_target_pairs={{0,2},{2,0},{4,6},{6,4},{8,10},{10,8},{12,14},{14,12},{16,18},{18,... | collective-permute-start | bytes 5013512 | tf_op jit(solution)/shard_map/ppermute | solution.py:19
  128.0 6.1 %collective-permute-start.17 = (bf16[1632,512]{1,0:T(8,128)(2,1)S(1)}, bf16[1632,512]{1,0:T(8,128)(2,1)}, u32[]{:S(2)}, u32[]{:S(2)}) collective-permute-start(bf16[1632,512]{1,0:T(8,128)(2,1)S(1)} %collective-permute-done.10.refs_1_.refs_6_), channel_id=1, source_target_pairs={{0,2},{2,0},{4,6},{6,4},{8,10},{10,8},{12,14},{14,12},{16,18},{18,... | collective-permute-start | bytes 5013512 | tf_op jit(solution)/shard_map/ppermute | solution.py:19
  129.7 16.2 %collective-permute-start.15 = (bf16[1120,512]{1,0:T(8,128)(2,1)}, bf16[1120,512]{1,0:T(8,128)(2,1)}, u32[]{:S(2)}, u32[]{:S(2)}) collective-permute-start(bf16[1120,512]{1,0:T(8,128)(2,1)} %slice_select_fusion), channel_id=1, source_target_pairs={{0,8},{8,16},{16,24},{24,28},{28,20},{20,12},{12,4},{4,0},{10,2},{... | collective-permute-start | bytes 3440648 | tf_op jit(solution)/shard_map/ppermute | solution.py:558
  131.3 11.7 %collective-permute-start.18 = (bf16[160,256]{1,0:T(8,128)(2,1)S(1)}, bf16[160,256]{1,0:T(8,128)(2,1)S(1)}, u32[]{:S(2)}, u32[]{:S(2)}) collective-permute-start(bf16[160,256]{1,0:T(8,128)(2,1)S(1)} %convert_element_type.44), channel_id=1, source_target_pairs={{0,1},{1,0},{2,3},{3,2},{4,5},{5,4},{6,7},{7,6},{8,9},{9,8},{10,11... | collective-permute-start | bytes 245768 | tf_op jit(solution)/shard_map/ppermute | solution.py:19
  143.0 10.6 %copy-start.10 = (f32[512,256]{1,0:T(8,128)}, f32[512,256]{1,0:T(8,128)S(1)}, u32[]{:S(2)}) copy-start(f32[512,256]{1,0:T(8,128)S(1)} %add_grads.6.refs_4_) | copy-start | bytes 1572868
  145.8 3.0 %collective-permute-start.20 = (bf16[1120,512]{1,0:T(8,128)(2,1)}, bf16[1120,512]{1,0:T(8,128)(2,1)S(1)}, u32[]{:S(2)}, u32[]{:S(2)}) collective-permute-start(bf16[1120,512]{1,0:T(8,128)(2,1)} %collective-permute-done.15.refs_0_.refs_7_), channel_id=1, source_target_pairs={{0,2},{2,0},{4,6},{6,4},{8,10},{10,8},{12,14},{14,12},{16,18},{18,... | collective-permute-start | bytes 3440648 | tf_op jit(solution)/shard_map/ppermute | solution.py:19
  145.8 9.2 %collective-permute-start.19 = (bf16[512,512]{1,0:T(8,128)(2,1)S(1)}, bf16[512,512]{1,0:T(8,128)(2,1)S(1)}, u32[]{:S(2)}, u32[]{:S(2)}) collective-permute-start(bf16[512,512]{1,0:T(8,128)(2,1)S(1)} %slice_select_fusion.1), channel_id=1, source_target_pairs={{0,8},{8,16},{16,24},{24,28},{28,20},{20,12},{12,4},{4,0},{10,2},{... | collective-permute-start | bytes 1572872 | tf_op jit(solution)/shard_map/ppermute | solution.py:566
  147.4 6.2 %collective-permute-start.21 = (bf16[160,256]{1,0:T(8,128)(2,1)S(1)}, bf16[160,256]{1,0:T(8,128)(2,1)S(1)}, u32[]{:S(2)}, u32[]{:S(2)}) collective-permute-start(bf16[160,256]{1,0:T(8,128)(2,1)S(1)} %convert_element_type.45), channel_id=1, source_target_pairs={{0,1},{1,0},{2,3},{3,2},{4,5},{5,4},{6,7},{7,6},{8,9},{9,8},{10,11... | collective-permute-start | bytes 245768 | tf_op jit(solution)/shard_map/ppermute | solution.py:19
  155.0 1.9 collective-permute-start.22
  155.0 5.6 %collective-permute-start.23 = (bf16[80,256]{1,0:T(8,128)(2,1)S(1)}, bf16[80,256]{1,0:T(8,128)(2,1)S(1)}, u32[]{:S(2)}, u32[]{:S(2)}) collective-permute-start(bf16[80,256]{1,0:T(8,128)(2,1)S(1)} %convert_element_type.46), channel_id=1, source_target_pairs={{0,1},{1,0},{2,3},{3,2},{4,5},{5,4},{6,7},{7,6},{8,9},{9,8},{10,11... | collective-permute-start | bytes 122888 | tf_op jit(solution)/shard_map/ppermute | solution.py:19
  161.7 2.2 collective-permute-start.24
  164.2 7.4 %collective-permute-start.25 = (bf16[2,32,640]{2,1,0:T(8,128)(2,1)S(1)}, bf16[2,32,640]{2,1,0:T(8,128)(2,1)S(1)}, u32[]{:S(2)}, u32[]{:S(2)}) collective-permute-start(bf16[2,32,640]{2,1,0:T(8,128)(2,1)S(1)} %get-tuple-element.68), channel_id=1, source_target_pairs={{0,4},{2,6},{4,0},{6,2},{8,12},{10,14},{12,8},{14,10},{16,20},{18,... | collective-permute-start | bytes 245768 | tf_op jit(solution)/shard_map/ppermute | solution.py:19
  165.0 10.2 %collective-permute-start.26 = (bf16[2,32,640]{2,1,0:T(8,128)(2,1)S(1)}, bf16[2,32,640]{2,1,0:T(8,128)(2,1)S(1)}, u32[]{:S(2)}, u32[]{:S(2)}) collective-permute-start(bf16[2,32,640]{2,1,0:T(8,128)(2,1)S(1)} %get-tuple-element.69), channel_id=1, source_target_pairs={{0,8},{2,10},{4,12},{6,14},{8,0},{10,2},{12,4},{14,6},{16,24},{18,... | collective-permute-start | bytes 245768 | tf_op jit(solution)/shard_map/ppermute | solution.py:19
  167.3 10.9 %collective-permute-start.27 = (bf16[2,32,640]{2,1,0:T(8,128)(2,1)S(1)}, bf16[2,32,640]{2,1,0:T(8,128)(2,1)S(1)}, u32[]{:S(2)}, u32[]{:S(2)}) collective-permute-start(bf16[2,32,640]{2,1,0:T(8,128)(2,1)S(1)} %get-tuple-element.70), channel_id=1, source_target_pairs={{0,12},{2,14},{4,8},{6,10},{8,4},{10,6},{12,0},{14,2},{16,28},{18,... | collective-permute-start | bytes 245768 | tf_op jit(solution)/shard_map/ppermute | solution.py:19
  168.6 12.2 %collective-permute-start.28 = (bf16[2,32,640]{2,1,0:T(8,128)(2,1)S(1)}, bf16[2,32,640]{2,1,0:T(8,128)(2,1)S(1)}, u32[]{:S(2)}, u32[]{:S(2)}) collective-permute-start(bf16[2,32,640]{2,1,0:T(8,128)(2,1)S(1)} %get-tuple-element.71), channel_id=1, source_target_pairs={{0,16},{2,18},{4,20},{6,22},{8,24},{10,26},{12,28},{14,30},{16,0},... | collective-permute-start | bytes 245768 | tf_op jit(solution)/shard_map/ppermute | solution.py:19
  171.2 11.9 %collective-permute-start.29 = (bf16[2,32,640]{2,1,0:T(8,128)(2,1)S(1)}, bf16[2,32,640]{2,1,0:T(8,128)(2,1)S(1)}, u32[]{:S(2)}, u32[]{:S(2)}) collective-permute-start(bf16[2,32,640]{2,1,0:T(8,128)(2,1)S(1)} %get-tuple-element.72), channel_id=1, source_target_pairs={{0,20},{2,22},{4,16},{6,18},{8,28},{10,30},{12,24},{14,26},{16,4},... | collective-permute-start | bytes 245768 | tf_op jit(solution)/shard_map/ppermute | solution.py:19
  171.6 11.4 %collective-permute-start.30 = (bf16[2,32,640]{2,1,0:T(8,128)(2,1)S(1)}, bf16[2,32,640]{2,1,0:T(8,128)(2,1)S(1)}, u32[]{:S(2)}, u32[]{:S(2)}) collective-permute-start(bf16[2,32,640]{2,1,0:T(8,128)(2,1)S(1)} %get-tuple-element.73), channel_id=1, source_target_pairs={{0,24},{2,26},{4,28},{6,30},{8,16},{10,18},{12,20},{14,22},{16,8},... | collective-permute-start | bytes 245768 | tf_op jit(solution)/shard_map/ppermute | solution.py:19
  175.2 7.9 %collective-permute-start.31 = (bf16[2,32,640]{2,1,0:T(8,128)(2,1)S(1)}, bf16[2,32,640]{2,1,0:T(8,128)(2,1)S(1)}, u32[]{:S(2)}, u32[]{:S(2)}) collective-permute-start(bf16[2,32,640]{2,1,0:T(8,128)(2,1)S(1)} %get-tuple-element.74), channel_id=1, source_target_pairs={{0,28},{2,30},{4,24},{6,26},{8,20},{10,22},{12,16},{14,18},{16,12}... | collective-permute-start | bytes 245768 | tf_op jit(solution)/shard_map/ppermute | solution.py:19
  183.2 7.5 %collective-permute-start.34 = (bf16[32,640]{1,0:T(8,128)(2,1)S(1)}, bf16[32,640]{1,0:T(8,128)(2,1)S(1)}, u32[]{:S(2)}, u32[]{:S(2)}) collective-permute-start(bf16[32,640]{1,0:T(8,128)(2,1)S(1)} %bitcast.225), channel_id=1, source_target_pairs={{0,24},{2,26},{4,28},{6,30},{8,16},{10,18},{12,20},{14,22},{16,8},... | collective-permute-start | bytes 122888 | tf_op jit(solution)/shard_map/ppermute | solution.py:19
  186.2 5.0 %collective-permute-start.33 = (bf16[32,640]{1,0:T(8,128)(2,1)S(1)}, bf16[32,640]{1,0:T(8,128)(2,1)S(1)}, u32[]{:S(2)}, u32[]{:S(2)}) collective-permute-start(bf16[32,640]{1,0:T(8,128)(2,1)S(1)} %bitcast.226), channel_id=1, source_target_pairs={{0,16},{2,18},{4,20},{6,22},{8,24},{10,26},{12,28},{14,30},{16,0},... | collective-permute-start | bytes 122888 | tf_op jit(solution)/shard_map/ppermute | solution.py:19
  188.6 4.0 %collective-permute-start.32 = (bf16[32,640]{1,0:T(8,128)(2,1)S(1)}, bf16[32,640]{1,0:T(8,128)(2,1)S(1)}, u32[]{:S(2)}, u32[]{:S(2)}) collective-permute-start(bf16[32,640]{1,0:T(8,128)(2,1)S(1)} %bitcast.227), channel_id=1, source_target_pairs={{0,8},{2,10},{4,12},{6,14},{8,0},{10,2},{12,4},{14,6},{16,24},{18,... | collective-permute-start | bytes 122888 | tf_op jit(solution)/shard_map/ppermute | solution.py:19
  189.1 8.6 %collective-permute-start.39 = (f32[32,320]{1,0:T(8,128)S(1)}, f32[32,320]{1,0:T(8,128)S(1)}, u32[]{:S(2)}, u32[]{:S(2)}) collective-permute-start(f32[32,320]{1,0:T(8,128)S(1)} %get-tuple-element.88), channel_id=1, source_target_pairs={{0,1},{2,0},{4,3},{6,2},{8,5},{10,4},{12,7},{14,6},{16,9},{18,8},{... | collective-permute-start | bytes 122888 | tf_op jit(solution)/shard_map/ppermute | solution.py:484
  189.8 7.8 %collective-permute-start.38 = (f32[32,320]{1,0:T(8,128)S(1)}, f32[32,320]{1,0:T(8,128)S(1)}, u32[]{:S(2)}, u32[]{:S(2)}) collective-permute-start(f32[32,320]{1,0:T(8,128)S(1)} %get-tuple-element.89), channel_id=1, source_target_pairs={{0,0},{2,1},{4,2},{6,3},{8,4},{10,5},{12,6},{14,7},{16,8},{18,9},{... | collective-permute-start | bytes 122888 | tf_op jit(solution)/shard_map/ppermute | solution.py:484
  192.6 12.7 %collective-permute-start.36 = (bf16[4,32,640]{2,1,0:T(8,128)(2,1)S(1)}, bf16[4,32,640]{2,1,0:T(8,128)(2,1)S(1)}, u32[]{:S(2)}, u32[]{:S(2)}) collective-permute-start(bf16[4,32,640]{2,1,0:T(8,128)(2,1)S(1)} %get-tuple-element.87), channel_id=1, source_target_pairs={{0,1},{1,0},{2,3},{3,2},{4,5},{5,4},{6,7},{7,6},{8,9},{9,8},{10,11... | collective-permute-start | bytes 491528 | tf_op jit(solution)/shard_map/ppermute | solution.py:467
  196.0 9.2 %collective-permute-start.35 = (bf16[4,32,640]{2,1,0:T(8,128)(2,1)S(1)}, bf16[4,32,640]{2,1,0:T(8,128)(2,1)S(1)}, u32[]{:S(2)}, u32[]{:S(2)}) collective-permute-start(bf16[4,32,640]{2,1,0:T(8,128)(2,1)S(1)} %get-tuple-element.87), channel_id=1, source_target_pairs={{0,4},{1,5},{2,6},{3,7},{4,0},{5,1},{6,2},{7,3},{8,12},{9,13},{10,... | collective-permute-start | bytes 491528 | tf_op jit(solution)/shard_map/ppermute | solution.py:467
  197.1 8.2 %collective-permute-start.37 = (bf16[4,32,640]{2,1,0:T(8,128)(2,1)S(1)}, bf16[4,32,640]{2,1,0:T(8,128)(2,1)S(1)}, u32[]{:S(2)}, u32[]{:S(2)}) collective-permute-start(bf16[4,32,640]{2,1,0:T(8,128)(2,1)S(1)} %get-tuple-element.87), channel_id=1, source_target_pairs={{0,5},{1,4},{2,7},{3,6},{4,1},{5,0},{6,3},{7,2},{8,13},{9,12},{10,... | collective-permute-start | bytes 491528 | tf_op jit(solution)/shard_map/ppermute | solution.py:467
  205.4 2.2 collective-permute-start.40
  (13 other events, 59.7 us)

commit v4 on v3

--- a/solution.py
+++ b/solution.py
@@ -403,9 +403,11 @@
 def token_sums(grad_proj_t, sums, gots, order, pair_rows):
     blocks, width, tokens = grad_proj_t.shape
     pairs = blocks // 2
-    rows = pairs * pair_rows
+    top = lax.axis_size("dp") // blocks
+    assert top == 2
+    rows = len(order) * pair_rows
     order = jnp.stack(order).astype(jnp.int32)
-    me = lax.axis_index("dp")
+    me = lax.axis_index("dp") % blocks
     whole = pl.BlockSpec(memory_space=pltpu.VMEM)
     if width % 16 == 0 and pair_rows % 16 == 0 and gots:
         params = pltpu.CompilerParams(vmem_limit_bytes=VMEM_BYTES)
@@ -452,20 +454,14 @@
     total = ours[0].astype(F32)
     for r in range(1, pairs):
         total += flip(ours[r], "dp", 2 * r).astype(F32)
+    total += flip(total.astype(BF16), "dp", blocks).astype(F32)
     return total[0], total[1]
 
 
 def gather_scaled(scaled, diag):
-    pairs, n_mp = lax.axis_size("dp") // 2, lax.axis_size("mp")
-    x = jnp.stack([scaled] + [flip(scaled, "dp", 2 * r) for r in range(2, pairs, 2)])
-    parts = {}
-    for m in range(n_mp):
-        for low in range(2):
-            hops = []
-            for i in range(2 * pairs):
-                hops += [(i * n_mp + k, (i ^ (2 * low)) * n_mp + (k ^ m)) for k in range(n_mp)]
-            parts[m, low] = lax.ppermute(x, ("dp", "mp"), hops) if m or low else x
-    x = jnp.stack([jnp.stack([parts[m, 0], parts[m, 1]], axis=1) for m in range(n_mp)])
+    pairs = lax.axis_size("dp") // 4
+    x = gather_near_first(scaled, "mp")
+    x = jnp.stack([x] + [flip(x, "dp", 2 * r) for r in range(1, pairs)])
     x, diag = lax.optimization_barrier((x, diag))
     return x, flip(x, "dp", 1), diag
 
@@ -473,17 +469,21 @@
 def place_diag(diag_t):
     n_dp, n_mp = lax.axis_size("dp"), lax.axis_size("mp")
     width, rows = diag_t.shape[0], diag_t.shape[1] // n_mp
-    here, block = lax.axis_index("mp"), lax.axis_index("mp") * n_dp + lax.axis_index("dp")
-    out = jnp.zeros((n_mp, width, rows), diag_t.dtype)
-    for k in range(n_mp):
-        pairs = []
-        for b in range(n_mp * n_dp):
-            pairs.append(((b % n_dp) * n_mp + b // n_dp, (b // n_mp) * n_mp + (b + k) % n_mp))
-        target = (block + k) % n_mp
+    share, blocks = n_mp // 2, n_dp // 2
+    here, me = lax.axis_index("mp"), lax.axis_index("dp")
+    block = here * blocks + me % blocks
+    out = jnp.zeros((share, width, rows), diag_t.dtype)
+    for k in range(share):
+        hops = []
+        for m in range(n_mp):
+            for i in range(n_dp):
+                b = m * blocks + i % blocks
+                hops.append((i * n_mp + m, (b // share) * n_mp + 2 * ((b + k) % share) + i // blocks))
+        target = 2 * ((block + k) % share) + me // blocks
         sent = lax.dynamic_slice(diag_t, (0, target * rows), (width, rows))
-        got = lax.ppermute(sent, ("dp", "mp"), pairs)
-        out = lax.dynamic_update_slice(out, got[None], ((here - k) % n_mp, 0, 0))
-    return out.reshape((n_mp * width, rows)).T
+        got = lax.ppermute(sent, ("dp", "mp"), hops)
+        out = lax.dynamic_update_slice(out, got[None], ((here // 2 - k) % share, 0, 0))
+    return out.reshape((share * width, rows)).T
 
 
 def on_device(acts, grads, basis_in, basis_out, damping):
@@ -515,8 +515,7 @@
     wide_grads = gather_doubling(grads, "mp")
 
     ahead, back_hops = ring_hops(n_dp)
-    everyone = (ahead[0] + ahead[1], back_hops[0] + back_hops[1])
-    last_hops = ahead[0] + back_hops[1]
+    everyone = (ahead[0] + back_hops[1], back_hops[0] + ahead[1])
     began = ring_place("dp")
     grad_proj_t = jnp.zeros((directions, tok_rows), F32)
     owns, others, pairs, sums, gots = [], [], [], [], []
@@ -528,7 +527,8 @@
         grad_proj_t = add_grads(pieces, origins, wide_grads, grad_proj_t, n_dp)
 
     def use(pieces, where_from, grads_too=True, costed=False, known=()):
-        swapped = list(known) + [flip(piece, "dp", 1) for piece in pieces[len(known) :]]
+        fresh = [flip(piece, "dp", 1) for piece in pieces[len(known) :]]
+        swapped = list(known) + fresh[::-1]
         sums.append(project(pieces, swapped, rows, core, acts, costed))
         gots.append([flip(sums[-1].astype(BF16), "mp", 1)] if n_mp == 2 else [])
         owns.extend(pieces)
@@ -553,17 +553,16 @@
             waiting = [], []
         if step == min(2, half // 2 - 1):
             rows_near = gather_near_first(rows_near, "mp")
-        waiting = waiting[0] + moving, waiting[1] + [began(step), began(-step)]
-
-    last = lax.ppermute(
-        jnp.where(core == 0, moving[0][:in_rows], moving[1][:in_rows]), "dp", last_hops
-    )
-    held = jnp.where(core == 0, moving[0][in_rows:], moving[1][in_rows:])
+        way = (1 - 2 * core) * step
+        waiting = waiting[0] + moving, waiting[1] + [began(way), began(-way)]
+
+    last = lax.ppermute(moving[0][:in_rows], "dp", everyone[0])
+    held = moving[0][in_rows:]
     use(*waiting)
     held, last, sums[-1], gots[:-1], grad_proj_t = lax.optimization_barrier(
         (held, last, sums[-1], gots[:-1], grad_proj_t)
     )
-    last_out = lax.ppermute(held, "dp", last_hops)
+    last_out = lax.ppermute(held, "dp", everyone[0])
     last_pair = began(half // 2)
     use([last], [last_pair], False, True)
     last_out, sums[-1], gots[:-1] = lax.optimization_barrier((last_out, sums[-1], gots[:-1]))
@@ -575,12 +574,12 @@
         n_dp,
     )
 
-    rows_near = rows_near.reshape((n_mp, half, 2, width, out_units))
-    rows_near = near_first(near_first(rows_near, 1, me // 2), 2, core)
-    rows_near = rows_near.transpose(2, 0, 1, 3, 4).reshape((n_mp * directions, out_units))
+    rows_near = rows_near.reshape((n_mp, half // 2, 2, 2 * width, out_units))
+    rows_near = near_first(near_first(rows_near, 1, (me // 2) % (half // 2)), 2, core)
+    rows_near = rows_near.transpose(2, 1, 0, 3, 4).reshape((n_mp * directions, out_units))
 
     rotated, squares = token_sums(
-        grad_proj_t.reshape((n_dp, width, tok_rows)), sums, [got for part in gots for got in part], pairs, rows
+        grad_proj_t.reshape((half, 2 * width, tok_rows)), sums, [got for part in gots for got in part], pairs, rows
     )
     diag_t = squares / tokens_all
     scaled = (rotated / (diag_t + damping[0])).astype(BF16)

time: 226 us -> 221 us (0.978)
  starting transfers between devices: 41.5 us -> 27.5 us
  waiting for transfers between devices: 105 us -> 112 us
  local copies, waits for them, and re-layouts: 6.07 us -> 9.05 us
  other arithmetic: 13.8 us -> 11.2 us
    ppermute x28 -> x26, waiting for transfers between devices: 27.6 us -> 45.7 us  [flip(): return lax.ppermute(x, axis_name, [(i, i ^ bit) for i in range(size)])]
    ppermute x7 -> x3, waiting for transfers between devices: 11.8 us -> 3.74 us  [the longest x1 2.32 us: on_device(): last = lax.ppermute(moving[0][:in_rows], 'dp', everyone[0])]
    ppermute x28 -> x26, starting transfers between devices: 25.7 us -> 18.4 us  [flip(): return lax.ppermute(x, axis_name, [(i, i ^ bit) for i in range(size)])]
    ppermute x7 -> x3, starting transfers between devices: 9.74 us -> 3 us  [the longest x1 1.06 us: on_device(): last = lax.ppermute(moving[0][:in_rows], 'dp', everyone[0])]
    ppermute x6, waiting for transfers between devices: 66 us -> 62.4 us  [on_device(): moving = [lax.ppermute(x, 'dp', everyone[k]) for k, x in enumerate(moving)]]
    select_n x4 -> x2, other arithmetic: 2.72 us -> 0.44 us  [near_first(): x = jnp.where((me >> k) % 2 == 1, swapped, parts).reshape(x.shape)]
    unnamed x67 -> x66, local copies, waits for them, and re-layouts: 3.75 us -> 5.83 us
  transfers between devices with their start and end apart: 41 -> 35, of which waited for: 20 -> 23; matrix products, arithmetic and copies ran while one was open for 7% -> 6% of each run, Pallas kernels for 17% -> 17%
where the time goes in v4:
time: 221 us; the launch traced here: 219 us
  waiting for transfers between devices  112 us (51%)
  Pallas kernels  57.7 us (26%)
  starting transfers between devices  27.5 us (12%)
  other arithmetic  11.2 us (5%)
  local copies, waits for them, and re-layouts  9.05 us (4%)
    ppermute x6, waiting for transfers between devices, on_device(): moving = [lax.ppermute(x, 'dp', everyone[k]) for k, x in enumerate(moving)]  62.4 us
    ppermute x26, waiting for transfers between devices, flip(): return lax.ppermute(x, axis_name, [(i, i ^ bit) for i in range(size)])  45.7 us
    pallas_call x4, Pallas kernels, project(): pl.pallas_call(functools.partial(project_kernel, tiles, rows), grid_spec=...  22 us
    ppermute x26, starting transfers between devices, flip(): return lax.ppermute(x, axis_name, [(i, i ^ bit) for i in range(size)])  18.4 us
    pallas_call x1, Pallas kernels, expand(): pl.pallas_call(functools.partial(expand_kernel, tiles, rows), grid_spec=p...  17.8 us
    pallas_call x4, Pallas kernels, add_grads(): pl.pallas_call(add_grads_kernel, grid_spec=pltpu.PrefetchScalarGridSpec(n...  16.1 us
    ppermute x6, starting transfers between devices, on_device(): moving = [lax.ppermute(x, 'dp', everyone[k]) for k, x in enumerate(moving)]  6.08 us
    unnamed x66, local copies, waits for them, and re-layouts  5.83 us
  transfers between devices with their start and end apart: 35, of which 23 were waited for; matrix products, arithmetic and copies ran while one was open for 6% of the time, Pallas kernels for 17%

profile of v4, /device:TPU:0, one launch (start us, length us, event | category | flops | bytes accessed | tf_op | source)
XLA Modules:
  0.0 219.3 jit_solution(2327389224256205093)
XLA Ops:
  0.7 1.4 dynamic-slice_bitcast_fusion.1
  2.7 2.6 %collective-permute-start.8 = (bf16[1,256,4096]{2,1,0:T(8,128)(2,1)}, bf16[1,256,4096]{2,1,0:T(8,128)(2,1)}, u32[]{:S(2)}, u32[]{:S(2)}) collective-permute-start(bf16[1,256,4096]{2,1,0:T(8,128)(2,1)} %bitcast.60), channel_id=1, source_target_pairs={{0,1},{1,0},{2,3},{3,2},{4,5},{5,4},{6,7},{7,6},{8,9},{9,8},{10,11... | collective-permute-start | bytes 6291464 | tf_op jit(solution)/shard_map/ppermute | solution.py:19
  5.3 1.0 copy.8
  6.8 1.2 pad_maximum_fusion.refs_0_
  8.2 1.5 collective-permute-start.2
  10.3 1.5 collective-permute-done.3.refs_3_.refs_8_
  11.8 35.2 %collective-permute-done.2.refs_2_ = bf16[1632,512]{1,0:T(8,128)(2,1)S(1)} collective-permute-done((bf16[1632,512]{1,0:T(8,128)(2,1)S(1)}, bf16[1632,512]{1,0:T(8,128)(2,1)S(1)}, u32[]{:S(2)}, u32[]{:S(2)}) %collective-permute-start.2) | collective-permute-done | bytes 1671200 | tf_op jit(solution)/shard_map/ppermute | solution.py:543
  47.8 1.6 collective-permute-start.4
  50.0 1.9 collective-permute-done.8
  51.8 2.5 %select_bitcast_fusion.1 = (bf16[1,1,256,4096]{3,2,1,0:T(8,128)(2,1)S(1)}, bf16[1,1,256,4096]{3,2,1,0:T(8,128)(2,1)S(1)}) fusion(bf16[1,256,4096]{2,1,0:T(8,128)(2,1)} %collective-permute-done.8, pred[]{:T(512)S(6)} %eq.57, bf16[256,4096]{1,0:T(8,128)(2,1)} %param.6), kind=kLoop, calls=%fused_computation.2 | loop fusion | flops 2097152 | bytes 8388609 | tf_op jit(solution)/shard_map/stack | solution.py:36
  54.3 2.4 %maximum_bitcast_fusion.refs_6_.refs_7_.refs_8_.refs_9_.refs_10_.refs_11_.refs_4_.refs_5_.refs_2_.refs_3_ = bf16[2,256,4096]{2,1,0:T(8,128)(2,1)} fusion(bf16[1,1,256,4096]{3,2,1,0:T(8,128)(2,1)S(1)} %get-tuple-element.71, bf16[1,1,256,4096]{3,2,1,0:T(8,128)(2,1)S(1)} %get-tuple-element.70), kind=kLoop, calls=%fused_computation | loop fusion | flops 2097152 | bytes 8388608 | tf_op jit(solution)/shard_map/reshape | solution.py:36
  56.7 5.9 %project_acts.4.refs_0_ = f32[240,256]{1,0:T(8,128)S(1)} custom-call(s32[1]{0:T(128)} %bitcast.at_ref, bf16[256,14336]{1,0:T(8,128)(2,1)} %acts_ref.7, bf16[1632,512]{1,0:T(8,128)(2,1)S(1)} %pad_maximum_fusion.refs_0_, bf16[1632,512]{1,0:T(8,128)(2,1)} %collective-permute-done.1.refs_1_, bf16[1632,512]{1,0:T(8,128)(2,1)S(1)} %collective-permute-done.2.refs_2_, ...), custom_call_target="tpu_custom_call" | custom-call | flops 1 | bytes 1 | tf_op jit(solution)/shard_map/project_acts/pallas_call | solution.py:123
  63.4 5.0 %add_grads.4.refs_8_ = f32[512,256]{1,0:T(8,128)S(1)} custom-call(s32[12]{0:T(128)S(1)} %stack.332.at_ref, bf16[1632,512]{1,0:T(8,128)(2,1)S(1)} %pad_maximum_fusion.refs_0_, bf16[1632,512]{1,0:T(8,128)(2,1)} %collective-permute-done.1.refs_1_, bf16[1632,512]{1,0:T(8,128)(2,1)S(1)} %collective-permute-done.2.refs_2_, ...), custom_call_target="tpu_custom_call" | custom-call | flops 1 | bytes 1 | tf_op jit(solution)/shard_map/add_grads/pallas_call | solution.py:179
  69.2 18.3 %collective-permute-done.4.refs_0_.refs_3_ = bf16[1632,512]{1,0:T(8,128)(2,1)} collective-permute-done((bf16[1632,512]{1,0:T(8,128)(2,1)}, bf16[1632,512]{1,0:T(8,128)(2,1)}, u32[]{:S(2)}, u32[]{:S(2)}) %collective-permute-start.4) | collective-permute-done | bytes 1671200 | tf_op jit(solution)/shard_map/ppermute | solution.py:543
  88.0 1.1 collective-permute-start.9
  91.7 12.0 %collective-permute-done.14 = bf16[1,512,512]{2,1,0:T(8,128)(2,1)} collective-permute-done((bf16[1,512,512]{2,1,0:T(8,128)(2,1)}, bf16[1,512,512]{2,1,0:T(8,128)(2,1)}, u32[]{:S(2)}, u32[]{:S(2)}) %collective-permute-start.14) | collective-permute-done | bytes 524320 | tf_op jit(solution)/shard_map/ppermute | solution.py:19
  104.4 2.3 %pad_maximum_fusion.2 = bf16[2,512,512]{2,1,0:T(8,128)(2,1)} fusion(bf16[1,512,512]{2,1,0:T(8,128)(2,1)} %collective-permute-done.14, bf16[1,512,512]{2,1,0:T(8,128)(2,1)} %bitcast.72), kind=kLoop, calls=%fused_computation.9 | loop fusion | flops 524288 | bytes 2097152 | tf_op jit(solution)/shard_map/concatenate | solution.py:345
  106.7 6.2 %project_acts.5.refs_1_ = f32[160,256]{1,0:T(8,128)S(1)} custom-call(s32[1]{0:T(128)} %bitcast.at_ref, bf16[256,14336]{1,0:T(8,128)(2,1)} %acts_ref.7, bf16[1632,512]{1,0:T(8,128)(2,1)} %collective-permute-done.4.refs_0_.refs_3_, bf16[1632,512]{1,0:T(8,128)(2,1)} %collective-permute-done.5.refs_1_.refs_4_, ...), custom_call_target="tpu_custom_call" | custom-call | flops 1 | bytes 1 | tf_op jit(solution)/shard_map/project_acts/pallas_call | solution.py:123
  112.9 4.4 %add_grads.5.refs_8_ = f32[512,256]{1,0:T(8,128)S(1)} custom-call(s32[8]{0:T(128)S(1)} %stack.344.at_ref, bf16[1632,512]{1,0:T(8,128)(2,1)} %collective-permute-done.4.refs_0_.refs_3_, bf16[1632,512]{1,0:T(8,128)(2,1)} %collective-permute-done.5.refs_1_.refs_4_, bf16[1632,512]{1,0:T(8,128)(2,1)S(1)} %collective-permute-done.11.refs_2_.refs_11_, ...), custom_call_target="tpu_custom_call" | custom-call | flops 1 | bytes 1 | tf_op jit(solution)/shard_map/add_grads/pallas_call | solution.py:179
  118.7 8.7 %collective-permute-done.9.refs_0_.refs_5_ = bf16[1632,512]{1,0:T(8,128)(2,1)S(1)} collective-permute-done((bf16[1632,512]{1,0:T(8,128)(2,1)}, bf16[1632,512]{1,0:T(8,128)(2,1)S(1)}, u32[]{:S(2)}, u32[]{:S(2)}) %collective-permute-start.9) | collective-permute-done | bytes 1671200 | tf_op jit(solution)/shard_map/ppermute | solution.py:543
  128.0 1.1 slice.125
  129.0 1.1 collective-permute-start.15
  133.5 5.2 %project_acts.6.refs_2_ = f32[160,256]{1,0:T(8,128)S(1)} custom-call(s32[1]{0:T(128)} %bitcast.at_ref, bf16[256,14336]{1,0:T(8,128)(2,1)} %acts_ref.7, bf16[1632,512]{1,0:T(8,128)(2,1)S(1)} %collective-permute-done.9.refs_0_.refs_5_, bf16[1632,512]{1,0:T(8,128)(2,1)} %collective-permute-done.10.refs_1_.refs_6_, ...), custom_call_target="tpu_custom_call" | custom-call | flops 1 | bytes 1 | tf_op jit(solution)/shard_map/project_acts/pallas_call | solution.py:123
  138.8 4.1 %add_grads.6.refs_4_ = f32[512,256]{1,0:T(8,128)S(1)} custom-call(s32[8]{0:T(128)S(1)} %stack.353.at_ref, bf16[1632,512]{1,0:T(8,128)(2,1)S(1)} %collective-permute-done.9.refs_0_.refs_5_, bf16[1632,512]{1,0:T(8,128)(2,1)} %collective-permute-done.10.refs_1_.refs_6_, bf16[1632,512]{1,0:T(8,128)(2,1)S(1)} %collective-permute-done.16.refs_2_.refs_13_, ...), custom_call_target="tpu_custom_call" | custom-call | flops 1 | bytes 1 | tf_op jit(solution)/shard_map/add_grads/pallas_call | solution.py:179
  142.9 2.3 %collective-permute-done.15.refs_0_.refs_7_ = bf16[1120,512]{1,0:T(8,128)(2,1)} collective-permute-done((bf16[1120,512]{1,0:T(8,128)(2,1)}, bf16[1120,512]{1,0:T(8,128)(2,1)}, u32[]{:S(2)}, u32[]{:S(2)}) %collective-permute-start.15) | collective-permute-done | bytes 1146912 | tf_op jit(solution)/shard_map/ppermute | solution.py:559
  145.2 1.1 collective-permute-start.19
  147.0 1.2 collective-permute-done.20.refs_1_.refs_15_
  148.2 4.7 %project_acts.7.refs_3_ = f32[80,256]{1,0:T(8,128)S(1)} custom-call(s32[1]{0:T(128)} %bitcast.at_ref, bf16[256,14336]{1,0:T(8,128)(2,1)} %acts_ref.7, bf16[1120,512]{1,0:T(8,128)(2,1)} %collective-permute-done.15.refs_0_.refs_7_, bf16[1120,512]{1,0:T(8,128)(2,1)S(1)} %collective-permute-done.20.refs_1_.refs_15_), custom_call_target="tpu_custom_call" | custom-call | flops 587202560 | bytes 9633792 | tf_op jit(solution)/shard_map/project_acts/pallas_call | solution.py:123
  153.0 1.4 collective-permute-done.19.refs_0_
  155.2 1.1 collective-permute-done.22.refs_1_
  156.3 1.0 copy-done.12
  157.3 2.6 %add_grads.7 = f32[512,256]{1,0:T(8,128)S(1)} custom-call(s32[4]{0:T(128)S(1)} %pad_add_fusion.at_ref, bf16[512,512]{1,0:T(8,128)(2,1)S(1)} %collective-permute-done.19.refs_0_, bf16[512,512]{1,0:T(8,128)(2,1)S(1)} %collective-permute-done.22.refs_1_, ...), custom_call_target="tpu_custom_call" | custom-call | flops 1 | bytes 1 | tf_op jit(solution)/shard_map/add_grads/pallas_call | solution.py:179
  160.0 1.4 sums_for_other_core.1
  161.6 2.0 collective-permute-done.24.got_ref
  164.0 1.2 collective-permute-start.25
  165.2 1.4 collective-permute-start.26
  167.5 2.7 %collective-permute-done.25 = bf16[2,64,640]{2,1,0:T(8,128)(2,1)S(1)} collective-permute-done((bf16[2,64,640]{2,1,0:T(8,128)(2,1)S(1)}, bf16[2,64,640]{2,1,0:T(8,128)(2,1)S(1)}, u32[]{:S(2)}, u32[]{:S(2)}) %collective-permute-start.25) | collective-permute-done | bytes 163872 | tf_op jit(solution)/shard_map/ppermute | solution.py:19
  170.3 2.0 collective-permute-done.26
  172.2 2.7 %collective-permute-done.27 = bf16[2,64,640]{2,1,0:T(8,128)(2,1)S(1)} collective-permute-done((bf16[2,64,640]{2,1,0:T(8,128)(2,1)S(1)}, bf16[2,64,640]{2,1,0:T(8,128)(2,1)S(1)}, u32[]{:S(2)}, u32[]{:S(2)}) %collective-permute-start.27) | collective-permute-done | bytes 163872 | tf_op jit(solution)/shard_map/ppermute | solution.py:19
  175.0 2.1 collective-permute-start.28
  177.8 6.8 %collective-permute-done.28 = bf16[2,64,640]{2,1,0:T(8,128)(2,1)S(1)} collective-permute-done((bf16[2,64,640]{2,1,0:T(8,128)(2,1)S(1)}, bf16[2,64,640]{2,1,0:T(8,128)(2,1)S(1)}, u32[]{:S(2)}, u32[]{:S(2)}) %collective-permute-start.28) | collective-permute-done | bytes 163872 | tf_op jit(solution)/shard_map/ppermute | solution.py:19
  185.4 3.9 %collective-permute-done.29 = bf16[1,64,640]{2,1,0:T(8,128)(2,1)S(1)} collective-permute-done((bf16[1,64,640]{2,1,0:T(8,128)(2,1)S(1)}, bf16[1,64,640]{2,1,0:T(8,128)(2,1)S(1)}, u32[]{:S(2)}, u32[]{:S(2)}) %collective-permute-start.29) | collective-permute-done | bytes 81952 | tf_op jit(solution)/shard_map/ppermute | solution.py:19
  189.4 1.3 collective-permute-start.30
  190.6 2.2 %collective-permute-start.32 = (bf16[2,64,640]{2,1,0:T(8,128)(2,1)S(1)}, bf16[2,64,640]{2,1,0:T(8,128)(2,1)S(1)}, u32[]{:S(2)}, u32[]{:S(2)}) collective-permute-start(bf16[2,64,640]{2,1,0:T(8,128)(2,1)S(1)} %get-tuple-element.79), channel_id=1, source_target_pairs={{0,12},{2,14},{4,8},{6,10},{8,4},{10,6},{12,0},{14,2},{16,28},{18,... | collective-permute-start | bytes 491528 | tf_op jit(solution)/shard_map/ppermute | solution.py:19
  193.9 1.6 collective-permute-done.31
  195.7 2.8 %collective-permute-done.32 = bf16[2,64,640]{2,1,0:T(8,128)(2,1)S(1)} collective-permute-done((bf16[2,64,640]{2,1,0:T(8,128)(2,1)S(1)}, bf16[2,64,640]{2,1,0:T(8,128)(2,1)S(1)}, u32[]{:S(2)}, u32[]{:S(2)}) %collective-permute-start.32) | collective-permute-done | bytes 163872 | tf_op jit(solution)/shard_map/ppermute | solution.py:19
  199.5 1.3 collective-permute-done.34
  200.8 17.8 %expand_update.1 = bf16[14336,512]{1,0:T(8,128)(2,1)} custom-call(s32[9]{0:T(128)S(1)} %stack.281.at_ref, bf16[512,640]{1,0:T(8,128)(2,1)S(1)} %bitcast.199, bf16[512,640]{1,0:T(8,128)(2,1)S(1)} %bitcast.200, bf16[1024,512]{1,0:T(8,128)(2,1)S(1)} %bitcast.198, bf16[1632,512]{1,0:T(8,128)(2,1)} %copy-done, bf16[1632,512]{1,0:T(8,128)(2,1)} %collective-permute-done.1.refs_1_, ...), custom_call_target="tpu_custom_call" | custom-call | flops 9395240960 | bytes 14680064 | tf_op jit(solution)/shard_map/expand_update/pallas_call | solution.py:314
  (132 shorter events, 20.6 us)
Async XLA Ops:
  0.7 4.7 %copy-start.18 = (bf16[512,512]{1,0:T(8,128)(2,1)S(1)}, bf16[512,512]{1,0:T(8,128)(2,1)}, u32[]{:S(2)}) copy-start(bf16[512,512]{1,0:T(8,128)(2,1)} %param.8) | copy-start | bytes 1572868
  2.2 4.3 %collective-permute-start = (bf16[14,40,512]{2,1,0:T(8,128)(2,1)S(1)}, bf16[14,40,512]{2,1,0:T(8,128)(2,1)S(1)}, u32[]{:S(2)}, u32[]{:S(2)}) collective-permute-start(bf16[14,40,512]{2,1,0:T(8,128)(2,1)S(1)} %constant_dynamic-update-slice_fusion.14), channel_id=1, source_target_pairs={{0,2},{2,0},{4,6},{6,4},{8,10},{10,8},{12,14},{14,12},{16,18},{18,... | collective-permute-start | bytes 1720328 | tf_op jit(solution)/shard_map/ppermute | solution.py:19
  2.7 49.1 %collective-permute-start.8 = (bf16[1,256,4096]{2,1,0:T(8,128)(2,1)}, bf16[1,256,4096]{2,1,0:T(8,128)(2,1)}, u32[]{:S(2)}, u32[]{:S(2)}) collective-permute-start(bf16[1,256,4096]{2,1,0:T(8,128)(2,1)} %bitcast.60), channel_id=1, source_target_pairs={{0,1},{1,0},{2,3},{3,2},{4,5},{5,4},{6,7},{7,6},{8,9},{9,8},{10,11... | collective-permute-start | bytes 6291464 | tf_op jit(solution)/shard_map/ppermute | solution.py:19
  8.0 55.4 %copy-start = (bf16[1632,512]{1,0:T(8,128)(2,1)}, bf16[1632,512]{1,0:T(8,128)(2,1)S(1)}, u32[]{:S(2)}) copy-start(bf16[1632,512]{1,0:T(8,128)(2,1)S(1)} %pad_maximum_fusion.refs_0_) | copy-start | bytes 5013508
  8.0 3.7 %collective-permute-start.3 = (bf16[1632,512]{1,0:T(8,128)(2,1)S(1)}, bf16[1632,512]{1,0:T(8,128)(2,1)}, u32[]{:S(2)}, u32[]{:S(2)}) collective-permute-start(bf16[1632,512]{1,0:T(8,128)(2,1)S(1)} %pad_maximum_fusion.refs_0_), channel_id=1, source_target_pairs={{0,2},{2,0},{4,6},{6,4},{8,10},{10,8},{12,14},{14,12},{16,18},{18,... | collective-permute-start | bytes 5013512 | tf_op jit(solution)/shard_map/ppermute | solution.py:19
  8.2 38.8 %collective-permute-start.2 = (bf16[1632,512]{1,0:T(8,128)(2,1)S(1)}, bf16[1632,512]{1,0:T(8,128)(2,1)S(1)}, u32[]{:S(2)}, u32[]{:S(2)}) collective-permute-start(bf16[1632,512]{1,0:T(8,128)(2,1)S(1)} %pad_maximum_fusion.refs_0_), channel_id=1, source_target_pairs={{8,0},{16,8},{24,16},{28,24},{20,28},{12,20},{4,12},{0,4},{2,10},{... | collective-permute-start | bytes 5013512 | tf_op jit(solution)/shard_map/ppermute | solution.py:543
  9.8 37.3 %collective-permute-start.1 = (bf16[1632,512]{1,0:T(8,128)(2,1)S(1)}, bf16[1632,512]{1,0:T(8,128)(2,1)}, u32[]{:S(2)}, u32[]{:S(2)}) collective-permute-start(bf16[1632,512]{1,0:T(8,128)(2,1)S(1)} %pad_maximum_fusion.refs_0_), channel_id=1, source_target_pairs={{0,8},{8,16},{16,24},{24,28},{28,20},{20,12},{12,4},{4,0},{10,2},{... | collective-permute-start | bytes 5013512 | tf_op jit(solution)/shard_map/ppermute | solution.py:543
  47.0 16.4 %copy-start.2 = (bf16[1632,512]{1,0:T(8,128)(2,1)}, bf16[1632,512]{1,0:T(8,128)(2,1)S(1)}, u32[]{:S(2)}) copy-start(bf16[1632,512]{1,0:T(8,128)(2,1)S(1)} %collective-permute-done.2.refs_2_) | copy-start | bytes 5013508
  47.1 9.6 %collective-permute-start.7 = (bf16[1632,512]{1,0:T(8,128)(2,1)}, bf16[1632,512]{1,0:T(8,128)(2,1)}, u32[]{:S(2)}, u32[]{:S(2)}) collective-permute-start(bf16[1632,512]{1,0:T(8,128)(2,1)} %collective-permute-done.1.refs_1_), channel_id=1, source_target_pairs={{0,2},{2,0},{4,6},{6,4},{8,10},{10,8},{12,14},{14,12},{16,18},{18,... | collective-permute-start | bytes 5013512 | tf_op jit(solution)/shard_map/ppermute | solution.py:19
  47.8 8.9 %collective-permute-start.6 = (bf16[1632,512]{1,0:T(8,128)(2,1)S(1)}, bf16[1632,512]{1,0:T(8,128)(2,1)}, u32[]{:S(2)}, u32[]{:S(2)}) collective-permute-start(bf16[1632,512]{1,0:T(8,128)(2,1)S(1)} %collective-permute-done.2.refs_2_), channel_id=1, source_target_pairs={{0,2},{2,0},{4,6},{6,4},{8,10},{10,8},{12,14},{14,12},{16,18},{18,... | collective-permute-start | bytes 5013512 | tf_op jit(solution)/shard_map/ppermute | solution.py:19
  47.8 39.7 %collective-permute-start.4 = (bf16[1632,512]{1,0:T(8,128)(2,1)}, bf16[1632,512]{1,0:T(8,128)(2,1)}, u32[]{:S(2)}, u32[]{:S(2)}) collective-permute-start(bf16[1632,512]{1,0:T(8,128)(2,1)} %collective-permute-done.1.refs_1_), channel_id=1, source_target_pairs={{0,8},{8,16},{16,24},{24,28},{28,20},{20,12},{12,4},{4,0},{10,2},{... | collective-permute-start | bytes 5013512 | tf_op jit(solution)/shard_map/ppermute | solution.py:543
  49.4 38.1 %collective-permute-start.5 = (bf16[1632,512]{1,0:T(8,128)(2,1)S(1)}, bf16[1632,512]{1,0:T(8,128)(2,1)}, u32[]{:S(2)}, u32[]{:S(2)}) collective-permute-start(bf16[1632,512]{1,0:T(8,128)(2,1)S(1)} %collective-permute-done.2.refs_2_), channel_id=1, source_target_pairs={{8,0},{16,8},{24,16},{28,24},{20,28},{12,20},{4,12},{0,4},{2,10},{... | collective-permute-start | bytes 5013512 | tf_op jit(solution)/shard_map/ppermute | solution.py:543
  87.5 19.1 %collective-permute-start.12 = (bf16[1632,512]{1,0:T(8,128)(2,1)}, bf16[1632,512]{1,0:T(8,128)(2,1)}, u32[]{:S(2)}, u32[]{:S(2)}) collective-permute-start(bf16[1632,512]{1,0:T(8,128)(2,1)} %collective-permute-done.4.refs_0_.refs_3_), channel_id=1, source_target_pairs={{0,2},{2,0},{4,6},{6,4},{8,10},{10,8},{12,14},{14,12},{16,18},{18,... | collective-permute-start | bytes 5013512 | tf_op jit(solution)/shard_map/ppermute | solution.py:19
  87.6 19.0 %collective-permute-start.11 = (bf16[1632,512]{1,0:T(8,128)(2,1)}, bf16[1632,512]{1,0:T(8,128)(2,1)S(1)}, u32[]{:S(2)}, u32[]{:S(2)}) collective-permute-start(bf16[1632,512]{1,0:T(8,128)(2,1)} %collective-permute-done.5.refs_1_.refs_4_), channel_id=1, source_target_pairs={{0,2},{2,0},{4,6},{6,4},{8,10},{10,8},{12,14},{14,12},{16,18},{18,... | collective-permute-start | bytes 5013512 | tf_op jit(solution)/shard_map/ppermute | solution.py:19
  88.0 39.4 %collective-permute-start.9 = (bf16[1632,512]{1,0:T(8,128)(2,1)}, bf16[1632,512]{1,0:T(8,128)(2,1)S(1)}, u32[]{:S(2)}, u32[]{:S(2)}) collective-permute-start(bf16[1632,512]{1,0:T(8,128)(2,1)} %collective-permute-done.4.refs_0_.refs_3_), channel_id=1, source_target_pairs={{0,8},{8,16},{16,24},{24,28},{28,20},{20,12},{12,4},{4,0},{10,2},{... | collective-permute-start | bytes 5013512 | tf_op jit(solution)/shard_map/ppermute | solution.py:543
  89.2 38.3 %collective-permute-start.10 = (bf16[1632,512]{1,0:T(8,128)(2,1)}, bf16[1632,512]{1,0:T(8,128)(2,1)}, u32[]{:S(2)}, u32[]{:S(2)}) collective-permute-start(bf16[1632,512]{1,0:T(8,128)(2,1)} %collective-permute-done.5.refs_1_.refs_4_), channel_id=1, source_target_pairs={{8,0},{16,8},{24,16},{28,24},{20,28},{12,20},{4,12},{0,4},{2,10},{... | collective-permute-start | bytes 5013512 | tf_op jit(solution)/shard_map/ppermute | solution.py:543
  90.1 13.7 %collective-permute-start.14 = (bf16[1,512,512]{2,1,0:T(8,128)(2,1)}, bf16[1,512,512]{2,1,0:T(8,128)(2,1)}, u32[]{:S(2)}, u32[]{:S(2)}) collective-permute-start(bf16[1,512,512]{2,1,0:T(8,128)(2,1)} %bitcast.72), channel_id=1, source_target_pairs={{0,1},{1,0},{2,3},{3,2},{4,5},{5,4},{6,7},{7,6},{8,9},{9,8},{10,11... | collective-permute-start | bytes 1572872 | tf_op jit(solution)/shard_map/ppermute | solution.py:19
  103.7 14.3 %collective-permute-start.13 = (bf16[240,256]{1,0:T(8,128)(2,1)S(1)}, bf16[240,256]{1,0:T(8,128)(2,1)S(1)}, u32[]{:S(2)}, u32[]{:S(2)}) collective-permute-start(bf16[240,256]{1,0:T(8,128)(2,1)S(1)} %convert_element_type.34), channel_id=1, source_target_pairs={{0,1},{1,0},{2,3},{3,2},{4,5},{5,4},{6,7},{7,6},{8,9},{9,8},{10,11... | collective-permute-start | bytes 368648 | tf_op jit(solution)/shard_map/ppermute | solution.py:19
  106.6 6.2 %copy-start.8 = (f32[512,256]{1,0:T(8,128)S(1)}, f32[512,256]{1,0:T(8,128)}, u32[]{:S(2)}) copy-start(f32[512,256]{1,0:T(8,128)} %copy-done.7) | copy-start | bytes 1572868
  106.6 6.2 %copy-start.3 = (bf16[1632,512]{1,0:T(8,128)(2,1)}, bf16[1632,512]{1,0:T(8,128)(2,1)S(1)}, u32[]{:S(2)}) copy-start(bf16[1632,512]{1,0:T(8,128)(2,1)S(1)} %collective-permute-done.11.refs_2_.refs_11_) | copy-start | bytes 5013508
  127.4 11.3 %copy-start.1 = (bf16[1632,512]{1,0:T(8,128)(2,1)}, bf16[1632,512]{1,0:T(8,128)(2,1)S(1)}, u32[]{:S(2)}) copy-start(bf16[1632,512]{1,0:T(8,128)(2,1)S(1)} %collective-permute-done.9.refs_0_.refs_5_) | copy-start | bytes 5013508
  127.4 5.1 %collective-permute-start.16 = (bf16[1632,512]{1,0:T(8,128)(2,1)}, bf16[1632,512]{1,0:T(8,128)(2,1)S(1)}, u32[]{:S(2)}, u32[]{:S(2)}) collective-permute-start(bf16[1632,512]{1,0:T(8,128)(2,1)} %collective-permute-done.10.refs_1_.refs_6_), channel_id=1, source_target_pairs={{0,2},{2,0},{4,6},{6,4},{8,10},{10,8},{12,14},{14,12},{16,18},{18,... | collective-permute-start | bytes 5013512 | tf_op jit(solution)/shard_map/ppermute | solution.py:19
  127.6 6.0 %collective-permute-start.17 = (bf16[1632,512]{1,0:T(8,128)(2,1)S(1)}, bf16[1632,512]{1,0:T(8,128)(2,1)}, u32[]{:S(2)}, u32[]{:S(2)}) collective-permute-start(bf16[1632,512]{1,0:T(8,128)(2,1)S(1)} %collective-permute-done.9.refs_0_.refs_5_), channel_id=1, source_target_pairs={{0,2},{2,0},{4,6},{6,4},{8,10},{10,8},{12,14},{14,12},{16,18},{18,... | collective-permute-start | bytes 5013512 | tf_op jit(solution)/shard_map/ppermute | solution.py:19
  129.0 16.2 %collective-permute-start.15 = (bf16[1120,512]{1,0:T(8,128)(2,1)}, bf16[1120,512]{1,0:T(8,128)(2,1)}, u32[]{:S(2)}, u32[]{:S(2)}) collective-permute-start(bf16[1120,512]{1,0:T(8,128)(2,1)} %slice.125), channel_id=1, source_target_pairs={{0,8},{8,16},{16,24},{24,28},{28,20},{20,12},{12,4},{4,0},{10,2},{... | collective-permute-start | bytes 3440648 | tf_op jit(solution)/shard_map/ppermute | solution.py:559
  130.7 12.1 %collective-permute-start.18 = (bf16[160,256]{1,0:T(8,128)(2,1)}, bf16[160,256]{1,0:T(8,128)(2,1)}, u32[]{:S(2)}, u32[]{:S(2)}) collective-permute-start(bf16[160,256]{1,0:T(8,128)(2,1)} %convert_element_type.35), channel_id=1, source_target_pairs={{0,1},{1,0},{2,3},{3,2},{4,5},{5,4},{6,7},{7,6},{8,9},{9,8},{10,11... | collective-permute-start | bytes 245768 | tf_op jit(solution)/shard_map/ppermute | solution.py:19
  131.5 7.3 %copy-start.10 = (f32[512,256]{1,0:T(8,128)S(1)}, f32[512,256]{1,0:T(8,128)}, u32[]{:S(2)}) copy-start(f32[512,256]{1,0:T(8,128)} %copy-done.9) | copy-start | bytes 1572868
  132.5 6.2 %copy-start.4 = (bf16[1632,512]{1,0:T(8,128)(2,1)}, bf16[1632,512]{1,0:T(8,128)(2,1)S(1)}, u32[]{:S(2)}) copy-start(bf16[1632,512]{1,0:T(8,128)(2,1)S(1)} %collective-permute-done.16.refs_2_.refs_13_) | copy-start | bytes 5013508
  138.7 7.5 %copy-start.13 = (f32[160,256]{1,0:T(8,128)}, f32[160,256]{1,0:T(8,128)S(1)}, u32[]{:S(2)}) copy-start(f32[160,256]{1,0:T(8,128)S(1)} %project_acts.6.refs_2_) | copy-start | bytes 491524
  142.9 10.1 %copy-start.11 = (f32[512,256]{1,0:T(8,128)}, f32[512,256]{1,0:T(8,128)S(1)}, u32[]{:S(2)}) copy-start(f32[512,256]{1,0:T(8,128)S(1)} %add_grads.6.refs_4_) | copy-start | bytes 1572868
  145.2 3.0 %collective-permute-start.20 = (bf16[1120,512]{1,0:T(8,128)(2,1)}, bf16[1120,512]{1,0:T(8,128)(2,1)S(1)}, u32[]{:S(2)}, u32[]{:S(2)}) collective-permute-start(bf16[1120,512]{1,0:T(8,128)(2,1)} %collective-permute-done.15.refs_0_.refs_7_), channel_id=1, source_target_pairs={{0,2},{2,0},{4,6},{6,4},{8,10},{10,8},{12,14},{14,12},{16,18},{18,... | collective-permute-start | bytes 3440648 | tf_op jit(solution)/shard_map/ppermute | solution.py:19
  145.2 9.2 %collective-permute-start.19 = (bf16[512,512]{1,0:T(8,128)(2,1)S(1)}, bf16[512,512]{1,0:T(8,128)(2,1)S(1)}, u32[]{:S(2)}, u32[]{:S(2)}) collective-permute-start(bf16[512,512]{1,0:T(8,128)(2,1)S(1)} %slice.124), channel_id=1, source_target_pairs={{0,8},{8,16},{16,24},{24,28},{28,20},{20,12},{12,4},{4,0},{10,2},{... | collective-permute-start | bytes 1572872 | tf_op jit(solution)/shard_map/ppermute | solution.py:565
  146.3 6.7 %collective-permute-start.21 = (bf16[160,256]{1,0:T(8,128)(2,1)S(1)}, bf16[160,256]{1,0:T(8,128)(2,1)S(1)}, u32[]{:S(2)}, u32[]{:S(2)}) collective-permute-start(bf16[160,256]{1,0:T(8,128)(2,1)S(1)} %convert_element_type.36), channel_id=1, source_target_pairs={{0,1},{1,0},{2,3},{3,2},{4,5},{5,4},{6,7},{7,6},{8,9},{9,8},{10,11... | collective-permute-start | bytes 245768 | tf_op jit(solution)/shard_map/ppermute | solution.py:19
  154.4 1.9 collective-permute-start.22
  154.4 5.6 %collective-permute-start.23 = (bf16[80,256]{1,0:T(8,128)(2,1)S(1)}, bf16[80,256]{1,0:T(8,128)(2,1)S(1)}, u32[]{:S(2)}, u32[]{:S(2)}) collective-permute-start(bf16[80,256]{1,0:T(8,128)(2,1)S(1)} %convert_element_type.37), channel_id=1, source_target_pairs={{0,1},{1,0},{2,3},{3,2},{4,5},{5,4},{6,7},{7,6},{8,9},{9,8},{10,11... | collective-permute-start | bytes 122888 | tf_op jit(solution)/shard_map/ppermute | solution.py:19
  155.2 4.8 %copy-start.6 = (f32[240,256]{1,0:T(8,128)S(1)}, f32[240,256]{1,0:T(8,128)}, u32[]{:S(2)}) copy-start(f32[240,256]{1,0:T(8,128)} %copy-done.5) | copy-start | bytes 737284
  157.3 2.6 %copy-start.16 = (bf16[240,256]{1,0:T(8,128)(2,1)S(1)}, bf16[240,256]{1,0:T(8,128)(2,1)}, u32[]{:S(2)}) copy-start(bf16[240,256]{1,0:T(8,128)(2,1)} %copy-done.15) | copy-start | bytes 368644
  161.4 2.2 collective-permute-start.24
  164.0 6.3 %collective-permute-start.25 = (bf16[2,64,640]{2,1,0:T(8,128)(2,1)S(1)}, bf16[2,64,640]{2,1,0:T(8,128)(2,1)S(1)}, u32[]{:S(2)}, u32[]{:S(2)}) collective-permute-start(bf16[2,64,640]{2,1,0:T(8,128)(2,1)S(1)} %get-tuple-element.64), channel_id=1, source_target_pairs={{0,4},{2,6},{4,0},{6,2},{8,12},{10,14},{12,8},{14,10},{16,20},{18,... | collective-permute-start | bytes 491528 | tf_op jit(solution)/shard_map/ppermute | solution.py:19
  165.2 7.1 %collective-permute-start.26 = (bf16[2,64,640]{2,1,0:T(8,128)(2,1)S(1)}, bf16[2,64,640]{2,1,0:T(8,128)(2,1)S(1)}, u32[]{:S(2)}, u32[]{:S(2)}) collective-permute-start(bf16[2,64,640]{2,1,0:T(8,128)(2,1)S(1)} %get-tuple-element.65), channel_id=1, source_target_pairs={{0,8},{2,10},{4,12},{6,14},{8,0},{10,2},{12,4},{14,6},{16,24},{18,... | collective-permute-start | bytes 491528 | tf_op jit(solution)/shard_map/ppermute | solution.py:19
  166.6 8.4 %collective-permute-start.27 = (bf16[2,64,640]{2,1,0:T(8,128)(2,1)S(1)}, bf16[2,64,640]{2,1,0:T(8,128)(2,1)S(1)}, u32[]{:S(2)}, u32[]{:S(2)}) collective-permute-start(bf16[2,64,640]{2,1,0:T(8,128)(2,1)S(1)} %get-tuple-element.66), channel_id=1, source_target_pairs={{0,12},{2,14},{4,8},{6,10},{8,4},{10,6},{12,0},{14,2},{16,28},{18,... | collective-permute-start | bytes 491528 | tf_op jit(solution)/shard_map/ppermute | solution.py:19
  175.0 9.6 %collective-permute-start.28 = (bf16[2,64,640]{2,1,0:T(8,128)(2,1)S(1)}, bf16[2,64,640]{2,1,0:T(8,128)(2,1)S(1)}, u32[]{:S(2)}, u32[]{:S(2)}) collective-permute-start(bf16[2,64,640]{2,1,0:T(8,128)(2,1)S(1)} %fusion.2), channel_id=1, source_target_pairs={{0,16},{2,18},{4,20},{6,22},{8,24},{10,26},{12,28},{14,30},{16,0},... | collective-permute-start | bytes 491528 | tf_op jit(solution)/shard_map/ppermute | solution.py:19
  177.8 20.9 %copy-start.17 = (bf16[2,512,512]{2,1,0:T(8,128)(2,1)S(1)}, bf16[2,512,512]{2,1,0:T(8,128)(2,1)}, u32[]{:S(2)}) copy-start(bf16[2,512,512]{2,1,0:T(8,128)(2,1)} %pad_maximum_fusion.2) | copy-start | bytes 3145732
  184.8 4.5 %collective-permute-start.29 = (bf16[1,64,640]{2,1,0:T(8,128)(2,1)S(1)}, bf16[1,64,640]{2,1,0:T(8,128)(2,1)S(1)}, u32[]{:S(2)}, u32[]{:S(2)}) collective-permute-start(bf16[1,64,640]{2,1,0:T(8,128)(2,1)S(1)} %get-tuple-element.77), channel_id=1, source_target_pairs={{0,1},{1,0},{2,3},{3,2},{4,5},{5,4},{6,7},{7,6},{8,9},{9,8},{10,11... | collective-permute-start | bytes 245768 | tf_op jit(solution)/shard_map/ppermute | solution.py:19
  189.3 6.2 %collective-permute-start.31 = (bf16[2,64,640]{2,1,0:T(8,128)(2,1)S(1)}, bf16[2,64,640]{2,1,0:T(8,128)(2,1)S(1)}, u32[]{:S(2)}, u32[]{:S(2)}) collective-permute-start(bf16[2,64,640]{2,1,0:T(8,128)(2,1)S(1)} %get-tuple-element.79), channel_id=1, source_target_pairs={{0,8},{2,10},{4,12},{6,14},{8,0},{10,2},{12,4},{14,6},{16,24},{18,... | collective-permute-start | bytes 491528 | tf_op jit(solution)/shard_map/ppermute | solution.py:19
  189.4 6.4 %collective-permute-start.30 = (bf16[2,64,640]{2,1,0:T(8,128)(2,1)S(1)}, bf16[2,64,640]{2,1,0:T(8,128)(2,1)S(1)}, u32[]{:S(2)}, u32[]{:S(2)}) collective-permute-start(bf16[2,64,640]{2,1,0:T(8,128)(2,1)S(1)} %get-tuple-element.79), channel_id=1, source_target_pairs={{0,4},{2,6},{4,0},{6,2},{8,12},{10,14},{12,8},{14,10},{16,20},{18,... | collective-permute-start | bytes 491528 | tf_op jit(solution)/shard_map/ppermute | solution.py:19
  190.6 7.9 %collective-permute-start.32 = (bf16[2,64,640]{2,1,0:T(8,128)(2,1)S(1)}, bf16[2,64,640]{2,1,0:T(8,128)(2,1)S(1)}, u32[]{:S(2)}, u32[]{:S(2)}) collective-permute-start(bf16[2,64,640]{2,1,0:T(8,128)(2,1)S(1)} %get-tuple-element.79), channel_id=1, source_target_pairs={{0,12},{2,14},{4,8},{6,10},{8,4},{10,6},{12,0},{14,2},{16,28},{18,... | collective-permute-start | bytes 491528 | tf_op jit(solution)/shard_map/ppermute | solution.py:19
  193.0 5.6 %collective-permute-start.33 = (f32[64,320]{1,0:T(8,128)S(1)}, f32[64,320]{1,0:T(8,128)S(1)}, u32[]{:S(2)}, u32[]{:S(2)}) collective-permute-start(f32[64,320]{1,0:T(8,128)S(1)} %dynamic-slice_bitcast_fusion.2), channel_id=1, source_target_pairs={{0,0},{2,2},{4,4},{6,6},{8,8},{10,10},{12,12},{14,14},{16,1},{18,3... | collective-permute-start | bytes 245768 | tf_op jit(solution)/shard_map/ppermute | solution.py:484
  198.7 2.2 collective-permute-start.34
  (6 other events, 6.6 us)

commit v5 on v4

--- a/solution.py
+++ b/solution.py
@@ -9,8 +9,8 @@
 
 BF16, F32 = jnp.bfloat16, jnp.float32
 VMEM_BYTES = 48 * 1024 * 1024
-EXPAND_ROWS = 4096
-AHEAD = 2
+FIRST = 2
+AHEAD = 3
 PROJECT_UNITS = 8192
 
 
@@ -147,26 +147,32 @@
     return piece[: chunks * rows].reshape((chunks, rows, lanes)).transpose(1, 0, 2).reshape((rows, -1))
 
 
-def add_grads_kernel(at_ref, *refs):
+def add_grads_kernel(apart, at_ref, *refs):
     total_ref, out_ref, held, arrived = refs[-4:]
     count = (len(refs) - 4) // 2
     copies = []
+    if apart:
+        early = pltpu.make_async_copy(total_ref, out_ref, arrived.at[count])
+        early.start()
     for k in range(count):
         start = refs[k].shape[0] - held.shape[1]
         copies.append(
             pltpu.make_async_copy(refs[k].at[pl.ds(start, held.shape[1])], held.at[k], arrived.at[k])
         )
         copies[-1].start()
-    total = total_ref[...]
+    total = jnp.zeros(out_ref.shape, F32) if apart else total_ref[...]
     for k in range(count):
         copies[k].wait()
         total += lax.dot_general(
             held[k], refs[count + k][0], (((1,), (1,)), ((), ())), preferred_element_type=F32
         )
+    if apart:
+        early.wait()
+        total += out_ref[...]
     out_ref[...] = total
 
 
-def add_grads(pieces, origins, wide_grads, total, n_dp):
+def add_grads(pieces, origins, wide_grads, total, n_dp, apart=False):
     directions, units = total.shape[0], pieces[0].shape[1]
     n_mp, tokens, _ = wide_grads.shape
     share = n_dp // n_mp
@@ -177,17 +183,17 @@
         return pl.BlockSpec((1, tokens, units), lambda i, at_ref: (at_ref[2 * k], 0, at_ref[2 * k + 1]))
 
     return pl.pallas_call(
-        add_grads_kernel,
+        functools.partial(add_grads_kernel, apart),
         grid_spec=pltpu.PrefetchScalarGridSpec(
             num_scalar_prefetch=1,
             grid=(1,),
             in_specs=[pl.BlockSpec(memory_space=pl.ANY)] * count
             + [columns(k) for k in range(count)]
-            + [whole_block(total.shape)],
+            + [pl.BlockSpec(memory_space=pltpu.HBM) if apart else whole_block(total.shape)],
             out_specs=whole_block(total.shape),
             scratch_shapes=[
                 pltpu.VMEM((count, directions, units), BF16),
-                pltpu.SemaphoreType.DMA((count,)),
+                pltpu.SemaphoreType.DMA((count + 1,)),
             ],
         ),
         out_shape=jax.ShapeDtypeStruct(total.shape, F32),
@@ -215,27 +221,28 @@
     )(at, early, late)
 
 
-def expand_kernel(tiles, rows, at_ref, near_ref, far_ref, turn_ref, *refs):
-    count = (len(refs) - 9) // 2
-    owns, others, out_ref = refs[:count], refs[count : 2 * count], refs[2 * count]
+def expand_kernel(tiles, rows, at_ref, near_ref, far_ref, turn_ref, _, *refs):
+    count = (len(refs) - 11) // 2
+    groups, out_ref = (refs[:count], refs[count : 2 * count]), refs[2 * count]
     scaled, turned, back, held, pieces, sent, first_sem, piece_sem, out_sem = refs[-9:]
-    deep = pieces.shape[2]
-    ahead = min(AHEAD, tiles)
     depth, lanes = near_ref.shape[0], pieces.shape[3]
-    out_rows = sent.shape[1]
-
-    def fetch(group, half, t):
-        tile = half * tiles + t
+    half_units = out_ref.shape[0] // 2
+
+    def fetch(n):
+        half, first, chunks = tiles[n]
+        part = pl.ds(first * rows, chunks * rows)
         return [
-            pltpu.make_async_copy(ref.at[pl.ds(t * deep, deep)], pieces.at[tile, k], piece_sem.at[tile, k])
-            for k, ref in enumerate(group)
+            pltpu.make_async_copy(ref.at[part], pieces.at[half, k, part], piece_sem.at[n, k])
+            for k, ref in enumerate(groups[half])
         ]
 
-    def store(half, t):
+    def store(n):
+        half, first, chunks = tiles[n]
         side = at_ref[0] if half == 0 else 1 - at_ref[0]
-        tile = half * tiles + t
         return pltpu.make_async_copy(
-            sent.at[tile % 2], out_ref.at[pl.ds((side * tiles + t) * out_rows, out_rows)], out_sem.at[tile % 2]
+            sent.at[n % 2, pl.ds(0, chunks * lanes)],
+            out_ref.at[pl.ds(side * half_units + first * lanes, chunks * lanes)],
+            out_sem.at[n % 2],
         )
 
     opening = [
@@ -243,13 +250,13 @@
         pltpu.make_async_copy(far_ref, scaled.at[1], first_sem.at[1]),
         pltpu.make_async_copy(turn_ref, turned, first_sem.at[2]),
     ]
-    for copy in opening:
+    for copy in opening + fetch(0):
         copy.start()
-    for t in range(ahead):
-        for copy in fetch(owns, 0, t):
-            copy.start()
     for copy in opening:
         copy.wait()
+    for n in range(1, AHEAD):
+        for copy in fetch(n):
+            copy.start()
     dims = (((0,), (0,)), ((), ()))
     total = lax.dot_general(scaled[0], turned[:depth], dims, preferred_element_type=F32)
     total += lax.dot_general(scaled[1], turned[depth:], dims, preferred_element_type=F32)
@@ -258,42 +265,26 @@
         start = pl.multiple_of(at_ref[1 + k] * rows, 16)
         held[k * rows : (k + 1) * rows] = back[pl.ds(start, rows)]
 
-    def step(half, group, t, more, next_half, next_group, next_t, settled):
-        if more:
-            for copy in fetch(next_group, next_half, next_t):
+    for n, (half, first, chunks) in enumerate(tiles):
+        if n + AHEAD < len(tiles):
+            for copy in fetch(n + AHEAD):
                 copy.start()
-        for copy in fetch(group, half, t):
+        for copy in fetch(n):
             copy.wait()
-        tile = half * tiles + t
-        if settled is not None:
-            store(*settled).wait()
-        for c in range(deep // rows):
-            part = jnp.concatenate([pieces[tile, k, c * rows : (c + 1) * rows] for k in range(count)], axis=0)
-            sent[tile % 2, c * lanes : (c + 1) * lanes] = lax.dot_general(
+        if n >= 2:
+            store(n - 2).wait()
+        for c in range(chunks):
+            at = (first + c) * rows
+            part = jnp.concatenate([pieces[half, k, at : at + rows] for k in range(count)], axis=0)
+            sent[n % 2, c * lanes : (c + 1) * lanes] = lax.dot_general(
                 part, held[...], dims, preferred_element_type=F32
             ).astype(BF16)
-        store(half, t).start()
-
-    for half, group in ((0, owns), (1, others)):
-        for t in range(tiles):
-            tile = half * tiles + t
-            coming = tile + ahead
-            before = tile - 2
-            step(
-                half,
-                group,
-                t,
-                coming < 2 * tiles,
-                coming // tiles,
-                owns if coming < tiles else others,
-                coming % tiles,
-                (before // tiles, before % tiles) if before >= 0 else None,
-            )
-    for tile in (2 * tiles - 2, 2 * tiles - 1):
-        store(tile // tiles, tile % tiles).wait()
-
-
-def expand(owns, others, pairs, rows, units, core, near, far, turn):
+        store(n).start()
+    store(len(tiles) - 2).wait()
+    store(len(tiles) - 1).wait()
+
+
+def expand(owns, others, pairs, rows, units, core, near, far, turn, diag_t):
     lanes = owns[0].shape[1]
     chunks = units // 2 // lanes
     columns = turn.shape[1]
@@ -306,9 +297,11 @@
         for pieces in (owns, others):
             plain = jnp.concatenate([unchunk(piece, rows, chunks) for piece in pieces])
             sides.append(lax.dot_general(plain, held, (((0,), (0,)), ((), ())), preferred_element_type=F32).astype(BF16))
-        return jnp.where(core == 0, jnp.concatenate(sides), jnp.concatenate(sides[::-1]))
-    group = max(g for g in range(1, chunks + 1) if chunks % g == 0 and g * lanes <= EXPAND_ROWS)
-    tiles = chunks // group
+        return jnp.where(core == 0, jnp.concatenate(sides), jnp.concatenate(sides[::-1])), diag_t
+    size = max(1, (chunks - FIRST) // 2)
+    cuts = sorted({0, min(FIRST, chunks)} | set(range(FIRST, chunks, size)) | {chunks})
+    spans = [(low, high - low) for low, high in zip(cuts, cuts[1:])]
+    tiles = [(0, low, n) for low, n in spans] + [(1, chunks - low - n, n) for low, n in spans[::-1]]
     count = len(owns)
     anywhere = pl.BlockSpec(memory_space=pl.ANY)
     return pl.pallas_call(
@@ -316,27 +309,28 @@
         grid_spec=pltpu.PrefetchScalarGridSpec(
             num_scalar_prefetch=1,
             grid=(1,),
-            in_specs=[anywhere] * (3 + 2 * count),
-            out_specs=anywhere,
+            in_specs=[anywhere] * 3 + [pl.BlockSpec(memory_space=pltpu.HBM)] + [anywhere] * (2 * count),
+            out_specs=[anywhere, pl.BlockSpec(memory_space=pltpu.HBM)],
             scratch_shapes=[
                 pltpu.VMEM((2,) + near.shape, BF16),
                 pltpu.VMEM(turn.shape, BF16),
                 pltpu.VMEM((count * rows, columns), BF16),
                 pltpu.VMEM((count * rows, columns), BF16),
-                pltpu.VMEM((2 * tiles, count, group * rows, lanes), BF16),
-                pltpu.VMEM((2, group * lanes, columns), BF16),
+                pltpu.VMEM((2, count, chunks * rows, lanes), BF16),
+                pltpu.VMEM((2, max(n for _, _, n in tiles) * lanes, columns), BF16),
                 pltpu.SemaphoreType.DMA((3,)),
-                pltpu.SemaphoreType.DMA((2 * tiles, count)),
+                pltpu.SemaphoreType.DMA((len(tiles), count)),
                 pltpu.SemaphoreType.DMA((2,)),
             ],
         ),
-        out_shape=jax.ShapeDtypeStruct((units, columns), BF16),
+        out_shape=[jax.ShapeDtypeStruct((units, columns), BF16), jax.ShapeDtypeStruct(diag_t.shape, F32)],
+        input_output_aliases={4: 1},
         compiler_params=pltpu.CompilerParams(vmem_limit_bytes=VMEM_BYTES),
         cost_estimate=pl.CostEstimate(
             flops=2 * rows * count * units * columns, bytes_accessed=2 * units * columns, transcendentals=0
         ),
         name="expand_update",
-    )(at, near, far, turn, *owns, *others)
+    )(at, near, far, turn, diag_t, *owns, *others)
 
 
 def gather_near_first(x, axis_name):
@@ -483,7 +477,7 @@
         sent = lax.dynamic_slice(diag_t, (0, target * rows), (width, rows))
         got = lax.ppermute(sent, ("dp", "mp"), hops)
         out = lax.dynamic_update_slice(out, got[None], ((here // 2 - k) % share, 0, 0))
-    return out.reshape((share * width, rows)).T
+    return out.reshape((share * width, rows))
 
 
 def on_device(acts, grads, basis_in, basis_out, damping):
@@ -572,6 +566,7 @@
         wide_grads,
         grad_proj_t,
         n_dp,
+        True,
     )
 
     rows_near = rows_near.reshape((n_mp, half // 2, 2, 2 * width, out_units))
@@ -585,7 +580,8 @@
     scaled = (rotated / (diag_t + damping[0])).astype(BF16)
     near, far, diag = gather_scaled(scaled, place_diag(diag_t))
     near, far = (x.reshape((directions * n_mp // 2, -1)) for x in (near, far))
-    return (expand(owns, others, pairs, rows, units, core, near, far, rows_near), diag)
+    update, diag_t = expand(owns, others, pairs, rows, units, core, near, far, rows_near, diag)
+    return (update, diag_t.T)
 
 
 def solution(mesh):

time: 221 us -> 219 us (level)
  no operation moved by 1% of the time
where the time goes in v5:
time: 219 us; the launch traced here: 217 us
  waiting for transfers between devices  111 us (51%)
  Pallas kernels  56.6 us (26%)
  starting transfers between devices  27.5 us (13%)
  other arithmetic  11.2 us (5%)
  local copies, waits for them, and re-layouts  8.78 us (4%)
    ppermute x6, waiting for transfers between devices, on_device(): moving = [lax.ppermute(x, 'dp', everyone[k]) for k, x in enumerate(moving)]  62.4 us
    ppermute x26, waiting for transfers between devices, flip(): return lax.ppermute(x, axis_name, [(i, i ^ bit) for i in range(size)])  45.7 us
    pallas_call x4, Pallas kernels, project(): pl.pallas_call(functools.partial(project_kernel, tiles, rows), grid_spec=...  22 us
    ppermute x26, starting transfers between devices, flip(): return lax.ppermute(x, axis_name, [(i, i ^ bit) for i in range(size)])  18.5 us
    pallas_call x1, Pallas kernels, expand(): pl.pallas_call(functools.partial(expand_kernel, tiles, rows), grid_spec=p...  17.1 us
    pallas_call x4, Pallas kernels, add_grads(): pl.pallas_call(functools.partial(add_grads_kernel, apart), grid_spec=pltp...  15.8 us
    ppermute x6, starting transfers between devices, on_device(): moving = [lax.ppermute(x, 'dp', everyone[k]) for k, x in enumerate(moving)]  6.08 us
    unnamed x66, local copies, waits for them, and re-layouts  5.54 us
  transfers between devices with their start and end apart: 35, of which 23 were waited for; matrix products, arithmetic and copies ran while one was open for 6% of the time, Pallas kernels for 17%

profile of v5, /device:TPU:0, one launch (start us, length us, event | category | flops | bytes accessed | tf_op | source)
XLA Modules:
  0.0 217.1 jit_solution(2737023447531164347)
XLA Ops:
  0.7 1.4 dynamic-slice_bitcast_fusion.1
  2.7 2.6 %collective-permute-start.8 = (bf16[1,256,4096]{2,1,0:T(8,128)(2,1)}, bf16[1,256,4096]{2,1,0:T(8,128)(2,1)}, u32[]{:S(2)}, u32[]{:S(2)}) collective-permute-start(bf16[1,256,4096]{2,1,0:T(8,128)(2,1)} %bitcast.60), channel_id=1, source_target_pairs={{0,1},{1,0},{2,3},{3,2},{4,5},{5,4},{6,7},{7,6},{8,9},{9,8},{10,11... | collective-permute-start | bytes 6291464 | tf_op jit(solution)/shard_map/ppermute | solution.py:19
  5.3 1.0 copy.9
  6.8 1.2 pad_maximum_fusion.refs_0_
  8.2 1.5 collective-permute-start.2
  10.3 1.5 collective-permute-done.3.refs_3_.refs_8_
  11.8 35.2 %collective-permute-done.2.refs_2_ = bf16[1632,512]{1,0:T(8,128)(2,1)S(1)} collective-permute-done((bf16[1632,512]{1,0:T(8,128)(2,1)S(1)}, bf16[1632,512]{1,0:T(8,128)(2,1)S(1)}, u32[]{:S(2)}, u32[]{:S(2)}) %collective-permute-start.2) | collective-permute-done | bytes 1671200 | tf_op jit(solution)/shard_map/ppermute | solution.py:537
  47.8 1.6 collective-permute-start.4
  50.0 1.9 collective-permute-done.8
  51.8 2.5 %select_bitcast_fusion.1 = (bf16[1,1,256,4096]{3,2,1,0:T(8,128)(2,1)S(1)}, bf16[1,1,256,4096]{3,2,1,0:T(8,128)(2,1)S(1)}) fusion(bf16[1,256,4096]{2,1,0:T(8,128)(2,1)} %collective-permute-done.8, pred[]{:T(512)S(6)} %eq.57, bf16[256,4096]{1,0:T(8,128)(2,1)} %param.6), kind=kLoop, calls=%fused_computation.2 | loop fusion | flops 2097152 | bytes 8388609 | tf_op jit(solution)/shard_map/stack | solution.py:36
  54.3 2.4 %maximum_bitcast_fusion.refs_6_.refs_7_.refs_8_.refs_9_.refs_10_.refs_11_.refs_4_.refs_5_.refs_2_.refs_3_ = bf16[2,256,4096]{2,1,0:T(8,128)(2,1)} fusion(bf16[1,1,256,4096]{3,2,1,0:T(8,128)(2,1)S(1)} %get-tuple-element.75, bf16[1,1,256,4096]{3,2,1,0:T(8,128)(2,1)S(1)} %get-tuple-element.74), kind=kLoop, calls=%fused_computation | loop fusion | flops 2097152 | bytes 8388608 | tf_op jit(solution)/shard_map/reshape | solution.py:36
  56.7 5.9 %project_acts.4.refs_0_ = f32[240,256]{1,0:T(8,128)S(1)} custom-call(s32[1]{0:T(128)} %bitcast.at_ref, bf16[256,14336]{1,0:T(8,128)(2,1)} %acts_ref.7, bf16[1632,512]{1,0:T(8,128)(2,1)S(1)} %pad_maximum_fusion.refs_0_, bf16[1632,512]{1,0:T(8,128)(2,1)} %collective-permute-done.1.refs_1_, bf16[1632,512]{1,0:T(8,128)(2,1)S(1)} %collective-permute-done.2.refs_2_, ...), custom_call_target="tpu_custom_call" | custom-call | flops 1 | bytes 1 | tf_op jit(solution)/shard_map/project_acts/pallas_call | solution.py:123
  63.4 5.0 %add_grads.4.refs_8_ = f32[512,256]{1,0:T(8,128)S(1)} custom-call(s32[12]{0:T(128)S(1)} %stack.332.at_ref, bf16[1632,512]{1,0:T(8,128)(2,1)S(1)} %pad_maximum_fusion.refs_0_, bf16[1632,512]{1,0:T(8,128)(2,1)} %collective-permute-done.1.refs_1_, bf16[1632,512]{1,0:T(8,128)(2,1)S(1)} %collective-permute-done.2.refs_2_, ...), custom_call_target="tpu_custom_call" | custom-call | flops 1 | bytes 1 | tf_op jit(solution)/shard_map/add_grads/pallas_call | solution.py:185
  69.2 18.3 %collective-permute-done.4.refs_0_.refs_3_ = bf16[1632,512]{1,0:T(8,128)(2,1)} collective-permute-done((bf16[1632,512]{1,0:T(8,128)(2,1)}, bf16[1632,512]{1,0:T(8,128)(2,1)}, u32[]{:S(2)}, u32[]{:S(2)}) %collective-permute-start.4) | collective-permute-done | bytes 1671200 | tf_op jit(solution)/shard_map/ppermute | solution.py:537
  88.0 1.1 collective-permute-start.9
  91.7 12.0 %collective-permute-done.14 = bf16[1,512,512]{2,1,0:T(8,128)(2,1)} collective-permute-done((bf16[1,512,512]{2,1,0:T(8,128)(2,1)}, bf16[1,512,512]{2,1,0:T(8,128)(2,1)}, u32[]{:S(2)}, u32[]{:S(2)}) %collective-permute-start.14) | collective-permute-done | bytes 524320 | tf_op jit(solution)/shard_map/ppermute | solution.py:19
  104.4 2.3 %pad_maximum_fusion.2 = bf16[2,512,512]{2,1,0:T(8,128)(2,1)} fusion(bf16[1,512,512]{2,1,0:T(8,128)(2,1)} %collective-permute-done.14, bf16[1,512,512]{2,1,0:T(8,128)(2,1)} %bitcast.72), kind=kLoop, calls=%fused_computation.9 | loop fusion | flops 524288 | bytes 2097152 | tf_op jit(solution)/shard_map/concatenate | solution.py:339
  106.6 6.2 %project_acts.5.refs_1_ = f32[160,256]{1,0:T(8,128)S(1)} custom-call(s32[1]{0:T(128)} %bitcast.at_ref, bf16[256,14336]{1,0:T(8,128)(2,1)} %acts_ref.7, bf16[1632,512]{1,0:T(8,128)(2,1)} %collective-permute-done.4.refs_0_.refs_3_, bf16[1632,512]{1,0:T(8,128)(2,1)} %collective-permute-done.5.refs_1_.refs_4_, ...), custom_call_target="tpu_custom_call" | custom-call | flops 1 | bytes 1 | tf_op jit(solution)/shard_map/project_acts/pallas_call | solution.py:123
  112.9 4.4 %add_grads.5.refs_8_ = f32[512,256]{1,0:T(8,128)S(1)} custom-call(s32[8]{0:T(128)S(1)} %stack.344.at_ref, bf16[1632,512]{1,0:T(8,128)(2,1)} %collective-permute-done.4.refs_0_.refs_3_, bf16[1632,512]{1,0:T(8,128)(2,1)} %collective-permute-done.5.refs_1_.refs_4_, bf16[1632,512]{1,0:T(8,128)(2,1)S(1)} %collective-permute-done.11.refs_2_.refs_11_, ...), custom_call_target="tpu_custom_call" | custom-call | flops 1 | bytes 1 | tf_op jit(solution)/shard_map/add_grads/pallas_call | solution.py:185
  118.7 8.7 %collective-permute-done.9.refs_0_.refs_5_ = bf16[1632,512]{1,0:T(8,128)(2,1)S(1)} collective-permute-done((bf16[1632,512]{1,0:T(8,128)(2,1)}, bf16[1632,512]{1,0:T(8,128)(2,1)S(1)}, u32[]{:S(2)}, u32[]{:S(2)}) %collective-permute-start.9) | collective-permute-done | bytes 1671200 | tf_op jit(solution)/shard_map/ppermute | solution.py:537
  128.0 1.1 slice.125
  129.0 1.1 collective-permute-start.15
  132.5 1.0 collective-permute-done.17.refs_3_.refs_14_
  133.5 5.2 %project_acts.6.refs_2_ = f32[160,256]{1,0:T(8,128)S(1)} custom-call(s32[1]{0:T(128)} %bitcast.at_ref, bf16[256,14336]{1,0:T(8,128)(2,1)} %acts_ref.7, bf16[1632,512]{1,0:T(8,128)(2,1)S(1)} %collective-permute-done.9.refs_0_.refs_5_, bf16[1632,512]{1,0:T(8,128)(2,1)} %collective-permute-done.10.refs_1_.refs_6_, ...), custom_call_target="tpu_custom_call" | custom-call | flops 1 | bytes 1 | tf_op jit(solution)/shard_map/project_acts/pallas_call | solution.py:123
  138.7 4.1 %add_grads.6.refs_4_ = f32[512,256]{1,0:T(8,128)S(1)} custom-call(s32[8]{0:T(128)S(1)} %stack.353.at_ref, bf16[1632,512]{1,0:T(8,128)(2,1)S(1)} %collective-permute-done.9.refs_0_.refs_5_, bf16[1632,512]{1,0:T(8,128)(2,1)} %collective-permute-done.10.refs_1_.refs_6_, bf16[1632,512]{1,0:T(8,128)(2,1)S(1)} %collective-permute-done.16.refs_2_.refs_13_, ...), custom_call_target="tpu_custom_call" | custom-call | flops 1 | bytes 1 | tf_op jit(solution)/shard_map/add_grads/pallas_call | solution.py:185
  143.7 1.5 collective-permute-done.15.refs_0_.refs_7_
  145.2 1.1 collective-permute-start.19
  147.0 1.2 collective-permute-done.20.refs_1_.refs_15_
  148.2 4.7 %project_acts.7.refs_3_ = f32[80,256]{1,0:T(8,128)S(1)} custom-call(s32[1]{0:T(128)} %bitcast.at_ref, bf16[256,14336]{1,0:T(8,128)(2,1)} %acts_ref.7, bf16[1120,512]{1,0:T(8,128)(2,1)} %collective-permute-done.15.refs_0_.refs_7_, bf16[1120,512]{1,0:T(8,128)(2,1)S(1)} %collective-permute-done.20.refs_1_.refs_15_), custom_call_target="tpu_custom_call" | custom-call | flops 587202560 | bytes 9633792 | tf_op jit(solution)/shard_map/project_acts/pallas_call | solution.py:123
  153.0 1.4 collective-permute-done.19.refs_0_
  155.2 1.1 collective-permute-done.22.refs_1_
  156.3 2.3 %add_grads.7 = f32[512,256]{1,0:T(8,128)S(1)} custom-call(s32[4]{0:T(128)S(1)} %pad_add_fusion.at_ref, bf16[512,512]{1,0:T(8,128)(2,1)S(1)} %collective-permute-done.19.refs_0_, bf16[512,512]{1,0:T(8,128)(2,1)S(1)} %collective-permute-done.22.refs_1_, ...), custom_call_target="tpu_custom_call" | custom-call | flops 1 | bytes 1 | tf_op jit(solution)/shard_map/add_grads/pallas_call | solution.py:185
  158.6 1.4 sums_for_other_core.1
  160.2 2.0 collective-permute-done.24.got_ref
  162.6 1.2 collective-permute-start.25
  163.8 1.4 collective-permute-start.26
  166.1 2.8 %collective-permute-done.25 = bf16[2,64,640]{2,1,0:T(8,128)(2,1)S(1)} collective-permute-done((bf16[2,64,640]{2,1,0:T(8,128)(2,1)S(1)}, bf16[2,64,640]{2,1,0:T(8,128)(2,1)S(1)}, u32[]{:S(2)}, u32[]{:S(2)}) %collective-permute-start.25) | collective-permute-done | bytes 163872 | tf_op jit(solution)/shard_map/ppermute | solution.py:19
  168.9 2.0 collective-permute-done.26
  170.9 2.7 %collective-permute-done.27 = bf16[2,64,640]{2,1,0:T(8,128)(2,1)S(1)} collective-permute-done((bf16[2,64,640]{2,1,0:T(8,128)(2,1)S(1)}, bf16[2,64,640]{2,1,0:T(8,128)(2,1)S(1)}, u32[]{:S(2)}, u32[]{:S(2)}) %collective-permute-start.27) | collective-permute-done | bytes 163872 | tf_op jit(solution)/shard_map/ppermute | solution.py:19
  173.7 2.1 collective-permute-start.28
  176.4 6.8 %collective-permute-done.28 = bf16[2,64,640]{2,1,0:T(8,128)(2,1)S(1)} collective-permute-done((bf16[2,64,640]{2,1,0:T(8,128)(2,1)S(1)}, bf16[2,64,640]{2,1,0:T(8,128)(2,1)S(1)}, u32[]{:S(2)}, u32[]{:S(2)}) %collective-permute-start.28) | collective-permute-done | bytes 163872 | tf_op jit(solution)/shard_map/ppermute | solution.py:19
  184.0 3.8 %collective-permute-done.29 = bf16[1,64,640]{2,1,0:T(8,128)(2,1)S(1)} collective-permute-done((bf16[1,64,640]{2,1,0:T(8,128)(2,1)S(1)}, bf16[1,64,640]{2,1,0:T(8,128)(2,1)S(1)}, u32[]{:S(2)}, u32[]{:S(2)}) %collective-permute-start.29) | collective-permute-done | bytes 81952 | tf_op jit(solution)/shard_map/ppermute | solution.py:19
  188.0 1.3 collective-permute-start.30
  189.3 2.2 %collective-permute-start.32 = (bf16[2,64,640]{2,1,0:T(8,128)(2,1)S(1)}, bf16[2,64,640]{2,1,0:T(8,128)(2,1)S(1)}, u32[]{:S(2)}, u32[]{:S(2)}) collective-permute-start(bf16[2,64,640]{2,1,0:T(8,128)(2,1)S(1)} %get-tuple-element.83), channel_id=1, source_target_pairs={{0,12},{2,14},{4,8},{6,10},{8,4},{10,6},{12,0},{14,2},{16,28},{18,... | collective-permute-start | bytes 491528 | tf_op jit(solution)/shard_map/ppermute | solution.py:19
  192.6 1.6 collective-permute-done.31
  194.3 2.8 %collective-permute-done.32 = bf16[2,64,640]{2,1,0:T(8,128)(2,1)S(1)} collective-permute-done((bf16[2,64,640]{2,1,0:T(8,128)(2,1)S(1)}, bf16[2,64,640]{2,1,0:T(8,128)(2,1)S(1)}, u32[]{:S(2)}, u32[]{:S(2)}) %collective-permute-start.32) | collective-permute-done | bytes 163872 | tf_op jit(solution)/shard_map/ppermute | solution.py:19
  198.1 1.3 collective-permute-done.34
  199.4 17.1 %expand_update.1 = (bf16[14336,512]{1,0:T(8,128)(2,1)}, f32[64,320]{1,0:T(8,128)S(1)}) custom-call(s32[9]{0:T(128)S(1)} %stack.281.at_ref, bf16[512,640]{1,0:T(8,128)(2,1)S(1)} %bitcast.199, bf16[512,640]{1,0:T(8,128)(2,1)S(1)} %bitcast.201, bf16[1024,512]{1,0:T(8,128)(2,1)S(1)} %bitcast.198, ...), custom_call_target="tpu_custom_call", output_to_operand_aliasing={{1}: (4, {})} | custom-call | flops 9395240960 | bytes 14680064 | tf_op jit(solution)/shard_map/expand_update/pallas_call | solution.py:307
  (132 shorter events, 20.3 us)
Async XLA Ops:
  0.7 4.7 %copy-start.18 = (bf16[512,512]{1,0:T(8,128)(2,1)S(1)}, bf16[512,512]{1,0:T(8,128)(2,1)}, u32[]{:S(2)}) copy-start(bf16[512,512]{1,0:T(8,128)(2,1)} %param.8) | copy-start | bytes 1572868
  2.2 4.3 %collective-permute-start = (bf16[14,40,512]{2,1,0:T(8,128)(2,1)S(1)}, bf16[14,40,512]{2,1,0:T(8,128)(2,1)S(1)}, u32[]{:S(2)}, u32[]{:S(2)}) collective-permute-start(bf16[14,40,512]{2,1,0:T(8,128)(2,1)S(1)} %constant_dynamic-update-slice_fusion.14), channel_id=1, source_target_pairs={{0,2},{2,0},{4,6},{6,4},{8,10},{10,8},{12,14},{14,12},{16,18},{18,... | collective-permute-start | bytes 1720328 | tf_op jit(solution)/shard_map/ppermute | solution.py:19
  2.7 49.1 %collective-permute-start.8 = (bf16[1,256,4096]{2,1,0:T(8,128)(2,1)}, bf16[1,256,4096]{2,1,0:T(8,128)(2,1)}, u32[]{:S(2)}, u32[]{:S(2)}) collective-permute-start(bf16[1,256,4096]{2,1,0:T(8,128)(2,1)} %bitcast.60), channel_id=1, source_target_pairs={{0,1},{1,0},{2,3},{3,2},{4,5},{5,4},{6,7},{7,6},{8,9},{9,8},{10,11... | collective-permute-start | bytes 6291464 | tf_op jit(solution)/shard_map/ppermute | solution.py:19
  8.0 55.4 %copy-start = (bf16[1632,512]{1,0:T(8,128)(2,1)}, bf16[1632,512]{1,0:T(8,128)(2,1)S(1)}, u32[]{:S(2)}) copy-start(bf16[1632,512]{1,0:T(8,128)(2,1)S(1)} %pad_maximum_fusion.refs_0_) | copy-start | bytes 5013508
  8.0 3.7 %collective-permute-start.3 = (bf16[1632,512]{1,0:T(8,128)(2,1)S(1)}, bf16[1632,512]{1,0:T(8,128)(2,1)}, u32[]{:S(2)}, u32[]{:S(2)}) collective-permute-start(bf16[1632,512]{1,0:T(8,128)(2,1)S(1)} %pad_maximum_fusion.refs_0_), channel_id=1, source_target_pairs={{0,2},{2,0},{4,6},{6,4},{8,10},{10,8},{12,14},{14,12},{16,18},{18,... | collective-permute-start | bytes 5013512 | tf_op jit(solution)/shard_map/ppermute | solution.py:19
  8.2 38.8 %collective-permute-start.2 = (bf16[1632,512]{1,0:T(8,128)(2,1)S(1)}, bf16[1632,512]{1,0:T(8,128)(2,1)S(1)}, u32[]{:S(2)}, u32[]{:S(2)}) collective-permute-start(bf16[1632,512]{1,0:T(8,128)(2,1)S(1)} %pad_maximum_fusion.refs_0_), channel_id=1, source_target_pairs={{8,0},{16,8},{24,16},{28,24},{20,28},{12,20},{4,12},{0,4},{2,10},{... | collective-permute-start | bytes 5013512 | tf_op jit(solution)/shard_map/ppermute | solution.py:537
  9.8 37.3 %collective-permute-start.1 = (bf16[1632,512]{1,0:T(8,128)(2,1)S(1)}, bf16[1632,512]{1,0:T(8,128)(2,1)}, u32[]{:S(2)}, u32[]{:S(2)}) collective-permute-start(bf16[1632,512]{1,0:T(8,128)(2,1)S(1)} %pad_maximum_fusion.refs_0_), channel_id=1, source_target_pairs={{0,8},{8,16},{16,24},{24,28},{28,20},{20,12},{12,4},{4,0},{10,2},{... | collective-permute-start | bytes 5013512 | tf_op jit(solution)/shard_map/ppermute | solution.py:537
  47.0 16.4 %copy-start.2 = (bf16[1632,512]{1,0:T(8,128)(2,1)}, bf16[1632,512]{1,0:T(8,128)(2,1)S(1)}, u32[]{:S(2)}) copy-start(bf16[1632,512]{1,0:T(8,128)(2,1)S(1)} %collective-permute-done.2.refs_2_) | copy-start | bytes 5013508
  47.1 9.6 %collective-permute-start.7 = (bf16[1632,512]{1,0:T(8,128)(2,1)}, bf16[1632,512]{1,0:T(8,128)(2,1)}, u32[]{:S(2)}, u32[]{:S(2)}) collective-permute-start(bf16[1632,512]{1,0:T(8,128)(2,1)} %collective-permute-done.1.refs_1_), channel_id=1, source_target_pairs={{0,2},{2,0},{4,6},{6,4},{8,10},{10,8},{12,14},{14,12},{16,18},{18,... | collective-permute-start | bytes 5013512 | tf_op jit(solution)/shard_map/ppermute | solution.py:19
  47.8 8.9 %collective-permute-start.6 = (bf16[1632,512]{1,0:T(8,128)(2,1)S(1)}, bf16[1632,512]{1,0:T(8,128)(2,1)}, u32[]{:S(2)}, u32[]{:S(2)}) collective-permute-start(bf16[1632,512]{1,0:T(8,128)(2,1)S(1)} %collective-permute-done.2.refs_2_), channel_id=1, source_target_pairs={{0,2},{2,0},{4,6},{6,4},{8,10},{10,8},{12,14},{14,12},{16,18},{18,... | collective-permute-start | bytes 5013512 | tf_op jit(solution)/shard_map/ppermute | solution.py:19
  47.8 39.7 %collective-permute-start.4 = (bf16[1632,512]{1,0:T(8,128)(2,1)}, bf16[1632,512]{1,0:T(8,128)(2,1)}, u32[]{:S(2)}, u32[]{:S(2)}) collective-permute-start(bf16[1632,512]{1,0:T(8,128)(2,1)} %collective-permute-done.1.refs_1_), channel_id=1, source_target_pairs={{0,8},{8,16},{16,24},{24,28},{28,20},{20,12},{12,4},{4,0},{10,2},{... | collective-permute-start | bytes 5013512 | tf_op jit(solution)/shard_map/ppermute | solution.py:537
  49.4 38.1 %collective-permute-start.5 = (bf16[1632,512]{1,0:T(8,128)(2,1)S(1)}, bf16[1632,512]{1,0:T(8,128)(2,1)}, u32[]{:S(2)}, u32[]{:S(2)}) collective-permute-start(bf16[1632,512]{1,0:T(8,128)(2,1)S(1)} %collective-permute-done.2.refs_2_), channel_id=1, source_target_pairs={{8,0},{16,8},{24,16},{28,24},{20,28},{12,20},{4,12},{0,4},{2,10},{... | collective-permute-start | bytes 5013512 | tf_op jit(solution)/shard_map/ppermute | solution.py:537
  87.5 19.1 %collective-permute-start.12 = (bf16[1632,512]{1,0:T(8,128)(2,1)}, bf16[1632,512]{1,0:T(8,128)(2,1)}, u32[]{:S(2)}, u32[]{:S(2)}) collective-permute-start(bf16[1632,512]{1,0:T(8,128)(2,1)} %collective-permute-done.4.refs_0_.refs_3_), channel_id=1, source_target_pairs={{0,2},{2,0},{4,6},{6,4},{8,10},{10,8},{12,14},{14,12},{16,18},{18,... | collective-permute-start | bytes 5013512 | tf_op jit(solution)/shard_map/ppermute | solution.py:19
  87.6 19.0 %collective-permute-start.11 = (bf16[1632,512]{1,0:T(8,128)(2,1)}, bf16[1632,512]{1,0:T(8,128)(2,1)S(1)}, u32[]{:S(2)}, u32[]{:S(2)}) collective-permute-start(bf16[1632,512]{1,0:T(8,128)(2,1)} %collective-permute-done.5.refs_1_.refs_4_), channel_id=1, source_target_pairs={{0,2},{2,0},{4,6},{6,4},{8,10},{10,8},{12,14},{14,12},{16,18},{18,... | collective-permute-start | bytes 5013512 | tf_op jit(solution)/shard_map/ppermute | solution.py:19
  88.0 39.4 %collective-permute-start.9 = (bf16[1632,512]{1,0:T(8,128)(2,1)}, bf16[1632,512]{1,0:T(8,128)(2,1)S(1)}, u32[]{:S(2)}, u32[]{:S(2)}) collective-permute-start(bf16[1632,512]{1,0:T(8,128)(2,1)} %collective-permute-done.4.refs_0_.refs_3_), channel_id=1, source_target_pairs={{0,8},{8,16},{16,24},{24,28},{28,20},{20,12},{12,4},{4,0},{10,2},{... | collective-permute-start | bytes 5013512 | tf_op jit(solution)/shard_map/ppermute | solution.py:537
  89.2 38.3 %collective-permute-start.10 = (bf16[1632,512]{1,0:T(8,128)(2,1)}, bf16[1632,512]{1,0:T(8,128)(2,1)}, u32[]{:S(2)}, u32[]{:S(2)}) collective-permute-start(bf16[1632,512]{1,0:T(8,128)(2,1)} %collective-permute-done.5.refs_1_.refs_4_), channel_id=1, source_target_pairs={{8,0},{16,8},{24,16},{28,24},{20,28},{12,20},{4,12},{0,4},{2,10},{... | collective-permute-start | bytes 5013512 | tf_op jit(solution)/shard_map/ppermute | solution.py:537
  90.0 13.7 %collective-permute-start.14 = (bf16[1,512,512]{2,1,0:T(8,128)(2,1)}, bf16[1,512,512]{2,1,0:T(8,128)(2,1)}, u32[]{:S(2)}, u32[]{:S(2)}) collective-permute-start(bf16[1,512,512]{2,1,0:T(8,128)(2,1)} %bitcast.72), channel_id=1, source_target_pairs={{0,1},{1,0},{2,3},{3,2},{4,5},{5,4},{6,7},{7,6},{8,9},{9,8},{10,11... | collective-permute-start | bytes 1572872 | tf_op jit(solution)/shard_map/ppermute | solution.py:19
  103.7 14.3 %collective-permute-start.13 = (bf16[240,256]{1,0:T(8,128)(2,1)S(1)}, bf16[240,256]{1,0:T(8,128)(2,1)S(1)}, u32[]{:S(2)}, u32[]{:S(2)}) collective-permute-start(bf16[240,256]{1,0:T(8,128)(2,1)S(1)} %convert_element_type.34), channel_id=1, source_target_pairs={{0,1},{1,0},{2,3},{3,2},{4,5},{5,4},{6,7},{7,6},{8,9},{9,8},{10,11... | collective-permute-start | bytes 368648 | tf_op jit(solution)/shard_map/ppermute | solution.py:19
  106.6 6.2 %copy-start.8 = (f32[512,256]{1,0:T(8,128)S(1)}, f32[512,256]{1,0:T(8,128)}, u32[]{:S(2)}) copy-start(f32[512,256]{1,0:T(8,128)} %copy-done.7) | copy-start | bytes 1572868
  106.6 6.2 %copy-start.3 = (bf16[1632,512]{1,0:T(8,128)(2,1)}, bf16[1632,512]{1,0:T(8,128)(2,1)S(1)}, u32[]{:S(2)}) copy-start(bf16[1632,512]{1,0:T(8,128)(2,1)S(1)} %collective-permute-done.11.refs_2_.refs_11_) | copy-start | bytes 5013508
  127.4 11.3 %copy-start.1 = (bf16[1632,512]{1,0:T(8,128)(2,1)}, bf16[1632,512]{1,0:T(8,128)(2,1)S(1)}, u32[]{:S(2)}) copy-start(bf16[1632,512]{1,0:T(8,128)(2,1)S(1)} %collective-permute-done.9.refs_0_.refs_5_) | copy-start | bytes 5013508
  127.4 5.1 %collective-permute-start.16 = (bf16[1632,512]{1,0:T(8,128)(2,1)}, bf16[1632,512]{1,0:T(8,128)(2,1)S(1)}, u32[]{:S(2)}, u32[]{:S(2)}) collective-permute-start(bf16[1632,512]{1,0:T(8,128)(2,1)} %collective-permute-done.10.refs_1_.refs_6_), channel_id=1, source_target_pairs={{0,2},{2,0},{4,6},{6,4},{8,10},{10,8},{12,14},{14,12},{16,18},{18,... | collective-permute-start | bytes 5013512 | tf_op jit(solution)/shard_map/ppermute | solution.py:19
  127.6 6.0 %collective-permute-start.17 = (bf16[1632,512]{1,0:T(8,128)(2,1)S(1)}, bf16[1632,512]{1,0:T(8,128)(2,1)}, u32[]{:S(2)}, u32[]{:S(2)}) collective-permute-start(bf16[1632,512]{1,0:T(8,128)(2,1)S(1)} %collective-permute-done.9.refs_0_.refs_5_), channel_id=1, source_target_pairs={{0,2},{2,0},{4,6},{6,4},{8,10},{10,8},{12,14},{14,12},{16,18},{18,... | collective-permute-start | bytes 5013512 | tf_op jit(solution)/shard_map/ppermute | solution.py:19
  129.0 16.2 %collective-permute-start.15 = (bf16[1120,512]{1,0:T(8,128)(2,1)}, bf16[1120,512]{1,0:T(8,128)(2,1)}, u32[]{:S(2)}, u32[]{:S(2)}) collective-permute-start(bf16[1120,512]{1,0:T(8,128)(2,1)} %slice.125), channel_id=1, source_target_pairs={{0,8},{8,16},{16,24},{24,28},{28,20},{20,12},{12,4},{4,0},{10,2},{... | collective-permute-start | bytes 3440648 | tf_op jit(solution)/shard_map/ppermute | solution.py:553
  130.7 12.9 %collective-permute-start.18 = (bf16[160,256]{1,0:T(8,128)(2,1)}, bf16[160,256]{1,0:T(8,128)(2,1)}, u32[]{:S(2)}, u32[]{:S(2)}) collective-permute-start(bf16[160,256]{1,0:T(8,128)(2,1)} %convert_element_type.35), channel_id=1, source_target_pairs={{0,1},{1,0},{2,3},{3,2},{4,5},{5,4},{6,7},{7,6},{8,9},{9,8},{10,11... | collective-permute-start | bytes 245768 | tf_op jit(solution)/shard_map/ppermute | solution.py:19
  131.5 7.2 %copy-start.10 = (f32[512,256]{1,0:T(8,128)S(1)}, f32[512,256]{1,0:T(8,128)}, u32[]{:S(2)}) copy-start(f32[512,256]{1,0:T(8,128)} %copy-done.9) | copy-start | bytes 1572868
  132.5 6.2 %copy-start.4 = (bf16[1632,512]{1,0:T(8,128)(2,1)}, bf16[1632,512]{1,0:T(8,128)(2,1)S(1)}, u32[]{:S(2)}) copy-start(bf16[1632,512]{1,0:T(8,128)(2,1)S(1)} %collective-permute-done.16.refs_2_.refs_13_) | copy-start | bytes 5013508
  138.7 7.5 %copy-start.13 = (f32[160,256]{1,0:T(8,128)}, f32[160,256]{1,0:T(8,128)S(1)}, u32[]{:S(2)}) copy-start(f32[160,256]{1,0:T(8,128)S(1)} %project_acts.6.refs_2_) | copy-start | bytes 491524
  145.2 3.0 %collective-permute-start.20 = (bf16[1120,512]{1,0:T(8,128)(2,1)}, bf16[1120,512]{1,0:T(8,128)(2,1)S(1)}, u32[]{:S(2)}, u32[]{:S(2)}) collective-permute-start(bf16[1120,512]{1,0:T(8,128)(2,1)} %collective-permute-done.15.refs_0_.refs_7_), channel_id=1, source_target_pairs={{0,2},{2,0},{4,6},{6,4},{8,10},{10,8},{12,14},{14,12},{16,18},{18,... | collective-permute-start | bytes 3440648 | tf_op jit(solution)/shard_map/ppermute | solution.py:19
  145.2 9.2 %collective-permute-start.19 = (bf16[512,512]{1,0:T(8,128)(2,1)S(1)}, bf16[512,512]{1,0:T(8,128)(2,1)S(1)}, u32[]{:S(2)}, u32[]{:S(2)}) collective-permute-start(bf16[512,512]{1,0:T(8,128)(2,1)S(1)} %slice.124), channel_id=1, source_target_pairs={{0,8},{8,16},{16,24},{24,28},{28,20},{20,12},{12,4},{4,0},{10,2},{... | collective-permute-start | bytes 1572872 | tf_op jit(solution)/shard_map/ppermute | solution.py:559
  146.3 10.0 %copy-start.12 = (f32[512,256]{1,0:T(8,128)S(1)}, f32[512,256]{1,0:T(8,128)}, u32[]{:S(2)}) copy-start(f32[512,256]{1,0:T(8,128)} %copy-done.11) | copy-start | bytes 1572868
  146.3 6.7 %collective-permute-start.21 = (bf16[160,256]{1,0:T(8,128)(2,1)S(1)}, bf16[160,256]{1,0:T(8,128)(2,1)S(1)}, u32[]{:S(2)}, u32[]{:S(2)}) collective-permute-start(bf16[160,256]{1,0:T(8,128)(2,1)S(1)} %convert_element_type.36), channel_id=1, source_target_pairs={{0,1},{1,0},{2,3},{3,2},{4,5},{5,4},{6,7},{7,6},{8,9},{9,8},{10,11... | collective-permute-start | bytes 245768 | tf_op jit(solution)/shard_map/ppermute | solution.py:19
  154.4 1.9 collective-permute-start.22
  154.4 4.2 %collective-permute-start.23 = (bf16[80,256]{1,0:T(8,128)(2,1)S(1)}, bf16[80,256]{1,0:T(8,128)(2,1)S(1)}, u32[]{:S(2)}, u32[]{:S(2)}) collective-permute-start(bf16[80,256]{1,0:T(8,128)(2,1)S(1)} %convert_element_type.37), channel_id=1, source_target_pairs={{0,1},{1,0},{2,3},{3,2},{4,5},{5,4},{6,7},{7,6},{8,9},{9,8},{10,11... | collective-permute-start | bytes 122888 | tf_op jit(solution)/shard_map/ppermute | solution.py:19
  155.2 3.4 %copy-start.14 = (f32[160,256]{1,0:T(8,128)S(1)}, f32[160,256]{1,0:T(8,128)}, u32[]{:S(2)}) copy-start(f32[160,256]{1,0:T(8,128)} %copy-done.13) | copy-start | bytes 491524
  155.2 3.4 %copy-start.16 = (bf16[240,256]{1,0:T(8,128)(2,1)S(1)}, bf16[240,256]{1,0:T(8,128)(2,1)}, u32[]{:S(2)}) copy-start(bf16[240,256]{1,0:T(8,128)(2,1)} %copy-done.15) | copy-start | bytes 368644
  160.0 2.2 collective-permute-start.24
  162.6 6.3 %collective-permute-start.25 = (bf16[2,64,640]{2,1,0:T(8,128)(2,1)S(1)}, bf16[2,64,640]{2,1,0:T(8,128)(2,1)S(1)}, u32[]{:S(2)}, u32[]{:S(2)}) collective-permute-start(bf16[2,64,640]{2,1,0:T(8,128)(2,1)S(1)} %get-tuple-element.66), channel_id=1, source_target_pairs={{0,4},{2,6},{4,0},{6,2},{8,12},{10,14},{12,8},{14,10},{16,20},{18,... | collective-permute-start | bytes 491528 | tf_op jit(solution)/shard_map/ppermute | solution.py:19
  163.8 7.1 %collective-permute-start.26 = (bf16[2,64,640]{2,1,0:T(8,128)(2,1)S(1)}, bf16[2,64,640]{2,1,0:T(8,128)(2,1)S(1)}, u32[]{:S(2)}, u32[]{:S(2)}) collective-permute-start(bf16[2,64,640]{2,1,0:T(8,128)(2,1)S(1)} %get-tuple-element.67), channel_id=1, source_target_pairs={{0,8},{2,10},{4,12},{6,14},{8,0},{10,2},{12,4},{14,6},{16,24},{18,... | collective-permute-start | bytes 491528 | tf_op jit(solution)/shard_map/ppermute | solution.py:19
  165.2 8.3 %collective-permute-start.27 = (bf16[2,64,640]{2,1,0:T(8,128)(2,1)S(1)}, bf16[2,64,640]{2,1,0:T(8,128)(2,1)S(1)}, u32[]{:S(2)}, u32[]{:S(2)}) collective-permute-start(bf16[2,64,640]{2,1,0:T(8,128)(2,1)S(1)} %get-tuple-element.68), channel_id=1, source_target_pairs={{0,12},{2,14},{4,8},{6,10},{8,4},{10,6},{12,0},{14,2},{16,28},{18,... | collective-permute-start | bytes 491528 | tf_op jit(solution)/shard_map/ppermute | solution.py:19
  173.7 9.6 %collective-permute-start.28 = (bf16[2,64,640]{2,1,0:T(8,128)(2,1)S(1)}, bf16[2,64,640]{2,1,0:T(8,128)(2,1)S(1)}, u32[]{:S(2)}, u32[]{:S(2)}) collective-permute-start(bf16[2,64,640]{2,1,0:T(8,128)(2,1)S(1)} %fusion.2), channel_id=1, source_target_pairs={{0,16},{2,18},{4,20},{6,22},{8,24},{10,26},{12,28},{14,30},{16,0},... | collective-permute-start | bytes 491528 | tf_op jit(solution)/shard_map/ppermute | solution.py:19
  176.4 20.9 %copy-start.17 = (bf16[2,512,512]{2,1,0:T(8,128)(2,1)S(1)}, bf16[2,512,512]{2,1,0:T(8,128)(2,1)}, u32[]{:S(2)}) copy-start(bf16[2,512,512]{2,1,0:T(8,128)(2,1)} %pad_maximum_fusion.2) | copy-start | bytes 3145732
  183.4 4.5 %collective-permute-start.29 = (bf16[1,64,640]{2,1,0:T(8,128)(2,1)S(1)}, bf16[1,64,640]{2,1,0:T(8,128)(2,1)S(1)}, u32[]{:S(2)}, u32[]{:S(2)}) collective-permute-start(bf16[1,64,640]{2,1,0:T(8,128)(2,1)S(1)} %get-tuple-element.81), channel_id=1, source_target_pairs={{0,1},{1,0},{2,3},{3,2},{4,5},{5,4},{6,7},{7,6},{8,9},{9,8},{10,11... | collective-permute-start | bytes 245768 | tf_op jit(solution)/shard_map/ppermute | solution.py:19
  187.9 6.2 %collective-permute-start.31 = (bf16[2,64,640]{2,1,0:T(8,128)(2,1)S(1)}, bf16[2,64,640]{2,1,0:T(8,128)(2,1)S(1)}, u32[]{:S(2)}, u32[]{:S(2)}) collective-permute-start(bf16[2,64,640]{2,1,0:T(8,128)(2,1)S(1)} %get-tuple-element.83), channel_id=1, source_target_pairs={{0,8},{2,10},{4,12},{6,14},{8,0},{10,2},{12,4},{14,6},{16,24},{18,... | collective-permute-start | bytes 491528 | tf_op jit(solution)/shard_map/ppermute | solution.py:19
  188.0 6.3 %collective-permute-start.30 = (bf16[2,64,640]{2,1,0:T(8,128)(2,1)S(1)}, bf16[2,64,640]{2,1,0:T(8,128)(2,1)S(1)}, u32[]{:S(2)}, u32[]{:S(2)}) collective-permute-start(bf16[2,64,640]{2,1,0:T(8,128)(2,1)S(1)} %get-tuple-element.83), channel_id=1, source_target_pairs={{0,4},{2,6},{4,0},{6,2},{8,12},{10,14},{12,8},{14,10},{16,20},{18,... | collective-permute-start | bytes 491528 | tf_op jit(solution)/shard_map/ppermute | solution.py:19
  189.3 7.8 %collective-permute-start.32 = (bf16[2,64,640]{2,1,0:T(8,128)(2,1)S(1)}, bf16[2,64,640]{2,1,0:T(8,128)(2,1)S(1)}, u32[]{:S(2)}, u32[]{:S(2)}) collective-permute-start(bf16[2,64,640]{2,1,0:T(8,128)(2,1)S(1)} %get-tuple-element.83), channel_id=1, source_target_pairs={{0,12},{2,14},{4,8},{6,10},{8,4},{10,6},{12,0},{14,2},{16,28},{18,... | collective-permute-start | bytes 491528 | tf_op jit(solution)/shard_map/ppermute | solution.py:19
  191.7 5.6 %collective-permute-start.33 = (f32[64,320]{1,0:T(8,128)S(1)}, f32[64,320]{1,0:T(8,128)S(1)}, u32[]{:S(2)}, u32[]{:S(2)}) collective-permute-start(f32[64,320]{1,0:T(8,128)S(1)} %dynamic-slice_bitcast_fusion.2), channel_id=1, source_target_pairs={{0,0},{2,2},{4,4},{6,6},{8,8},{10,10},{12,12},{14,14},{16,1},{18,3... | collective-permute-start | bytes 245768 | tf_op jit(solution)/shard_map/ppermute | solution.py:478
  197.3 2.2 collective-permute-start.34
  (6 other events, 7.1 us)

commit v6 on v5

--- a/solution.py
+++ b/solution.py
@@ -389,9 +389,10 @@
     rotated, squares = products(picked(me_ref, g_ref, 0), a_ref[...])
     rotated += got_ref[0].astype(F32)
     squares += got_ref[1].astype(F32)
-    for r, out_ref in enumerate(out_refs):
-        out_ref[0] = rotated[r * width : (r + 1) * width].astype(BF16)
-        out_ref[1] = squares[r * width : (r + 1) * width].astype(BF16)
+    pairs = len(out_refs) // 2
+    for r in range(pairs):
+        out_refs[r][...] = rotated[r * width : (r + 1) * width].astype(BF16)
+        out_refs[pairs + r][...] = squares[r * width : (r + 1) * width].astype(BF16)
 
 
 def token_sums(grad_proj_t, sums, gots, order, pair_rows):
@@ -428,8 +429,8 @@
         ours = pl.pallas_call(
             ours_kernel,
             in_specs=[index_spec, whole, whole, whole],
-            out_specs=[whole] * pairs,
-            out_shape=[jax.ShapeDtypeStruct((2, width, rows), BF16)] * pairs,
+            out_specs=[whole] * (2 * pairs),
+            out_shape=[jax.ShapeDtypeStruct((width, rows), BF16)] * (2 * pairs),
             compiler_params=params,
             cost_estimate=cost,
             name="sums_for_own_core",
@@ -444,12 +445,14 @@
         near = near.transpose(1, 0, 2, 3).reshape((2 * pairs * width, tokens))
         both = jnp.stack(products(near, act_proj_t)).reshape((2, 2, pairs, width, rows))
         total = both[:, 0] + flip(both[:, 1].astype(BF16), "dp", 1).astype(F32)
-        ours = [total[:, r].astype(BF16) for r in range(pairs)]
-    total = ours[0].astype(F32)
-    for r in range(1, pairs):
-        total += flip(ours[r], "dp", 2 * r).astype(F32)
-    total += flip(total.astype(BF16), "dp", blocks).astype(F32)
-    return total[0], total[1]
+        ours = [total[part, r].astype(BF16) for part in range(2) for r in range(pairs)]
+    totals = []
+    for part in (ours[:pairs], ours[pairs:]):
+        total = part[0].astype(F32)
+        for r in range(1, pairs):
+            total += flip(part[r], "dp", 2 * r).astype(F32)
+        totals.append(total + flip(total.astype(BF16), "dp", blocks).astype(F32))
+    return totals[0], totals[1]
 
 
 def gather_scaled(scaled, diag):

time: 219 us -> 217 us (level)
  waiting for transfers between devices: 111 us -> 104 us
  starting transfers between devices: 27.5 us -> 32.4 us
    ppermute x26 -> x30, waiting for transfers between devices: 45.7 us -> 38.2 us  [flip(): return lax.ppermute(x, axis_name, [(i, i ^ bit) for i in range(size)])]
    ppermute x26 -> x30, starting transfers between devices: 18.5 us -> 23.3 us  [flip(): return lax.ppermute(x, axis_name, [(i, i ^ bit) for i in range(size)])]
  transfers between devices with their start and end apart: 35 -> 39, of which waited for: 23 -> 23; matrix products, arithmetic and copies ran while one was open for 6% -> 7% of each run, Pallas kernels for 17% -> 18%
where the time goes in v6:
time: 217 us; the launch traced here: 215 us
  waiting for transfers between devices  104 us (48%)
  Pallas kernels  56.6 us (26%)
  starting transfers between devices  32.4 us (15%)
  other arithmetic  11.2 us (5%)
  local copies, waits for them, and re-layouts  8.78 us (4%)
    ppermute x6, waiting for transfers between devices, on_device(): moving = [lax.ppermute(x, 'dp', everyone[k]) for k, x in enumerate(moving)]  62.4 us
    ppermute x30, waiting for transfers between devices, flip(): return lax.ppermute(x, axis_name, [(i, i ^ bit) for i in range(size)])  38.2 us
    ppermute x30, starting transfers between devices, flip(): return lax.ppermute(x, axis_name, [(i, i ^ bit) for i in range(size)])  23.3 us
    pallas_call x4, Pallas kernels, project(): pl.pallas_call(functools.partial(project_kernel, tiles, rows), grid_spec=...  22 us
    pallas_call x1, Pallas kernels, expand(): pl.pallas_call(functools.partial(expand_kernel, tiles, rows), grid_spec=p...  17.1 us
    pallas_call x4, Pallas kernels, add_grads(): pl.pallas_call(functools.partial(add_grads_kernel, apart), grid_spec=pltp...  15.8 us
    ppermute x6, starting transfers between devices, on_device(): moving = [lax.ppermute(x, 'dp', everyone[k]) for k, x in enumerate(moving)]  6.08 us
    unnamed x66, local copies, waits for them, and re-layouts  5.53 us
  transfers between devices with their start and end apart: 39, of which 23 were waited for; matrix products, arithmetic and copies ran while one was open for 7% of the time, Pallas kernels for 18%

profile of v6, /device:TPU:0, one launch (start us, length us, event | category | flops | bytes accessed | tf_op | source)
XLA Modules:
  0.0 214.5 jit_solution(14495732908207761275)
XLA Ops:
  0.7 1.4 dynamic-slice_bitcast_fusion.1
  2.7 2.6 %collective-permute-start.8 = (bf16[1,256,4096]{2,1,0:T(8,128)(2,1)}, bf16[1,256,4096]{2,1,0:T(8,128)(2,1)}, u32[]{:S(2)}, u32[]{:S(2)}) collective-permute-start(bf16[1,256,4096]{2,1,0:T(8,128)(2,1)} %bitcast.60), channel_id=1, source_target_pairs={{0,1},{1,0},{2,3},{3,2},{4,5},{5,4},{6,7},{7,6},{8,9},{9,8},{10,11... | collective-permute-start | bytes 6291464 | tf_op jit(solution)/shard_map/ppermute | solution.py:19
  6.8 1.2 pad_maximum_fusion.refs_0_
  8.2 1.5 collective-permute-start.2
  10.2 1.5 collective-permute-done.3.refs_3_.refs_8_
  11.7 35.2 %collective-permute-done.2.refs_2_ = bf16[1632,512]{1,0:T(8,128)(2,1)S(1)} collective-permute-done((bf16[1632,512]{1,0:T(8,128)(2,1)S(1)}, bf16[1632,512]{1,0:T(8,128)(2,1)S(1)}, u32[]{:S(2)}, u32[]{:S(2)}) %collective-permute-start.2) | collective-permute-done | bytes 1671200 | tf_op jit(solution)/shard_map/ppermute | solution.py:540
  47.8 1.6 collective-permute-start.4
  49.9 1.9 collective-permute-done.8
  51.8 2.5 %select_bitcast_fusion.1 = (bf16[1,1,256,4096]{3,2,1,0:T(8,128)(2,1)S(1)}, bf16[1,1,256,4096]{3,2,1,0:T(8,128)(2,1)S(1)}) fusion(bf16[1,256,4096]{2,1,0:T(8,128)(2,1)} %collective-permute-done.8, pred[]{:T(512)S(6)} %eq.57, bf16[256,4096]{1,0:T(8,128)(2,1)} %param.6), kind=kLoop, calls=%fused_computation.2 | loop fusion | flops 2097152 | bytes 8388609 | tf_op jit(solution)/shard_map/stack | solution.py:36
  54.3 2.4 %maximum_bitcast_fusion.refs_6_.refs_7_.refs_8_.refs_9_.refs_10_.refs_11_.refs_4_.refs_5_.refs_2_.refs_3_ = bf16[2,256,4096]{2,1,0:T(8,128)(2,1)} fusion(bf16[1,1,256,4096]{3,2,1,0:T(8,128)(2,1)S(1)} %get-tuple-element.85, bf16[1,1,256,4096]{3,2,1,0:T(8,128)(2,1)S(1)} %get-tuple-element.84), kind=kLoop, calls=%fused_computation | loop fusion | flops 2097152 | bytes 8388608 | tf_op jit(solution)/shard_map/reshape | solution.py:36
  56.7 5.9 %project_acts.4.refs_0_ = f32[240,256]{1,0:T(8,128)S(1)} custom-call(s32[1]{0:T(128)} %bitcast.at_ref, bf16[256,14336]{1,0:T(8,128)(2,1)} %acts_ref.7, bf16[1632,512]{1,0:T(8,128)(2,1)S(1)} %pad_maximum_fusion.refs_0_, bf16[1632,512]{1,0:T(8,128)(2,1)} %collective-permute-done.1.refs_1_, bf16[1632,512]{1,0:T(8,128)(2,1)S(1)} %collective-permute-done.2.refs_2_, ...), custom_call_target="tpu_custom_call" | custom-call | flops 1 | bytes 1 | tf_op jit(solution)/shard_map/project_acts/pallas_call | solution.py:123
  63.4 5.0 %add_grads.4.refs_8_ = f32[512,256]{1,0:T(8,128)S(1)} custom-call(s32[12]{0:T(128)S(1)} %stack.332.at_ref, bf16[1632,512]{1,0:T(8,128)(2,1)S(1)} %pad_maximum_fusion.refs_0_, bf16[1632,512]{1,0:T(8,128)(2,1)} %collective-permute-done.1.refs_1_, bf16[1632,512]{1,0:T(8,128)(2,1)S(1)} %collective-permute-done.2.refs_2_, ...), custom_call_target="tpu_custom_call" | custom-call | flops 1 | bytes 1 | tf_op jit(solution)/shard_map/add_grads/pallas_call | solution.py:185
  69.2 18.3 %collective-permute-done.4.refs_0_.refs_3_ = bf16[1632,512]{1,0:T(8,128)(2,1)} collective-permute-done((bf16[1632,512]{1,0:T(8,128)(2,1)}, bf16[1632,512]{1,0:T(8,128)(2,1)}, u32[]{:S(2)}, u32[]{:S(2)}) %collective-permute-start.4) | collective-permute-done | bytes 1671200 | tf_op jit(solution)/shard_map/ppermute | solution.py:540
  88.0 1.1 collective-permute-start.9
  91.7 12.0 %collective-permute-done.14 = bf16[1,512,512]{2,1,0:T(8,128)(2,1)} collective-permute-done((bf16[1,512,512]{2,1,0:T(8,128)(2,1)}, bf16[1,512,512]{2,1,0:T(8,128)(2,1)}, u32[]{:S(2)}, u32[]{:S(2)}) %collective-permute-start.14) | collective-permute-done | bytes 524320 | tf_op jit(solution)/shard_map/ppermute | solution.py:19
  104.4 2.3 %pad_maximum_fusion.2 = bf16[2,512,512]{2,1,0:T(8,128)(2,1)} fusion(bf16[1,512,512]{2,1,0:T(8,128)(2,1)} %collective-permute-done.14, bf16[1,512,512]{2,1,0:T(8,128)(2,1)} %bitcast.72), kind=kLoop, calls=%fused_computation.9 | loop fusion | flops 524288 | bytes 2097152 | tf_op jit(solution)/shard_map/concatenate | solution.py:339
  106.7 6.2 %project_acts.5.refs_1_ = f32[160,256]{1,0:T(8,128)S(1)} custom-call(s32[1]{0:T(128)} %bitcast.at_ref, bf16[256,14336]{1,0:T(8,128)(2,1)} %acts_ref.7, bf16[1632,512]{1,0:T(8,128)(2,1)} %collective-permute-done.4.refs_0_.refs_3_, bf16[1632,512]{1,0:T(8,128)(2,1)} %collective-permute-done.5.refs_1_.refs_4_, ...), custom_call_target="tpu_custom_call" | custom-call | flops 1 | bytes 1 | tf_op jit(solution)/shard_map/project_acts/pallas_call | solution.py:123
  112.9 4.4 %add_grads.5.refs_8_ = f32[512,256]{1,0:T(8,128)S(1)} custom-call(s32[8]{0:T(128)S(1)} %stack.344.at_ref, bf16[1632,512]{1,0:T(8,128)(2,1)} %collective-permute-done.4.refs_0_.refs_3_, bf16[1632,512]{1,0:T(8,128)(2,1)} %collective-permute-done.5.refs_1_.refs_4_, bf16[1632,512]{1,0:T(8,128)(2,1)S(1)} %collective-permute-done.11.refs_2_.refs_11_, ...), custom_call_target="tpu_custom_call" | custom-call | flops 1 | bytes 1 | tf_op jit(solution)/shard_map/add_grads/pallas_call | solution.py:185
  118.7 8.7 %collective-permute-done.9.refs_0_.refs_5_ = bf16[1632,512]{1,0:T(8,128)(2,1)S(1)} collective-permute-done((bf16[1632,512]{1,0:T(8,128)(2,1)}, bf16[1632,512]{1,0:T(8,128)(2,1)S(1)}, u32[]{:S(2)}, u32[]{:S(2)}) %collective-permute-start.9) | collective-permute-done | bytes 1671200 | tf_op jit(solution)/shard_map/ppermute | solution.py:540
  127.9 1.1 slice.119
  129.0 1.1 collective-permute-start.15
  133.5 5.2 %project_acts.6.refs_2_ = f32[160,256]{1,0:T(8,128)S(1)} custom-call(s32[1]{0:T(128)} %bitcast.at_ref, bf16[256,14336]{1,0:T(8,128)(2,1)} %acts_ref.7, bf16[1632,512]{1,0:T(8,128)(2,1)S(1)} %collective-permute-done.9.refs_0_.refs_5_, bf16[1632,512]{1,0:T(8,128)(2,1)} %collective-permute-done.10.refs_1_.refs_6_, ...), custom_call_target="tpu_custom_call" | custom-call | flops 1 | bytes 1 | tf_op jit(solution)/shard_map/project_acts/pallas_call | solution.py:123
  138.7 4.1 %add_grads.6.refs_4_ = f32[512,256]{1,0:T(8,128)S(1)} custom-call(s32[8]{0:T(128)S(1)} %stack.353.at_ref, bf16[1632,512]{1,0:T(8,128)(2,1)S(1)} %collective-permute-done.9.refs_0_.refs_5_, bf16[1632,512]{1,0:T(8,128)(2,1)} %collective-permute-done.10.refs_1_.refs_6_, bf16[1632,512]{1,0:T(8,128)(2,1)S(1)} %collective-permute-done.16.refs_2_.refs_13_, ...), custom_call_target="tpu_custom_call" | custom-call | flops 1 | bytes 1 | tf_op jit(solution)/shard_map/add_grads/pallas_call | solution.py:185
  143.6 1.5 collective-permute-done.15.refs_0_.refs_7_
  145.2 1.1 collective-permute-start.19
  147.0 1.2 collective-permute-done.20.refs_1_.refs_15_
  148.2 4.7 %project_acts.7.refs_3_ = f32[80,256]{1,0:T(8,128)S(1)} custom-call(s32[1]{0:T(128)} %bitcast.at_ref, bf16[256,14336]{1,0:T(8,128)(2,1)} %acts_ref.7, bf16[1120,512]{1,0:T(8,128)(2,1)} %collective-permute-done.15.refs_0_.refs_7_, bf16[1120,512]{1,0:T(8,128)(2,1)S(1)} %collective-permute-done.20.refs_1_.refs_15_), custom_call_target="tpu_custom_call" | custom-call | flops 587202560 | bytes 9633792 | tf_op jit(solution)/shard_map/project_acts/pallas_call | solution.py:123
  152.9 1.4 collective-permute-done.19.refs_0_
  155.2 1.1 collective-permute-done.22.refs_1_
  156.3 2.3 %add_grads.7 = f32[512,256]{1,0:T(8,128)S(1)} custom-call(s32[4]{0:T(128)S(1)} %pad_add_fusion.at_ref, bf16[512,512]{1,0:T(8,128)(2,1)S(1)} %collective-permute-done.19.refs_0_, bf16[512,512]{1,0:T(8,128)(2,1)S(1)} %collective-permute-done.22.refs_1_, ...), custom_call_target="tpu_custom_call" | custom-call | flops 1 | bytes 1 | tf_op jit(solution)/shard_map/add_grads/pallas_call | solution.py:185
  158.6 1.4 sums_for_other_core.1
  160.2 2.0 collective-permute-done.24.got_ref
  162.6 1.2 collective-permute-start.25
  163.8 1.5 collective-permute-start.26
  166.1 1.1 collective-permute-start.29
  167.3 1.5 collective-permute-start.30
  169.6 1.8 collective-permute-done.27
  171.4 1.8 collective-permute-start.28
  173.2 1.7 collective-permute-done.31
  175.0 1.7 collective-permute-start.32
  177.3 2.9 %collective-permute-done.28 = bf16[64,640]{1,0:T(8,128)(2,1)S(1)} collective-permute-done((bf16[64,640]{1,0:T(8,128)(2,1)S(1)}, bf16[64,640]{1,0:T(8,128)(2,1)S(1)}, u32[]{:S(2)}, u32[]{:S(2)}) %collective-permute-start.28) | collective-permute-done | bytes 81952 | tf_op jit(solution)/shard_map/ppermute | solution.py:19
  182.0 3.9 %collective-permute-done.33 = bf16[1,64,640]{2,1,0:T(8,128)(2,1)S(1)} collective-permute-done((bf16[1,64,640]{2,1,0:T(8,128)(2,1)S(1)}, bf16[1,64,640]{2,1,0:T(8,128)(2,1)S(1)}, u32[]{:S(2)}, u32[]{:S(2)}) %collective-permute-start.33) | collective-permute-done | bytes 81952 | tf_op jit(solution)/shard_map/ppermute | solution.py:19
  186.0 1.2 collective-permute-start.34
  187.2 2.3 %collective-permute-start.36 = (bf16[2,64,640]{2,1,0:T(8,128)(2,1)S(1)}, bf16[2,64,640]{2,1,0:T(8,128)(2,1)S(1)}, u32[]{:S(2)}, u32[]{:S(2)}) collective-permute-start(bf16[2,64,640]{2,1,0:T(8,128)(2,1)S(1)} %get-tuple-element.91), channel_id=1, source_target_pairs={{0,12},{2,14},{4,8},{6,10},{8,4},{10,6},{12,0},{14,2},{16,28},{18,... | collective-permute-start | bytes 491528 | tf_op jit(solution)/shard_map/ppermute | solution.py:19
  190.5 1.5 collective-permute-done.35
  192.9 1.6 collective-permute-done.36
  195.5 1.3 collective-permute-done.38
  196.8 17.1 %expand_update.1 = (bf16[14336,512]{1,0:T(8,128)(2,1)}, f32[64,320]{1,0:T(8,128)S(1)}) custom-call(s32[9]{0:T(128)S(1)} %stack.281.at_ref, bf16[512,640]{1,0:T(8,128)(2,1)S(1)} %bitcast.199, bf16[512,640]{1,0:T(8,128)(2,1)S(1)} %bitcast.201, bf16[1024,512]{1,0:T(8,128)(2,1)S(1)} %bitcast.198, ...), custom_call_target="tpu_custom_call", output_to_operand_aliasing={{1}: (4, {})} | custom-call | flops 9395240960 | bytes 14680064 | tf_op jit(solution)/shard_map/expand_update/pallas_call | solution.py:307
  (140 shorter events, 25.0 us)
Async XLA Ops:
  2.2 4.3 %collective-permute-start = (bf16[14,40,512]{2,1,0:T(8,128)(2,1)S(1)}, bf16[14,40,512]{2,1,0:T(8,128)(2,1)S(1)}, u32[]{:S(2)}, u32[]{:S(2)}) collective-permute-start(bf16[14,40,512]{2,1,0:T(8,128)(2,1)S(1)} %constant_dynamic-update-slice_fusion.14), channel_id=1, source_target_pairs={{0,2},{2,0},{4,6},{6,4},{8,10},{10,8},{12,14},{14,12},{16,18},{18,... | collective-permute-start | bytes 1720328 | tf_op jit(solution)/shard_map/ppermute | solution.py:19
  2.7 49.1 %collective-permute-start.8 = (bf16[1,256,4096]{2,1,0:T(8,128)(2,1)}, bf16[1,256,4096]{2,1,0:T(8,128)(2,1)}, u32[]{:S(2)}, u32[]{:S(2)}) collective-permute-start(bf16[1,256,4096]{2,1,0:T(8,128)(2,1)} %bitcast.60), channel_id=1, source_target_pairs={{0,1},{1,0},{2,3},{3,2},{4,5},{5,4},{6,7},{7,6},{8,9},{9,8},{10,11... | collective-permute-start | bytes 6291464 | tf_op jit(solution)/shard_map/ppermute | solution.py:19
  8.0 55.4 %copy-start = (bf16[1632,512]{1,0:T(8,128)(2,1)}, bf16[1632,512]{1,0:T(8,128)(2,1)S(1)}, u32[]{:S(2)}) copy-start(bf16[1632,512]{1,0:T(8,128)(2,1)S(1)} %pad_maximum_fusion.refs_0_) | copy-start | bytes 5013508
  8.0 3.7 %collective-permute-start.3 = (bf16[1632,512]{1,0:T(8,128)(2,1)S(1)}, bf16[1632,512]{1,0:T(8,128)(2,1)}, u32[]{:S(2)}, u32[]{:S(2)}) collective-permute-start(bf16[1632,512]{1,0:T(8,128)(2,1)S(1)} %pad_maximum_fusion.refs_0_), channel_id=1, source_target_pairs={{0,2},{2,0},{4,6},{6,4},{8,10},{10,8},{12,14},{14,12},{16,18},{18,... | collective-permute-start | bytes 5013512 | tf_op jit(solution)/shard_map/ppermute | solution.py:19
  8.2 38.8 %collective-permute-start.2 = (bf16[1632,512]{1,0:T(8,128)(2,1)S(1)}, bf16[1632,512]{1,0:T(8,128)(2,1)S(1)}, u32[]{:S(2)}, u32[]{:S(2)}) collective-permute-start(bf16[1632,512]{1,0:T(8,128)(2,1)S(1)} %pad_maximum_fusion.refs_0_), channel_id=1, source_target_pairs={{8,0},{16,8},{24,16},{28,24},{20,28},{12,20},{4,12},{0,4},{2,10},{... | collective-permute-start | bytes 5013512 | tf_op jit(solution)/shard_map/ppermute | solution.py:540
  9.7 37.3 %collective-permute-start.1 = (bf16[1632,512]{1,0:T(8,128)(2,1)S(1)}, bf16[1632,512]{1,0:T(8,128)(2,1)}, u32[]{:S(2)}, u32[]{:S(2)}) collective-permute-start(bf16[1632,512]{1,0:T(8,128)(2,1)S(1)} %pad_maximum_fusion.refs_0_), channel_id=1, source_target_pairs={{0,8},{8,16},{16,24},{24,28},{28,20},{20,12},{12,4},{4,0},{10,2},{... | collective-permute-start | bytes 5013512 | tf_op jit(solution)/shard_map/ppermute | solution.py:540
  47.0 16.4 %copy-start.2 = (bf16[1632,512]{1,0:T(8,128)(2,1)}, bf16[1632,512]{1,0:T(8,128)(2,1)S(1)}, u32[]{:S(2)}) copy-start(bf16[1632,512]{1,0:T(8,128)(2,1)S(1)} %collective-permute-done.2.refs_2_) | copy-start | bytes 5013508
  47.1 9.6 %collective-permute-start.7 = (bf16[1632,512]{1,0:T(8,128)(2,1)}, bf16[1632,512]{1,0:T(8,128)(2,1)}, u32[]{:S(2)}, u32[]{:S(2)}) collective-permute-start(bf16[1632,512]{1,0:T(8,128)(2,1)} %collective-permute-done.1.refs_1_), channel_id=1, source_target_pairs={{0,2},{2,0},{4,6},{6,4},{8,10},{10,8},{12,14},{14,12},{16,18},{18,... | collective-permute-start | bytes 5013512 | tf_op jit(solution)/shard_map/ppermute | solution.py:19
  47.8 8.9 %collective-permute-start.6 = (bf16[1632,512]{1,0:T(8,128)(2,1)S(1)}, bf16[1632,512]{1,0:T(8,128)(2,1)}, u32[]{:S(2)}, u32[]{:S(2)}) collective-permute-start(bf16[1632,512]{1,0:T(8,128)(2,1)S(1)} %collective-permute-done.2.refs_2_), channel_id=1, source_target_pairs={{0,2},{2,0},{4,6},{6,4},{8,10},{10,8},{12,14},{14,12},{16,18},{18,... | collective-permute-start | bytes 5013512 | tf_op jit(solution)/shard_map/ppermute | solution.py:19
  47.8 39.7 %collective-permute-start.4 = (bf16[1632,512]{1,0:T(8,128)(2,1)}, bf16[1632,512]{1,0:T(8,128)(2,1)}, u32[]{:S(2)}, u32[]{:S(2)}) collective-permute-start(bf16[1632,512]{1,0:T(8,128)(2,1)} %collective-permute-done.1.refs_1_), channel_id=1, source_target_pairs={{0,8},{8,16},{16,24},{24,28},{28,20},{20,12},{12,4},{4,0},{10,2},{... | collective-permute-start | bytes 5013512 | tf_op jit(solution)/shard_map/ppermute | solution.py:540
  49.4 38.1 %collective-permute-start.5 = (bf16[1632,512]{1,0:T(8,128)(2,1)S(1)}, bf16[1632,512]{1,0:T(8,128)(2,1)}, u32[]{:S(2)}, u32[]{:S(2)}) collective-permute-start(bf16[1632,512]{1,0:T(8,128)(2,1)S(1)} %collective-permute-done.2.refs_2_), channel_id=1, source_target_pairs={{8,0},{16,8},{24,16},{28,24},{20,28},{12,20},{4,12},{0,4},{2,10},{... | collective-permute-start | bytes 5013512 | tf_op jit(solution)/shard_map/ppermute | solution.py:540
  87.5 19.1 %collective-permute-start.12 = (bf16[1632,512]{1,0:T(8,128)(2,1)}, bf16[1632,512]{1,0:T(8,128)(2,1)}, u32[]{:S(2)}, u32[]{:S(2)}) collective-permute-start(bf16[1632,512]{1,0:T(8,128)(2,1)} %collective-permute-done.4.refs_0_.refs_3_), channel_id=1, source_target_pairs={{0,2},{2,0},{4,6},{6,4},{8,10},{10,8},{12,14},{14,12},{16,18},{18,... | collective-permute-start | bytes 5013512 | tf_op jit(solution)/shard_map/ppermute | solution.py:19
  87.6 19.0 %collective-permute-start.11 = (bf16[1632,512]{1,0:T(8,128)(2,1)}, bf16[1632,512]{1,0:T(8,128)(2,1)S(1)}, u32[]{:S(2)}, u32[]{:S(2)}) collective-permute-start(bf16[1632,512]{1,0:T(8,128)(2,1)} %collective-permute-done.5.refs_1_.refs_4_), channel_id=1, source_target_pairs={{0,2},{2,0},{4,6},{6,4},{8,10},{10,8},{12,14},{14,12},{16,18},{18,... | collective-permute-start | bytes 5013512 | tf_op jit(solution)/shard_map/ppermute | solution.py:19
  88.0 39.4 %collective-permute-start.9 = (bf16[1632,512]{1,0:T(8,128)(2,1)}, bf16[1632,512]{1,0:T(8,128)(2,1)S(1)}, u32[]{:S(2)}, u32[]{:S(2)}) collective-permute-start(bf16[1632,512]{1,0:T(8,128)(2,1)} %collective-permute-done.4.refs_0_.refs_3_), channel_id=1, source_target_pairs={{0,8},{8,16},{16,24},{24,28},{28,20},{20,12},{12,4},{4,0},{10,2},{... | collective-permute-start | bytes 5013512 | tf_op jit(solution)/shard_map/ppermute | solution.py:540
  89.1 38.3 %collective-permute-start.10 = (bf16[1632,512]{1,0:T(8,128)(2,1)}, bf16[1632,512]{1,0:T(8,128)(2,1)}, u32[]{:S(2)}, u32[]{:S(2)}) collective-permute-start(bf16[1632,512]{1,0:T(8,128)(2,1)} %collective-permute-done.5.refs_1_.refs_4_), channel_id=1, source_target_pairs={{8,0},{16,8},{24,16},{28,24},{20,28},{12,20},{4,12},{0,4},{2,10},{... | collective-permute-start | bytes 5013512 | tf_op jit(solution)/shard_map/ppermute | solution.py:540
  90.0 13.7 %collective-permute-start.14 = (bf16[1,512,512]{2,1,0:T(8,128)(2,1)}, bf16[1,512,512]{2,1,0:T(8,128)(2,1)}, u32[]{:S(2)}, u32[]{:S(2)}) collective-permute-start(bf16[1,512,512]{2,1,0:T(8,128)(2,1)} %bitcast.72), channel_id=1, source_target_pairs={{0,1},{1,0},{2,3},{3,2},{4,5},{5,4},{6,7},{7,6},{8,9},{9,8},{10,11... | collective-permute-start | bytes 1572872 | tf_op jit(solution)/shard_map/ppermute | solution.py:19
  103.7 14.4 %collective-permute-start.13 = (bf16[240,256]{1,0:T(8,128)(2,1)S(1)}, bf16[240,256]{1,0:T(8,128)(2,1)S(1)}, u32[]{:S(2)}, u32[]{:S(2)}) collective-permute-start(bf16[240,256]{1,0:T(8,128)(2,1)S(1)} %convert_element_type.51), channel_id=1, source_target_pairs={{0,1},{1,0},{2,3},{3,2},{4,5},{5,4},{6,7},{7,6},{8,9},{9,8},{10,11... | collective-permute-start | bytes 368648 | tf_op jit(solution)/shard_map/ppermute | solution.py:19
  106.6 6.2 %copy-start.8 = (f32[512,256]{1,0:T(8,128)S(1)}, f32[512,256]{1,0:T(8,128)}, u32[]{:S(2)}) copy-start(f32[512,256]{1,0:T(8,128)} %copy-done.7) | copy-start | bytes 1572868
  127.4 11.3 %copy-start.1 = (bf16[1632,512]{1,0:T(8,128)(2,1)}, bf16[1632,512]{1,0:T(8,128)(2,1)S(1)}, u32[]{:S(2)}) copy-start(bf16[1632,512]{1,0:T(8,128)(2,1)S(1)} %collective-permute-done.9.refs_0_.refs_5_) | copy-start | bytes 5013508
  127.4 5.1 %collective-permute-start.16 = (bf16[1632,512]{1,0:T(8,128)(2,1)}, bf16[1632,512]{1,0:T(8,128)(2,1)S(1)}, u32[]{:S(2)}, u32[]{:S(2)}) collective-permute-start(bf16[1632,512]{1,0:T(8,128)(2,1)} %collective-permute-done.10.refs_1_.refs_6_), channel_id=1, source_target_pairs={{0,2},{2,0},{4,6},{6,4},{8,10},{10,8},{12,14},{14,12},{16,18},{18,... | collective-permute-start | bytes 5013512 | tf_op jit(solution)/shard_map/ppermute | solution.py:19
  127.5 6.0 %collective-permute-start.17 = (bf16[1632,512]{1,0:T(8,128)(2,1)S(1)}, bf16[1632,512]{1,0:T(8,128)(2,1)}, u32[]{:S(2)}, u32[]{:S(2)}) collective-permute-start(bf16[1632,512]{1,0:T(8,128)(2,1)S(1)} %collective-permute-done.9.refs_0_.refs_5_), channel_id=1, source_target_pairs={{0,2},{2,0},{4,6},{6,4},{8,10},{10,8},{12,14},{14,12},{16,18},{18,... | collective-permute-start | bytes 5013512 | tf_op jit(solution)/shard_map/ppermute | solution.py:19
  129.0 16.2 %collective-permute-start.15 = (bf16[1120,512]{1,0:T(8,128)(2,1)}, bf16[1120,512]{1,0:T(8,128)(2,1)}, u32[]{:S(2)}, u32[]{:S(2)}) collective-permute-start(bf16[1120,512]{1,0:T(8,128)(2,1)} %slice.119), channel_id=1, source_target_pairs={{0,8},{8,16},{16,24},{24,28},{28,20},{20,12},{12,4},{4,0},{10,2},{... | collective-permute-start | bytes 3440648 | tf_op jit(solution)/shard_map/ppermute | solution.py:556
  130.7 12.9 %collective-permute-start.18 = (bf16[160,256]{1,0:T(8,128)(2,1)}, bf16[160,256]{1,0:T(8,128)(2,1)}, u32[]{:S(2)}, u32[]{:S(2)}) collective-permute-start(bf16[160,256]{1,0:T(8,128)(2,1)} %convert_element_type.52), channel_id=1, source_target_pairs={{0,1},{1,0},{2,3},{3,2},{4,5},{5,4},{6,7},{7,6},{8,9},{9,8},{10,11... | collective-permute-start | bytes 245768 | tf_op jit(solution)/shard_map/ppermute | solution.py:19
  131.5 7.2 %copy-start.10 = (f32[512,256]{1,0:T(8,128)S(1)}, f32[512,256]{1,0:T(8,128)}, u32[]{:S(2)}) copy-start(f32[512,256]{1,0:T(8,128)} %copy-done.9) | copy-start | bytes 1572868
  132.5 6.2 %copy-start.4 = (bf16[1632,512]{1,0:T(8,128)(2,1)}, bf16[1632,512]{1,0:T(8,128)(2,1)S(1)}, u32[]{:S(2)}) copy-start(bf16[1632,512]{1,0:T(8,128)(2,1)S(1)} %collective-permute-done.16.refs_2_.refs_13_) | copy-start | bytes 5013508
  138.7 7.5 %copy-start.13 = (f32[160,256]{1,0:T(8,128)}, f32[160,256]{1,0:T(8,128)S(1)}, u32[]{:S(2)}) copy-start(f32[160,256]{1,0:T(8,128)S(1)} %project_acts.6.refs_2_) | copy-start | bytes 491524
  145.2 3.0 %collective-permute-start.20 = (bf16[1120,512]{1,0:T(8,128)(2,1)}, bf16[1120,512]{1,0:T(8,128)(2,1)S(1)}, u32[]{:S(2)}, u32[]{:S(2)}) collective-permute-start(bf16[1120,512]{1,0:T(8,128)(2,1)} %collective-permute-done.15.refs_0_.refs_7_), channel_id=1, source_target_pairs={{0,2},{2,0},{4,6},{6,4},{8,10},{10,8},{12,14},{14,12},{16,18},{18,... | collective-permute-start | bytes 3440648 | tf_op jit(solution)/shard_map/ppermute | solution.py:19
  145.2 9.2 %collective-permute-start.19 = (bf16[512,512]{1,0:T(8,128)(2,1)S(1)}, bf16[512,512]{1,0:T(8,128)(2,1)S(1)}, u32[]{:S(2)}, u32[]{:S(2)}) collective-permute-start(bf16[512,512]{1,0:T(8,128)(2,1)S(1)} %slice.118), channel_id=1, source_target_pairs={{0,8},{8,16},{16,24},{24,28},{28,20},{20,12},{12,4},{4,0},{10,2},{... | collective-permute-start | bytes 1572872 | tf_op jit(solution)/shard_map/ppermute | solution.py:562
  146.3 10.0 %copy-start.12 = (f32[512,256]{1,0:T(8,128)S(1)}, f32[512,256]{1,0:T(8,128)}, u32[]{:S(2)}) copy-start(f32[512,256]{1,0:T(8,128)} %copy-done.11) | copy-start | bytes 1572868
  146.3 6.7 %collective-permute-start.21 = (bf16[160,256]{1,0:T(8,128)(2,1)S(1)}, bf16[160,256]{1,0:T(8,128)(2,1)S(1)}, u32[]{:S(2)}, u32[]{:S(2)}) collective-permute-start(bf16[160,256]{1,0:T(8,128)(2,1)S(1)} %convert_element_type.53), channel_id=1, source_target_pairs={{0,1},{1,0},{2,3},{3,2},{4,5},{5,4},{6,7},{7,6},{8,9},{9,8},{10,11... | collective-permute-start | bytes 245768 | tf_op jit(solution)/shard_map/ppermute | solution.py:19
  154.4 1.9 collective-permute-start.22
  154.4 4.2 %collective-permute-start.23 = (bf16[80,256]{1,0:T(8,128)(2,1)S(1)}, bf16[80,256]{1,0:T(8,128)(2,1)S(1)}, u32[]{:S(2)}, u32[]{:S(2)}) collective-permute-start(bf16[80,256]{1,0:T(8,128)(2,1)S(1)} %convert_element_type.54), channel_id=1, source_target_pairs={{0,1},{1,0},{2,3},{3,2},{4,5},{5,4},{6,7},{7,6},{8,9},{9,8},{10,11... | collective-permute-start | bytes 122888 | tf_op jit(solution)/shard_map/ppermute | solution.py:19
  160.0 2.2 %collective-permute-start.24 = (bf16[2,256,640]{2,1,0:T(8,128)(2,1)S(1)}, bf16[2,256,640]{2,1,0:T(8,128)(2,1)S(1)}, u32[]{:S(2)}, u32[]{:S(2)}) collective-permute-start(bf16[2,256,640]{2,1,0:T(8,128)(2,1)S(1)} %get-tuple-element.68), channel_id=1, source_target_pairs={{0,2},{2,0},{4,6},{6,4},{8,10},{10,8},{12,14},{14,12},{16,18},{18,... | collective-permute-start | bytes 1966088 | tf_op jit(solution)/shard_map/ppermute | solution.py:19
  162.6 6.2 %collective-permute-start.25 = (bf16[64,640]{1,0:T(8,128)(2,1)S(1)}, bf16[64,640]{1,0:T(8,128)(2,1)S(1)}, u32[]{:S(2)}, u32[]{:S(2)}) collective-permute-start(bf16[64,640]{1,0:T(8,128)(2,1)S(1)} %get-tuple-element.70), channel_id=1, source_target_pairs={{0,4},{2,6},{4,0},{6,2},{8,12},{10,14},{12,8},{14,10},{16,20},{18,... | collective-permute-start | bytes 245768 | tf_op jit(solution)/shard_map/ppermute | solution.py:19
  163.8 5.8 %collective-permute-start.26 = (bf16[64,640]{1,0:T(8,128)(2,1)S(1)}, bf16[64,640]{1,0:T(8,128)(2,1)S(1)}, u32[]{:S(2)}, u32[]{:S(2)}) collective-permute-start(bf16[64,640]{1,0:T(8,128)(2,1)S(1)} %get-tuple-element.71), channel_id=1, source_target_pairs={{0,8},{2,10},{4,12},{6,14},{8,0},{10,2},{12,4},{14,6},{16,24},{18,... | collective-permute-start | bytes 245768 | tf_op jit(solution)/shard_map/ppermute | solution.py:19
  165.2 6.2 %collective-permute-start.27 = (bf16[64,640]{1,0:T(8,128)(2,1)S(1)}, bf16[64,640]{1,0:T(8,128)(2,1)S(1)}, u32[]{:S(2)}, u32[]{:S(2)}) collective-permute-start(bf16[64,640]{1,0:T(8,128)(2,1)S(1)} %get-tuple-element.72), channel_id=1, source_target_pairs={{0,12},{2,14},{4,8},{6,10},{8,4},{10,6},{12,0},{14,2},{16,28},{18,... | collective-permute-start | bytes 245768 | tf_op jit(solution)/shard_map/ppermute | solution.py:19
  166.1 7.1 %collective-permute-start.29 = (bf16[64,640]{1,0:T(8,128)(2,1)S(1)}, bf16[64,640]{1,0:T(8,128)(2,1)S(1)}, u32[]{:S(2)}, u32[]{:S(2)}) collective-permute-start(bf16[64,640]{1,0:T(8,128)(2,1)S(1)} %get-tuple-element.74), channel_id=1, source_target_pairs={{0,4},{2,6},{4,0},{6,2},{8,12},{10,14},{12,8},{14,10},{16,20},{18,... | collective-permute-start | bytes 245768 | tf_op jit(solution)/shard_map/ppermute | solution.py:19
  167.3 6.0 %collective-permute-start.30 = (bf16[64,640]{1,0:T(8,128)(2,1)S(1)}, bf16[64,640]{1,0:T(8,128)(2,1)S(1)}, u32[]{:S(2)}, u32[]{:S(2)}) collective-permute-start(bf16[64,640]{1,0:T(8,128)(2,1)S(1)} %get-tuple-element.75), channel_id=1, source_target_pairs={{0,8},{2,10},{4,12},{6,14},{8,0},{10,2},{12,4},{14,6},{16,24},{18,... | collective-permute-start | bytes 245768 | tf_op jit(solution)/shard_map/ppermute | solution.py:19
  168.7 6.2 %collective-permute-start.31 = (bf16[64,640]{1,0:T(8,128)(2,1)S(1)}, bf16[64,640]{1,0:T(8,128)(2,1)S(1)}, u32[]{:S(2)}, u32[]{:S(2)}) collective-permute-start(bf16[64,640]{1,0:T(8,128)(2,1)S(1)} %get-tuple-element.76), channel_id=1, source_target_pairs={{0,12},{2,14},{4,8},{6,10},{8,4},{10,6},{12,0},{14,2},{16,28},{18,... | collective-permute-start | bytes 245768 | tf_op jit(solution)/shard_map/ppermute | solution.py:19
  171.4 8.7 %collective-permute-start.28 = (bf16[64,640]{1,0:T(8,128)(2,1)S(1)}, bf16[64,640]{1,0:T(8,128)(2,1)S(1)}, u32[]{:S(2)}, u32[]{:S(2)}) collective-permute-start(bf16[64,640]{1,0:T(8,128)(2,1)S(1)} %fusion.2), channel_id=1, source_target_pairs={{0,16},{2,18},{4,20},{6,22},{8,24},{10,26},{12,28},{14,30},{16,0},... | collective-permute-start | bytes 245768 | tf_op jit(solution)/shard_map/ppermute | solution.py:19
  175.0 19.8 %copy-start.17 = (bf16[2,512,512]{2,1,0:T(8,128)(2,1)S(1)}, bf16[2,512,512]{2,1,0:T(8,128)(2,1)}, u32[]{:S(2)}) copy-start(bf16[2,512,512]{2,1,0:T(8,128)(2,1)} %pad_maximum_fusion.2) | copy-start | bytes 3145732
  175.0 6.2 %collective-permute-start.32 = (bf16[64,640]{1,0:T(8,128)(2,1)S(1)}, bf16[64,640]{1,0:T(8,128)(2,1)S(1)}, u32[]{:S(2)}, u32[]{:S(2)}) collective-permute-start(bf16[64,640]{1,0:T(8,128)(2,1)S(1)} %fusion.3), channel_id=1, source_target_pairs={{0,16},{2,18},{4,20},{6,22},{8,24},{10,26},{12,28},{14,30},{16,0},... | collective-permute-start | bytes 245768 | tf_op jit(solution)/shard_map/ppermute | solution.py:19
  181.4 4.5 %collective-permute-start.33 = (bf16[1,64,640]{2,1,0:T(8,128)(2,1)S(1)}, bf16[1,64,640]{2,1,0:T(8,128)(2,1)S(1)}, u32[]{:S(2)}, u32[]{:S(2)}) collective-permute-start(bf16[1,64,640]{2,1,0:T(8,128)(2,1)S(1)} %get-tuple-element.82), channel_id=1, source_target_pairs={{0,1},{1,0},{2,3},{3,2},{4,5},{5,4},{6,7},{7,6},{8,9},{9,8},{10,11... | collective-permute-start | bytes 245768 | tf_op jit(solution)/shard_map/ppermute | solution.py:19
  185.9 6.2 %collective-permute-start.35 = (bf16[2,64,640]{2,1,0:T(8,128)(2,1)S(1)}, bf16[2,64,640]{2,1,0:T(8,128)(2,1)S(1)}, u32[]{:S(2)}, u32[]{:S(2)}) collective-permute-start(bf16[2,64,640]{2,1,0:T(8,128)(2,1)S(1)} %get-tuple-element.91), channel_id=1, source_target_pairs={{0,8},{2,10},{4,12},{6,14},{8,0},{10,2},{12,4},{14,6},{16,24},{18,... | collective-permute-start | bytes 491528 | tf_op jit(solution)/shard_map/ppermute | solution.py:19
  186.0 6.9 %collective-permute-start.34 = (bf16[2,64,640]{2,1,0:T(8,128)(2,1)S(1)}, bf16[2,64,640]{2,1,0:T(8,128)(2,1)S(1)}, u32[]{:S(2)}, u32[]{:S(2)}) collective-permute-start(bf16[2,64,640]{2,1,0:T(8,128)(2,1)S(1)} %get-tuple-element.91), channel_id=1, source_target_pairs={{0,4},{2,6},{4,0},{6,2},{8,12},{10,14},{12,8},{14,10},{16,20},{18,... | collective-permute-start | bytes 491528 | tf_op jit(solution)/shard_map/ppermute | solution.py:19
  187.2 7.4 %collective-permute-start.36 = (bf16[2,64,640]{2,1,0:T(8,128)(2,1)S(1)}, bf16[2,64,640]{2,1,0:T(8,128)(2,1)S(1)}, u32[]{:S(2)}, u32[]{:S(2)}) collective-permute-start(bf16[2,64,640]{2,1,0:T(8,128)(2,1)S(1)} %get-tuple-element.91), channel_id=1, source_target_pairs={{0,12},{2,14},{4,8},{6,10},{8,4},{10,6},{12,0},{14,2},{16,28},{18,... | collective-permute-start | bytes 491528 | tf_op jit(solution)/shard_map/ppermute | solution.py:19
  189.7 5.0 %collective-permute-start.37 = (f32[64,320]{1,0:T(8,128)S(1)}, f32[64,320]{1,0:T(8,128)S(1)}, u32[]{:S(2)}, u32[]{:S(2)}) collective-permute-start(f32[64,320]{1,0:T(8,128)S(1)} %constant_dynamic-slice_fusion), channel_id=1, source_target_pairs={{0,0},{2,2},{4,4},{6,6},{8,8},{10,10},{12,12},{14,14},{16,1},{18,3... | collective-permute-start | bytes 245768 | tf_op jit(solution)/shard_map/ppermute | solution.py:481
  194.7 2.2 %collective-permute-start.38 = (bf16[4,2,64,640]{3,2,1,0:T(8,128)(2,1)S(1)}, bf16[4,2,64,640]{3,2,1,0:T(8,128)(2,1)S(1)}, u32[]{:S(2)}, u32[]{:S(2)}) collective-permute-start(bf16[4,2,64,640]{3,2,1,0:T(8,128)(2,1)S(1)} %pad_maximum_fusion.3), channel_id=1, source_target_pairs={{0,2},{2,0},{4,6},{6,4},{8,10},{10,8},{12,14},{14,12},{16,18},{18,... | collective-permute-start | bytes 1966088 | tf_op jit(solution)/shard_map/ppermute | solution.py:19
  (10 other events, 24.7 us)
